TPU v7x, 128 devices: a whole 4x4x4 slice. The times are simulated.
128 devices in a mesh: gx: 8 (over z, core), gy: 16 (over y, x).
Axes of the slice: x: 4, y: 4, z: 4, core: 2. Of those that a mesh axis runs over, the one named last changes fastest.
Arguments:
- residual: float32 [4, 96, 192, 384], P(None, 'gx', 'gy'), may hold values from -6 to 6
- sx_block: float32 [16, 8, 8], P('gx'), may hold values from -2 to 2
- sy_block: float32 [32, 8, 8], P('gy'), may hold values from -2 to 2
- depth_eigenvectors: float32 [64, 8, 8], replicated, may hold values from -2 to 2
- lam_x: float32 [16, 8], P('gx'), may hold values from 0.1 to 2
- lam_y: float32 [32, 8], P('gy'), may hold values from 0.1 to 2
- depth_eigenvalues: float32 [64, 8], replicated, may hold values from 0.1 to 2
- coarse_factor: bfloat16 [8, 16, 585, 7233], P('gx', 'gy'), may hold values from -0.1504 to 0.1504, as said below
Outputs:
- preconditioned: float32 [4, 96, 192, 384], P(None, 'gx', 'gy')
Inputs may be any that keep to these rules, and one draw needn't show every extreme that they name: `coarse_factor`: block [gx, gy] holds the rows of that device's (3) (3) (65) local vertices. A vertex held by several devices (on block boundaries, periodically) has the same row on each of them; such a row is zero in the own columns and in the columns of every tree level below the lowest level whose node contains all devices that hold the vertex. A vertex held by one device has no such zeros.
All inputs are finite; a program needn't handle non-finite values.
Results may differ from a plain program's by a relative error of at most 0.00045.
Values sent between devices are 32-bit elements; how exact they have to be, the bound alone decides.
No kernel may reach another device: no remote copies, remote signals or barrier semaphores. Data moves between devices by JAX's collectives and lax.ppermute only.
A program may use at most 128 MiB of HBM per device.

v0:
```python
import jax
import jax.numpy as jnp
import numpy as np
import ml_dtypes
from jax import lax
from jax.experimental import pallas as pl
from jax.experimental.pallas import tpu as pltpu
from jax.sharding import PartitionSpec as P

SEP = 1024
LEAF = 65
LEVELS = 7
VLOC = 585
COLS = 7233
WIDE = 8192
BF = jnp.bfloat16
F32 = jnp.float32

gauss_nodes = [
    -0.932469514203152,
    -0.6612093864662645,
    -0.2386191860831969,
    0.2386191860831969,
    0.6612093864662645,
    0.932469514203152,
]
gauss_weights = [
    0.17132449237917033,
    0.3607615730481386,
    0.46791393457269104,
    0.46791393457269104,
    0.3607615730481386,
    0.17132449237917033,
]
prolong_np = np.stack(
    [(1.0 - np.array(gauss_nodes)) / 2.0, (1.0 + np.array(gauss_nodes)) / 2.0]
).astype(np.float32)
restrict_np = (
    np.stack([(1.0 - np.array(gauss_nodes)) / 2.0, (1.0 + np.array(gauss_nodes)) / 2.0])
    * np.array(gauss_weights)[None, :]
).astype(np.float32)


def line_table(table, elems):
    out = np.zeros((elems * 6, elems + 1), np.float32)
    for c in range(elems):
        for k in range(6):
            out[6 * c + k, c] = table[0, k]
            out[6 * c + k, c + 1] = table[1, k]
    return out


def split_np(x):
    hi = x.astype(ml_dtypes.bfloat16)
    lo = (x - hi.astype(np.float32)).astype(ml_dtypes.bfloat16)
    return hi, lo


def split(x):
    hi = x.astype(BF)
    lo = (x - hi.astype(F32)).astype(BF)
    return hi, lo


def dot(a, b, dims=(((1,), (0,)), ((), ()))):
    return lax.dot_general(a, b, dims, preferred_element_type=F32)


NT = (((1,), (1,)), ((), ()))
TN = (((0,), (0,)), ((), ()))


def dot3(a, b, dims=(((1,), (0,)), ((), ()))):
    return dot(a[0], b[0], dims) + (dot(a[0], b[1], dims) + dot(a[1], b[0], dims))


def ab_mask(rows, cols):
    col = lax.broadcasted_iota(jnp.int32, (rows, cols), 1)
    ab = lax.broadcasted_iota(jnp.int32, (rows, cols), 0) // 8
    return jnp.logical_and(col >= ab * 65, col < ab * 65 + 65)


FACE = 12 * 384
SLAB = 14 * 384
CUT = 5120
TAIL = COLS - CUT
TAIL_WIDE = 2176
PADDED = 7296
BIG = 51 << 20
ROW_CHUNKS = ((512, 73), (0, 256), (256, 128), (384, 128))
SMALL = 24 << 20
HBM = pl.BlockSpec(memory_space=pltpu.HBM)
UNUSED = pl.BlockSpec(memory_space=pl.ANY)


def whole(shape):
    return pl.BlockSpec(shape, lambda i: (0,) * len(shape))


def parities():
    return lax.axis_index("gy") % 2 == 1, lax.axis_index("gx") % 2 == 1


def forward_kernel(
    r_hbm, rz_hbm, tile_hbm, f_ref,
    msg_ref, own_ref, y2_ref, x1_ref, x2_ref, keep_ref,
    r_ref, rz_ref, tile_ref, u_ref, acc_ref, small_sems, sems,
):
    small = []
    for k, (src, dst) in enumerate(((r_hbm, r_ref), (rz_hbm, rz_ref), (tile_hbm, tile_ref))):
        small.append(pltpu.make_async_copy(src, dst, small_sems.at[k]))
        small[-1].start()
    copies = []
    for k, (start, size) in enumerate(ROW_CHUNKS):
        rows = pl.ds(start, size)
        copies.append(pltpu.make_async_copy(f_ref.at[rows, :], keep_ref.at[rows, :], sems.at[k]))
        copies[-1].start()

    u_ref[...] = jnp.zeros_like(u_ref)
    small[0].wait()
    r0 = [float(v) for v in restrict_np[0]]
    r1 = [float(v) for v in restrict_np[1]]
    for y_elem in range(2):
        sums = []
        for j in range(6):
            y = 6 * y_elem + j
            lows = [r_ref[i, y] for i in range(6)]
            highs = [r_ref[6 + i, y] for i in range(6)]
            sums.append(
                [
                    sum(r0[i] * lows[i] for i in range(6)),
                    sum(r1[i] * lows[i] for i in range(6)) + sum(r0[i] * highs[i] for i in range(6)),
                    sum(r1[i] * highs[i] for i in range(6)),
                ]
            )
        for a in range(3):
            for t, table in ((0, r0), (1, r1)):
                row = (a * 3 + y_elem + t) * 8
                u_ref[row : row + 4, :] += sum(table[j] * sums[j][a] for j in range(6))
    small[1].wait()
    vert = dot3(split(u_ref[...]), (rz_ref[0], rz_ref[1])).astype(BF)
    small[2].wait()
    spread = dot(vert, tile_ref[...])
    spread = jnp.where(ab_mask(72, 640), spread, 0.0)
    v = sum(spread[8 * k : 8 * k + 8] for k in range(9)).astype(BF)[:, :VLOC]

    gy_odd, gx_odd = parities()
    for i in range(12):
        cols = slice(384 * i, 384 * i + 384)
        low, high = r_ref[i, 0], r_ref[i, 11]
        msg_ref[:, LEVELS * SEP + 384 * i : LEVELS * SEP + 384 * i + 384] = jnp.where(gy_odd, low, high)
        y2_ref[:, cols] = jnp.where(gy_odd, high, low)
        low, high = r_ref[0, i], r_ref[11, i]
        x1_ref[:, cols] = jnp.where(gx_odd, low, high)
        x2_ref[:, cols] = jnp.where(gx_odd, high, low)

    acc_ref[:, LEVELS * SEP :] = jnp.zeros((8, 128), F32)
    for k, (start, size) in enumerate(ROW_CHUNKS):
        copies[k].wait()
        rows = slice(start, start + size)
        product = dot(v[:, rows], keep_ref[rows, :])
        acc_ref[:, :COLS] = product if k == 0 else acc_ref[:, :COLS] + product
    own_ref[...] = acc_ref[:4, :128]
    msg_ref[:, : LEVELS * SEP] = pltpu.roll(acc_ref[...], PADDED - LEAF, 1)[:4, : LEVELS * SEP]


def forward(field, factor):
    rz = np.zeros((384, 128), np.float32)
    rz[:, :65] = line_table(restrict_np, 64)
    tile = np.zeros((128, 640), ml_dtypes.bfloat16)
    for ab in range(9):
        for c in range(65):
            tile[c, ab * 65 + c] = 1
    shapes = [(4, LEVELS * SEP + FACE), (4, 128), (4, FACE), (4, FACE), (4, FACE)]
    vm = pl.BlockSpec(memory_space=pltpu.VMEM)
    return pl.pallas_call(
        forward_kernel,
        in_specs=[HBM] * 4,
        out_specs=[vm] * 6,
        out_shape=[jax.ShapeDtypeStruct(v, F32) for v in shapes] + [jax.ShapeDtypeStruct((VLOC, COLS), BF)],
        scratch_shapes=[
            pltpu.VMEM((12, 12, 4, 384), F32),
            pltpu.VMEM((2, 384, 128), BF),
            pltpu.VMEM((128, 640), BF),
            pltpu.VMEM((72, 384), F32),
            pltpu.VMEM((8, PADDED), F32),
            pltpu.SemaphoreType.DMA((3,)),
            pltpu.SemaphoreType.DMA((len(ROW_CHUNKS),)),
        ],
        compiler_params=pltpu.CompilerParams(vmem_limit_bytes=BIG),
        cost_estimate=pl.CostEstimate(flops=2 * 8 * VLOC * COLS, bytes_accessed=9_500_000, transcendentals=0),
        name="forward",
    )(field, jnp.stack([jnp.asarray(v) for v in split_np(rz)]), jnp.asarray(tile), factor)


def faces_kernel(wait_ref, x1_ref, x2_ref, y1_ref, y2_ref, m1_ref, m2_ref):
    gy_odd, gx_odd = parities()
    m1_ref[:, :FACE] = x1_ref[...]
    m2_ref[:, :FACE] = x2_ref[...]
    tail = LEVELS * SEP
    low_x = slice(0, 384)
    high_x = slice(FACE - 384, FACE)

    def corner(cols):
        one = y1_ref[:, tail + cols.start : tail + cols.stop]
        two = y2_ref[:, cols]
        return jnp.where(gy_odd, one, two), jnp.where(gy_odd, two, one)

    low, high = corner(low_x), corner(high_x)
    for k in range(2):
        cols = slice(FACE + 384 * k, FACE + 384 * k + 384)
        m1_ref[:, cols] = jnp.where(gx_odd, low[k], high[k])
        m2_ref[:, cols] = jnp.where(gx_odd, high[k], low[k])


def faces(wait, x1, x2, y1, y2):
    vm = pl.BlockSpec(memory_space=pltpu.VMEM)
    return pl.pallas_call(
        faces_kernel,
        in_specs=[UNUSED] + [vm] * 4,
        out_specs=[vm] * 2,
        out_shape=[jax.ShapeDtypeStruct((4, SLAB), F32)] * 2,
        compiler_params=pltpu.CompilerParams(vmem_limit_bytes=SMALL),
        cost_estimate=pl.CostEstimate(flops=100_000, bytes_accessed=300_000, transcendentals=0),
        name="faces",
    )(wait, x1, x2, y1, y2)


def tables_kernel(wait_ref, sx_ref, sy_ref, dt_ref, lx_ref, ly_ref, lz_ref, a_ref, b_ref, zf_ref, zb_ref, rs_ref):
    lane = lax.broadcasted_iota(jnp.int32, (8, 256), 1)
    sub = lax.broadcasted_iota(jnp.int32, (8, 256), 0)
    slab = lane // 16
    xpos = jnp.where(slab < 12, slab + 1, jnp.where(slab == 12, 0, jnp.where(slab == 13, 13, 99)))
    yrow = lane % 16
    ypos = jnp.where(yrow < 12, yrow + 1, jnp.where(yrow == 12, 0, jnp.where(yrow == 13, 13, 99)))
    inner = jnp.logical_and(sub >= 1, sub <= 6)

    def exact(a, b, dims):
        return lax.dot_general(a, b, dims, precision=lax.Precision.HIGHEST, preferred_element_type=F32)

    def expand(mat_ref, pos, keep):
        parts = []
        for e in range(2):
            pick = jnp.where(jnp.logical_and(pos == 6 * e + sub, keep), 1.0, 0.0)
            parts.append(exact(mat_ref[e], pick, TN))
        return jnp.concatenate(parts, axis=0)

    everything = sub >= 0
    ax = expand(sx_ref, xpos, everything)
    ay = expand(sy_ref, ypos, everything)
    for i in range(16):
        hi, lo = split(ax[i : i + 1, :] * ay)
        a_ref[0, 16 * i : 16 * i + 16, :] = hi
        a_ref[1, 16 * i : 16 * i + 16, :] = lo
    bx = expand(sx_ref, xpos, inner)
    by = expand(sy_ref, ypos, inner)
    full = jnp.concatenate([bx[i : i + 1, :] * by for i in range(16)], axis=0)
    hi, lo = split(full.T)
    b_ref[0] = hi
    b_ref[1] = lo

    row = lax.broadcasted_iota(jnp.int32, (256, 8), 0)
    col = lax.broadcasted_iota(jnp.int32, (256, 8), 1)

    def column(lam_ref, group):
        total = jnp.zeros((256, 8), F32)
        for e in range(2):
            total += jnp.where(group == 8 * e + col, lam_ref[e : e + 1, :], 0.0)
        return jnp.sum(total, axis=1, keepdims=True)

    lateral = column(lx_ref, row // 16) + column(ly_ref, row % 16)

    for g in range(2):
        pick = jnp.where(
            lax.broadcasted_iota(jnp.int32, (64, 256), 0)
            == lax.broadcasted_iota(jnp.int32, (64, 256), 1) // 8 + 32 * g,
            1.0,
            0.0,
        )
        mine = sub == lane % 8
        spread = exact(dt_ref[...], pick, (((1,), (0,)), ((), ())))
        depth = exact(lz_ref[...], pick, (((1,), (0,)), ((), ())))
        depth = jnp.sum(jnp.where(mine, depth, 0.0), axis=0, keepdims=True)
        rs_ref[:, 256 * g : 256 * g + 256] = 1.0 / (lateral + depth)
        z = lax.broadcasted_iota(jnp.int32, (256, 256), 0) + 128 * g
        c = lax.broadcasted_iota(jnp.int32, (256, 256), 1) // 8 + 32 * g
        w = z + 1 - 6 * c
        table = jnp.zeros((256, 256), F32)
        for k in range(8):
            line = jnp.sum(jnp.where(mine, spread[8 * k : 8 * k + 8], 0.0), axis=0, keepdims=True)
            table = jnp.where(w == k, line, table)
        hi, lo = split(table)
        zf_ref[0, g] = hi
        zf_ref[1, g] = lo
        mid = jnp.logical_and(w >= 1, w <= 6)
        zb_ref[0, g] = jnp.where(mid, hi.astype(F32), 0.0).astype(BF)
        zb_ref[1, g] = jnp.where(mid, lo.astype(F32), 0.0).astype(BF)


def tables(wait, sx, sy, dt, lx, ly, lz):
    vm = pl.BlockSpec(memory_space=pltpu.VMEM)
    return pl.pallas_call(
        tables_kernel,
        in_specs=[UNUSED] + [vm] * 6,
        out_specs=[vm] * 5,
        out_shape=[
            jax.ShapeDtypeStruct((2, 256, 256), BF),
            jax.ShapeDtypeStruct((2, 256, 256), BF),
            jax.ShapeDtypeStruct((2, 2, 256, 256), BF),
            jax.ShapeDtypeStruct((2, 2, 256, 256), BF),
            jax.ShapeDtypeStruct((256, 512), F32),
        ],
        compiler_params=pltpu.CompilerParams(vmem_limit_bytes=SMALL),
        cost_estimate=pl.CostEstimate(flops=1_000_000_000, bytes_accessed=2_000_000, transcendentals=0),
        name="tables",
    )(wait, sx, sy, dt, lx, ly, lz)


def schwarz_kernel(
    first, wait_ref, r_ref, y1_ref, y2_ref, m1_ref, m2_ref, a_ref, b_ref, zf_ref, zb_ref, rs_ref, out_ref, x_ref
):
    gy_odd, gx_odd = parities()
    tail = LEVELS * SEP
    x_ref[...] = jnp.zeros_like(x_ref)
    for k in range(out_ref.shape[0]):
        n = first + k
        for x in range(12):
            x_ref[k, 16 * x : 16 * x + 12, :] = r_ref[x, :, n, :]
            one = y1_ref[n : n + 1, tail + 384 * x : tail + 384 * x + 384]
            two = y2_ref[n : n + 1, 384 * x : 384 * x + 384]
            x_ref[k, 16 * x + 12 : 16 * x + 13, :] = jnp.where(gy_odd, one, two)
            x_ref[k, 16 * x + 13 : 16 * x + 14, :] = jnp.where(gy_odd, two, one)
        for j in range(14):
            one = m1_ref[n : n + 1, 384 * j : 384 * j + 384]
            two = m2_ref[n : n + 1, 384 * j : 384 * j + 384]
            x_ref[k, 192 + j : 193 + j, :] = jnp.where(gx_odd, one, two)
            x_ref[k, 208 + j : 209 + j, :] = jnp.where(gx_odd, two, one)
        a = (a_ref[0][:, :224], a_ref[1][:, :224])
        t1 = split(dot3(a, split(x_ref[k])))
        backs = []
        for g in range(2):
            part = (t1[0][:, 128 * g : 128 * g + 256], t1[1][:, 128 * g : 128 * g + 256])
            t2 = dot3(part, (zf_ref[0, g], zf_ref[1, g]))
            t3 = split(t2 * rs_ref[:, 256 * g : 256 * g + 256])
            backs.append(dot3(t3, (zb_ref[0, g], zb_ref[1, g]), NT))
        t4 = split(
            jnp.concatenate(
                [backs[0][:, :128], backs[0][:, 128:] + backs[1][:, :128], backs[1][:, 128:]], axis=1
            )
        )
        out_ref[k] = dot3((b_ref[0][:192], b_ref[1][:192]), t4)


def schwarz(first, count, wait, field, y1, y2, m1, m2, tabs):
    vm = pl.BlockSpec(memory_space=pltpu.VMEM)
    kernel = lambda *refs: schwarz_kernel(first, *refs)
    return pl.pallas_call(
        kernel,
        in_specs=[UNUSED] + [vm] * 10,
        out_specs=vm,
        out_shape=jax.ShapeDtypeStruct((count, 192, 384), F32),
        scratch_shapes=[pltpu.VMEM((count, 224, 384), F32)],
        compiler_params=pltpu.CompilerParams(vmem_limit_bytes=SMALL),
        cost_estimate=pl.CostEstimate(flops=900_000_000 * count, bytes_accessed=700_000 * count, transcendentals=0),
        name="schwarz",
    )(wait, field, y1, y2, m1, m2, *tabs)


def early_kernel(
    wait_ref, sep_ref, own_ref, f_ref, pz_hbm, tile_hbm,
    v_ref, keep_ref, last_ref, pz_ref, tile_ref,
    nv_ref, sems,
):
    copies = []
    pairs = [(f_ref.at[:, pl.ds(CUT, LEVELS * SEP - CUT)], keep_ref), (pz_hbm, pz_ref)]
    pairs.append((tile_hbm, tile_ref))
    for k, (src, dst) in enumerate(pairs):
        copies.append(pltpu.make_async_copy(src, dst, sems.at[k]))
        copies[-1].start()
    lane = lax.broadcasted_iota(jnp.int32, (4, 128), 1)
    sep = pltpu.roll(jnp.concatenate([sep_ref[...], jnp.zeros((4, CUT), F32)], axis=0), LEAF, 1)
    first = jnp.where(lane < LEAF, own_ref[...], sep[:4, :128])
    first = jnp.concatenate([first, jnp.zeros((4, 128), F32)], axis=0)
    nv_ref[:, :128] = first.astype(BF)
    nv_ref[:, 128:] = sep[:, 128:].astype(BF)
    last_ref[:, LEAF:] = jnp.zeros((VLOC, 128 - LEAF), BF)
    last_ref[:, :LEAF] = f_ref[:, LEVELS * SEP :]
    v_ref[:, VLOC:] = jnp.zeros((8, 640 - VLOC), F32)
    v_ref[:, :VLOC] = dot(nv_ref[...], f_ref[:, :CUT], NT)
    for copy in copies:
        copy.wait()


def early(wait, sep, own, factor):
    pz = np.zeros((128, 384), np.float32)
    pz[:65] = line_table(prolong_np, 64).T
    tile = np.zeros((640, 128), ml_dtypes.bfloat16)
    for ab in range(9):
        for c in range(65):
            tile[ab * 65 + c, c] = 1
    vm = pl.BlockSpec(memory_space=pltpu.VMEM)
    return pl.pallas_call(
        early_kernel,
        in_specs=[UNUSED, vm, vm, vm, HBM, HBM],
        out_specs=[vm] * 5,
        out_shape=[
            jax.ShapeDtypeStruct((8, 640), F32),
            jax.ShapeDtypeStruct((VLOC, LEVELS * SEP - CUT), BF),
            jax.ShapeDtypeStruct((VLOC, 128), BF),
            jax.ShapeDtypeStruct((2, 128, 384), BF),
            jax.ShapeDtypeStruct((640, 128), BF),
        ],
        scratch_shapes=[
            pltpu.VMEM((8, CUT), BF),
            pltpu.SemaphoreType.DMA((3,)),
        ],
        compiler_params=pltpu.CompilerParams(vmem_limit_bytes=SMALL),
        cost_estimate=pl.CostEstimate(flops=2 * 8 * VLOC * CUT, bytes_accessed=9_000_000, transcendentals=0),
        name="early",
    )(wait, sep, own, factor, jnp.stack([jnp.asarray(v) for v in split_np(pz)]), jnp.asarray(tile))


def late_kernel(top_ref, v_ref, keep_ref, last_ref, s_ref, pz_ref, tile_ref, out_ref):
    nv = jnp.concatenate([top_ref[...], jnp.zeros((4, TAIL_WIDE), F32)], axis=0).astype(BF)
    v = v_ref[...]
    add = dot(nv[:, : LEVELS * SEP - CUT], keep_ref[...], NT)
    add = add + dot(nv[:, LEVELS * SEP - CUT :], last_ref[...], NT)
    v = v + jnp.concatenate([add, jnp.zeros((8, 640 - VLOC), F32)], axis=1)
    spread = jnp.where(ab_mask(72, 640), jnp.concatenate([v] * 9, axis=0), 0.0)
    hi, lo = split(spread)
    vert = dot(hi, tile_ref[...]) + dot(lo, tile_ref[...])
    lines = dot3(split(vert), (pz_ref[0], pz_ref[1]))
    p0 = [float(q) for q in prolong_np[0]]
    p1 = [float(q) for q in prolong_np[1]]
    for y in range(12):
        b, j = divmod(y, 6)
        planes = []
        for a in range(3):
            low = lines[(a * 3 + b) * 8 : (a * 3 + b) * 8 + 4, :]
            high = lines[(a * 3 + b + 1) * 8 : (a * 3 + b + 1) * 8 + 4, :]
            planes.append(p0[j] * low + p1[j] * high)
        for x in range(12):
            e, i = divmod(x, 6)
            out_ref[x, y] = s_ref[x, y] + (p0[i] * planes[e] + p1[i] * planes[e + 1])


def late(top, vertex, keep, last, solved, pz, tile):
    vm = pl.BlockSpec(memory_space=pltpu.VMEM)
    return pl.pallas_call(
        late_kernel,
        in_specs=[vm] * 7,
        out_specs=vm,
        out_shape=jax.ShapeDtypeStruct((12, 12, 4, 384), F32),
        compiler_params=pltpu.CompilerParams(vmem_limit_bytes=SMALL),
        cost_estimate=pl.CostEstimate(flops=2 * 8 * VLOC * TAIL, bytes_accessed=5_000_000, transcendentals=0),
        name="late",
    )(top, vertex, keep, last, solved, pz, tile)


def exchange(value, mask):
    return lax.ppermute(value, ("gx", "gy"), [(i, i ^ mask) for i in range(128)])


def odd_pairs(value, axis):
    count = lax.axis_size(axis)
    return lax.ppermute(value, axis, [(i, (i + 1) % count if i % 2 else (i - 1) % count) for i in range(count)])


MASKS = (1, 3, 4, 12, 16, 32, 96)


def local(residual, sx, sy, depth_vectors, lam_x, lam_y, lam_z, coarse_factor):
    factor = coarse_factor.reshape(VLOC, COLS)
    field = residual.transpose(1, 2, 0, 3)
    msg, own, y2, x1, x2, kept = forward(field, factor)
    got1 = exchange(msg, 1)
    got2 = odd_pairs(y2, "gy")
    tabs = tables(
        own, sx, sy, depth_vectors.transpose(1, 2, 0).reshape(64, 64), lam_x, lam_y, lam_z.transpose(1, 0)
    )
    sep = msg[:, : LEVELS * SEP] + got1[:, : LEVELS * SEP]
    done = [sep[:, :SEP]]
    sep = sep[:, SEP:]
    for mask in MASKS[1:]:
        sep = sep + exchange(sep, mask)
        done.append(sep[:, :SEP])
        sep = sep[:, SEP:]
    m1, m2 = faces(done[FACES_AFTER - 1], x1, x2, got1, got2)
    m1 = exchange(m1, 16)
    m2 = odd_pairs(m2, "gx")
    parts = [
        schwarz(first, count, done[level - 1], field, got1, got2, m1, m2, tabs)
        for first, count, level in SCHWARZ_AFTER
    ]
    vertex, keep, last, pz, tile = early(done[EARLY_AFTER - 1], jnp.concatenate(done[:5], axis=1), own, kept)
    solved = jnp.concatenate(parts, axis=0).reshape(4, 12, 16, 384)[:, :, :12].transpose(1, 2, 0, 3)
    top = jnp.concatenate([done[4][:, SEP - LEAF :], done[5], done[6], jnp.zeros((4, TAIL_WIDE - TAIL), F32)], axis=1)
    out = late(top, vertex, keep, last, solved, pz, tile)
    return out.transpose(2, 0, 1, 3)


FACES_AFTER = 2
SCHWARZ_AFTER = ((0, 1, 3), (1, 1, 3), (2, 1, 4), (3, 1, 5))
EARLY_AFTER = 5


def solution(mesh):
    return jax.shard_map(
        local,
        mesh=mesh,
        in_specs=(
            P(None, "gx", "gy", None),
            P("gx", None, None),
            P("gy", None, None),
            P(),
            P("gx", None),
            P("gy", None),
            P(),
            P("gx", "gy", None, None),
        ),
        out_specs=P(None, "gx", "gy", None),
        check_vma=False,
    )
```

profile of v0, /device:TPU:1, one launch (start us, length us, event | category | flops | bytes accessed | tf_op | source)
XLA Modules:
  0.0 54.7 jit_solution(789563621484201778)
XLA Ops:
  0.0 1.2 %copy-done = f32[4,12,12,384]{3,0,2,1:T(4,128)S(1)} copy-done((f32[4,12,12,384]{3,0,2,1:T(4,128)S(1)}, f32[4,12,12,384]{3,0,2,1:T(4,128)}, u32[]{:S(2)}) %copy-start) | copy-done | bytes 884760
  1.2 0.9 %copy-done.2 = bf16[2,384,128]{2,1,0:T(8,128)(2,1)S(1)} copy-done((bf16[2,384,128]{2,1,0:T(8,128)(2,1)S(1)}, bf16[2,384,128]{2,1,0:T(8,128)(2,1)}, u32[]{:S(2)}) %copy-start.2) | copy-done | bytes 196632
  2.1 0.9 %copy-done.6 = bf16[128,640]{1,0:T(8,128)(2,1)S(1)} copy-done((bf16[128,640]{1,0:T(8,128)(2,1)S(1)}, bf16[128,640]{1,0:T(8,128)(2,1)}, u32[]{:S(2)}) %copy-start.6) | copy-done | bytes 163864
  3.0 7.6 %forward.1 = (f32[4,11776]{1,0:T(4,128)S(1)}, f32[4,128]{1,0:T(4,128)S(1)}, f32[4,4608]{1,0:T(4,128)S(1)}, f32[4,4608]{1,0:T(4,128)S(1)}, f32[4,4608]{1,0:T(4,128)S(1)}, /*index=5*/bf16[585,7233]{1,0:T(8,128)(2,1)}) custom-call(f32[12,12,4,384]{3,2,1,0:T(4,128)S(1)} %bitcast.10, bf16[2,384,128]{2,1,0:T(8,128)(2,1)S(1)} %copy-done.2, ...), custom_call_target="tpu_custom_call" | custom-call | flops 67700880 | bytes 9500000 | tf_op jit(solution)/shard_map/forward/pallas_call | solution.py:176
  10.7 2.1 %collective-permute-start = (f32[4,11776]{1,0:T(4,128)S(1)}, f32[4,11776]{1,0:T(4,128)S(1)}, u32[]{:S(2)}, u32[]{:S(2)}) collective-permute-start(f32[4,11776]{1,0:T(4,128)S(1)} %get-tuple-element.23), channel_id=1, source_target_pairs={{0,1},{1,0},{2,3},{3,2},{4,5},{5,4},{6,7},{7,6},{8,9},{9,8},{10,11... | collective-permute-start | bytes 565256 | tf_op jit(solution)/shard_map/ppermute | solution.py:461
  12.8 4.3 %collective-permute-start.7 = (f32[4,4608]{1,0:T(4,128)S(1)}, f32[4,4608]{1,0:T(4,128)S(1)}, u32[]{:S(2)}, u32[]{:S(2)}) collective-permute-start(f32[4,4608]{1,0:T(4,128)S(1)} %get-tuple-element.29), channel_id=1, source_target_pairs={{0,15},{1,2},{2,1},{3,4},{4,3},{5,6},{6,5},{7,8},{8,7},{9,10},{10,... | collective-permute-start | bytes 221192 | tf_op jit(solution)/shard_map/ppermute | solution.py:466
  17.1 1.1 %tables.1 = (bf16[2,256,256]{2,1,0:T(8,128)(2,1)S(1)}, bf16[2,256,256]{2,1,0:T(8,128)(2,1)S(1)}, bf16[2,2,256,256]{3,2,1,0:T(8,128)(2,1)S(1)}, bf16[2,2,256,256]{3,2,1,0:T(8,128)(2,1)S(1)}, f32[256,512]{1,0:T(8,128)S(1)}) custom-call(f32[4,128]{1,0:T(4,128)S(1)} %get-tuple-element.24.own_ref.wait_ref, f32[2,8,8]{2,1,0:T(8,128)S(1)} %copy-done.12, ...), custom_call_target="tpu_custom_call" | custom-call | flops 1000000000 | bytes 2000000 | tf_op jit(solution)/shard_map/tables/pallas_call | solution.py:302
  18.3 1.5 %collective-permute-start.1 = (f32[4,6144]{1,0:T(4,128)S(1)}, f32[4,6144]{1,0:T(4,128)S(1)}, u32[]{:S(2)}, u32[]{:S(2)}) collective-permute-start(f32[4,6144]{1,0:T(4,128)S(1)} %slice.66), channel_id=1, source_target_pairs={{0,3},{1,2},{2,1},{3,0},{4,7},{5,6},{6,5},{7,4},{8,11},{9,10},{10,... | collective-permute-start | bytes 294920 | tf_op jit(solution)/shard_map/ppermute | solution.py:461
  19.8 3.3 %collective-permute-done.1 = f32[4,6144]{1,0:T(4,128)S(1)} collective-permute-done((f32[4,6144]{1,0:T(4,128)S(1)}, f32[4,6144]{1,0:T(4,128)S(1)}, u32[]{:S(2)}, u32[]{:S(2)}) %collective-permute-start.1) | collective-permute-done | bytes 98336 | tf_op jit(solution)/shard_map/ppermute | solution.py:461
  23.5 3.1 %collective-permute-start.8 = (f32[4,5376]{1,0:T(4,128)S(1)}, f32[4,5376]{1,0:T(4,128)S(1)}, u32[]{:S(2)}, u32[]{:S(2)}) collective-permute-start(f32[4,5376]{1,0:T(4,128)S(1)} %get-tuple-element.32), channel_id=1, source_target_pairs={{0,16},{1,17},{2,18},{3,19},{4,20},{5,21},{6,22},{7,23},{8,24},{9,... | collective-permute-start | bytes 258056 | tf_op jit(solution)/shard_map/ppermute | solution.py:461
  26.5 1.6 %collective-permute-start.9 = (f32[4,5376]{1,0:T(4,128)S(1)}, f32[4,5376]{1,0:T(4,128)S(1)}, u32[]{:S(2)}, u32[]{:S(2)}) collective-permute-start(f32[4,5376]{1,0:T(4,128)S(1)} %get-tuple-element.33), channel_id=1, source_target_pairs={{0,112},{16,32},{32,16},{48,64},{64,48},{80,96},{96,80},{112,0},{1... | collective-permute-start | bytes 258056 | tf_op jit(solution)/shard_map/ppermute | solution.py:466
  28.2 2.0 %collective-permute-start.3 = (f32[4,4096]{1,0:T(4,128)S(1)}, f32[4,4096]{1,0:T(4,128)S(1)}, u32[]{:S(2)}, u32[]{:S(2)}) collective-permute-start(f32[4,4096]{1,0:T(4,128)S(1)} %slice.68), channel_id=1, source_target_pairs={{0,12},{1,13},{2,14},{3,15},{4,8},{5,9},{6,10},{7,11},{8,4},{9,5},... | collective-permute-start | bytes 196616 | tf_op jit(solution)/shard_map/ppermute | solution.py:461
  30.4 1.5 %schwarz.5 = f32[1,192,384]{2,1,0:T(8,128)S(1)} custom-call(f32[4,1024]{1,0:T(4,128)S(1)} %get-tuple-element.43.refs_0_, f32[12,12,4,384]{3,2,1,0:T(4,128)S(1)} %bitcast.11, f32[4,11776]{1,0:T(4,128)S(1)} %collective-permute-done.y1_ref.refs_2_, f32[4,4608]{1,0:T(4,128)S(1)} %collective-permute-done.7.y2_ref.refs_3_, ...), custom_call_target="tpu_custom_call" | custom-call | flops 900000000 | bytes 700000 | tf_op jit(solution)/shard_map/schwarz/pallas_call | solution.py:357
  31.9 1.5 %schwarz.4 = f32[1,192,384]{2,1,0:T(8,128)S(1)} custom-call(f32[4,1024]{1,0:T(4,128)S(1)} %get-tuple-element.43.refs_0_, f32[12,12,4,384]{3,2,1,0:T(4,128)S(1)} %bitcast.12, f32[4,11776]{1,0:T(4,128)S(1)} %collective-permute-done.y1_ref.refs_2_, f32[4,4608]{1,0:T(4,128)S(1)} %collective-permute-done.7.y2_ref.refs_3_, ...), custom_call_target="tpu_custom_call" | custom-call | flops 900000000 | bytes 700000 | tf_op jit(solution)/shard_map/schwarz/pallas_call | solution.py:357
  33.4 3.0 %collective-permute-start.4 = (f32[4,3072]{1,0:T(4,128)S(1)}, f32[4,3072]{1,0:T(4,128)S(1)}, u32[]{:S(2)}, u32[]{:S(2)}) collective-permute-start(f32[4,3072]{1,0:T(4,128)S(1)} %slice.69), channel_id=1, source_target_pairs={{0,16},{1,17},{2,18},{3,19},{4,20},{5,21},{6,22},{7,23},{8,24},{9,... | collective-permute-start | bytes 147464 | tf_op jit(solution)/shard_map/ppermute | solution.py:461
  36.4 1.5 %schwarz.6 = f32[1,192,384]{2,1,0:T(8,128)S(1)} custom-call(f32[4,1024]{1,0:T(4,128)S(1)} %get-tuple-element.45.refs_0_, f32[12,12,4,384]{3,2,1,0:T(4,128)S(1)} %bitcast.13, f32[4,11776]{1,0:T(4,128)S(1)} %collective-permute-done.y1_ref.refs_2_, f32[4,4608]{1,0:T(4,128)S(1)} %collective-permute-done.7.y2_ref.refs_3_, ...), custom_call_target="tpu_custom_call" | custom-call | flops 900000000 | bytes 700000 | tf_op jit(solution)/shard_map/schwarz/pallas_call | solution.py:357
  37.9 1.1 %collective-permute-start.5 = (f32[4,2048]{1,0:T(4,128)S(1)}, f32[4,2048]{1,0:T(4,128)S(1)}, u32[]{:S(2)}, u32[]{:S(2)}) collective-permute-start(f32[4,2048]{1,0:T(4,128)S(1)} %slice.71), channel_id=1, source_target_pairs={{0,32},{1,33},{2,34},{3,35},{4,36},{5,37},{6,38},{7,39},{8,40},{9,... | collective-permute-start | bytes 98312 | tf_op jit(solution)/shard_map/ppermute | solution.py:461
  39.0 1.5 %schwarz.7 = f32[1,192,384]{2,1,0:T(8,128)S(1)} custom-call(f32[4,1024]{1,0:T(4,128)S(1)} %get-tuple-element.48.wait_ref.refs_0_, f32[12,12,4,384]{3,2,1,0:T(4,128)S(1)} %bitcast.14, f32[4,11776]{1,0:T(4,128)S(1)} %collective-permute-done.y1_ref.refs_2_, f32[4,4608]{1,0:T(4,128)S(1)} %collective-permute-done.7.y2_ref.refs_3_, ...), custom_call_target="tpu_custom_call" | custom-call | flops 900000000 | bytes 700000 | tf_op jit(solution)/shard_map/schwarz/pallas_call | solution.py:357
  41.4 2.6 %collective-permute-start.6 = (f32[4,1024]{1,0:T(4,128)S(1)}, f32[4,1024]{1,0:T(4,128)S(1)}, u32[]{:S(2)}, u32[]{:S(2)}) collective-permute-start(f32[4,1024]{1,0:T(4,128)S(1)} %slice.73), channel_id=1, source_target_pairs={{0,96},{1,97},{2,98},{3,99},{4,100},{5,101},{6,102},{7,103},{8,104... | collective-permute-start | bytes 49160 | tf_op jit(solution)/shard_map/ppermute | solution.py:461
  44.3 2.6 %early.1 = (f32[8,640]{1,0:T(8,128)S(1)}, bf16[585,2048]{1,0:T(8,128)(2,1)S(1)}, bf16[585,128]{1,0:T(8,128)(2,1)S(1)}, bf16[2,128,384]{2,1,0:T(8,128)(2,1)S(1)}, bf16[640,128]{1,0:T(8,128)(2,1)S(1)}) custom-call(f32[4,1024]{1,0:T(4,128)S(1)} %get-tuple-element.48.wait_ref.refs_0_, f32[4,5120]{1,0:T(4,128)S(1)} %get-tuple-element.47.sep_ref, ...), custom_call_target="tpu_custom_call" | custom-call | flops 47923200 | bytes 9000000 | tf_op jit(solution)/shard_map/early/pallas_call | solution.py:402
  48.8 0.8 %concatenate.9.top_ref = f32[4,2176]{1,0:T(4,128)S(1)} concatenate(f32[4,65]{1,0:T(4,128)S(1)} %slice.70, f32[4,1024]{1,0:T(4,128)} %get-tuple-element.50, f32[4,1024]{1,0:T(4,128)} %get-tuple-element.49, f32[4,63]{1,0:T(4,128)S(1)} %broadcast_in_dim.3), dimensions={1} | concatenate | bytes 69632 | tf_op jit(solution)/shard_map/concatenate | solution.py:497
  49.6 0.9 %copy-done.4 = bf16[640,128]{1,0:T(8,128)(2,1)S(1)} copy-done((bf16[640,128]{1,0:T(8,128)(2,1)S(1)}, bf16[640,128]{1,0:T(8,128)(2,1)}, u32[]{:S(2)}) %copy-start.4) | copy-done | bytes 163864
  50.6 0.9 %copy-done.8 = bf16[585,128]{1,0:T(8,128)(2,1)S(1)} copy-done((bf16[585,128]{1,0:T(8,128)(2,1)S(1)}, bf16[585,128]{1,0:T(8,128)(2,1)}, u32[]{:S(2)}) %copy-start.8) | copy-done | bytes 149784
  52.2 2.6 %late.1 = f32[12,12,4,384]{3,2,1,0:T(4,128)} custom-call(f32[4,2176]{1,0:T(4,128)S(1)} %concatenate.9.top_ref, f32[8,640]{1,0:T(8,128)S(1)} %copy-done.10, bf16[585,2048]{1,0:T(8,128)(2,1)S(1)} %get-tuple-element.27.keep_ref, bf16[585,128]{1,0:T(8,128)(2,1)S(1)} %copy-done.8, f32[12,12,4,384]{3,2,1,0:T(4,128)S(1)} %slice_bitcast_fusion.s_ref, ...), custom_call_target="tpu_custom_call" | custom-call | flops 19777680 | bytes 5000000 | tf_op jit(solution)/shard_map/late/pallas_call | solution.py:449
  (70 shorter events, 4.6 us)
Async XLA Ops:
  0.0 1.2 %copy-start = (f32[4,12,12,384]{3,0,2,1:T(4,128)S(1)}, f32[4,12,12,384]{3,0,2,1:T(4,128)}, u32[]{:S(2)}) copy-start(f32[4,12,12,384]{3,0,2,1:T(4,128)} %param.14) | copy-start | bytes 2654212
  1.2 0.9 %copy-start.2 = (bf16[2,384,128]{2,1,0:T(8,128)(2,1)S(1)}, bf16[2,384,128]{2,1,0:T(8,128)(2,1)}, u32[]{:S(2)}) copy-start(bf16[2,384,128]{2,1,0:T(8,128)(2,1)} %constant.28.rz_hbm) | copy-start | bytes 589828
  3.0 14.1 %copy-start.11 = (f32[64,8,8]{0,2,1:T(8,128)S(1)}, f32[64,8,8]{0,2,1:T(8,128)}, u32[]{:S(2)}) copy-start(f32[64,8,8]{0,2,1:T(8,128)} %param.17) | copy-start | bytes 49156
  3.0 14.1 %copy-start.12 = (f32[2,8,8]{2,1,0:T(8,128)S(1)}, f32[2,8,8]{2,1,0:T(8,128)}, u32[]{:S(2)}) copy-start(f32[2,8,8]{2,1,0:T(8,128)} %sx_ref.1) | copy-start | bytes 1540
  3.0 14.1 %copy-start.13 = (f32[2,8,8]{2,1,0:T(8,128)S(1)}, f32[2,8,8]{2,1,0:T(8,128)}, u32[]{:S(2)}) copy-start(f32[2,8,8]{2,1,0:T(8,128)} %sy_ref.1) | copy-start | bytes 1540
  3.0 14.1 %copy-start.14 = (f32[64,8]{0,1:T(8,128)S(1)}, f32[64,8]{0,1:T(8,128)}, u32[]{:S(2)}) copy-start(f32[64,8]{0,1:T(8,128)} %param.20) | copy-start | bytes 6148
  3.0 14.1 %copy-start.15 = (f32[2,8]{1,0:T(2,128)S(1)}, f32[2,8]{1,0:T(2,128)}, u32[]{:S(2)}) copy-start(f32[2,8]{1,0:T(2,128)} %lx_ref.1) | copy-start | bytes 196
  3.0 14.1 %copy-start.16 = (f32[2,8]{1,0:T(2,128)S(1)}, f32[2,8]{1,0:T(2,128)}, u32[]{:S(2)}) copy-start(f32[2,8]{1,0:T(2,128)} %ly_ref.1) | copy-start | bytes 196
  10.7 7.6 %collective-permute-start = (f32[4,11776]{1,0:T(4,128)S(1)}, f32[4,11776]{1,0:T(4,128)S(1)}, u32[]{:S(2)}, u32[]{:S(2)}) collective-permute-start(f32[4,11776]{1,0:T(4,128)S(1)} %get-tuple-element.23), channel_id=1, source_target_pairs={{0,1},{1,0},{2,3},{3,2},{4,5},{5,4},{6,7},{7,6},{8,9},{9,8},{10,11... | collective-permute-start | bytes 565256 | tf_op jit(solution)/shard_map/ppermute | solution.py:461
  12.8 10.6 %collective-permute-start.7 = (f32[4,4608]{1,0:T(4,128)S(1)}, f32[4,4608]{1,0:T(4,128)S(1)}, u32[]{:S(2)}, u32[]{:S(2)}) collective-permute-start(f32[4,4608]{1,0:T(4,128)S(1)} %get-tuple-element.29), channel_id=1, source_target_pairs={{0,15},{1,2},{2,1},{3,4},{4,3},{5,6},{6,5},{7,8},{8,7},{9,10},{10,... | collective-permute-start | bytes 221192 | tf_op jit(solution)/shard_map/ppermute | solution.py:466
  18.3 4.8 %collective-permute-start.1 = (f32[4,6144]{1,0:T(4,128)S(1)}, f32[4,6144]{1,0:T(4,128)S(1)}, u32[]{:S(2)}, u32[]{:S(2)}) collective-permute-start(f32[4,6144]{1,0:T(4,128)S(1)} %slice.66), channel_id=1, source_target_pairs={{0,3},{1,2},{2,1},{3,0},{4,7},{5,6},{6,5},{7,4},{8,11},{9,10},{10,... | collective-permute-start | bytes 294920 | tf_op jit(solution)/shard_map/ppermute | solution.py:461
  23.1 5.0 %collective-permute-start.2 = (f32[4,5120]{1,0:T(4,128)S(1)}, f32[4,5120]{1,0:T(4,128)S(1)}, u32[]{:S(2)}, u32[]{:S(2)}) collective-permute-start(f32[4,5120]{1,0:T(4,128)S(1)} %slice.67), channel_id=1, source_target_pairs={{0,4},{1,5},{2,6},{3,7},{4,0},{5,1},{6,2},{7,3},{8,12},{9,13},{10,... | collective-permute-start | bytes 245768 | tf_op jit(solution)/shard_map/ppermute | solution.py:461
  23.5 6.7 %collective-permute-start.8 = (f32[4,5376]{1,0:T(4,128)S(1)}, f32[4,5376]{1,0:T(4,128)S(1)}, u32[]{:S(2)}, u32[]{:S(2)}) collective-permute-start(f32[4,5376]{1,0:T(4,128)S(1)} %get-tuple-element.32), channel_id=1, source_target_pairs={{0,16},{1,17},{2,18},{3,19},{4,20},{5,21},{6,22},{7,23},{8,24},{9,... | collective-permute-start | bytes 258056 | tf_op jit(solution)/shard_map/ppermute | solution.py:461
  26.5 3.9 %collective-permute-start.9 = (f32[4,5376]{1,0:T(4,128)S(1)}, f32[4,5376]{1,0:T(4,128)S(1)}, u32[]{:S(2)}, u32[]{:S(2)}) collective-permute-start(f32[4,5376]{1,0:T(4,128)S(1)} %get-tuple-element.33), channel_id=1, source_target_pairs={{0,112},{16,32},{32,16},{48,64},{64,48},{80,96},{96,80},{112,0},{1... | collective-permute-start | bytes 258056 | tf_op jit(solution)/shard_map/ppermute | solution.py:466
  28.2 5.2 %collective-permute-start.3 = (f32[4,4096]{1,0:T(4,128)S(1)}, f32[4,4096]{1,0:T(4,128)S(1)}, u32[]{:S(2)}, u32[]{:S(2)}) collective-permute-start(f32[4,4096]{1,0:T(4,128)S(1)} %slice.68), channel_id=1, source_target_pairs={{0,12},{1,13},{2,14},{3,15},{4,8},{5,9},{6,10},{7,11},{8,4},{9,5},... | collective-permute-start | bytes 196616 | tf_op jit(solution)/shard_map/ppermute | solution.py:461
  30.4 13.8 %slice-start = ((s8[8638464]{0:T(1024)(128)(4,1)}), s8[4194304]{0:T(1024)(128)(4,1)S(1)}, s32[]{:S(2)}) async-start(s8[8638464]{0:T(1024)(128)(4,1)} %bitcast.15), calls=%async_computation | async-start | bytes 8388608
  31.9 12.3 %slice-start.1 = ((s8[8638464]{0:T(1024)(128)(4,1)}), s8[4194304]{0:T(1024)(128)(4,1)S(1)}, s32[]{:S(2)}) async-start(s8[8638464]{0:T(1024)(128)(4,1)} %bitcast.15), calls=%async_computation.1 | async-start | bytes 8388608
  33.4 4.4 %collective-permute-start.4 = (f32[4,3072]{1,0:T(4,128)S(1)}, f32[4,3072]{1,0:T(4,128)S(1)}, u32[]{:S(2)}, u32[]{:S(2)}) collective-permute-start(f32[4,3072]{1,0:T(4,128)S(1)} %slice.69), channel_id=1, source_target_pairs={{0,16},{1,17},{2,18},{3,19},{4,20},{5,21},{6,22},{7,23},{8,24},{9,... | collective-permute-start | bytes 147464 | tf_op jit(solution)/shard_map/ppermute | solution.py:461
  37.9 3.5 %collective-permute-start.5 = (f32[4,2048]{1,0:T(4,128)S(1)}, f32[4,2048]{1,0:T(4,128)S(1)}, u32[]{:S(2)}, u32[]{:S(2)}) collective-permute-start(f32[4,2048]{1,0:T(4,128)S(1)} %slice.71), channel_id=1, source_target_pairs={{0,32},{1,33},{2,34},{3,35},{4,36},{5,37},{6,38},{7,39},{8,40},{9,... | collective-permute-start | bytes 98312 | tf_op jit(solution)/shard_map/ppermute | solution.py:461
  39.0 5.2 %slice-start.2 = ((s8[8638464]{0:T(1024)(128)(4,1)}), s8[249856]{0:T(1024)(128)(4,1)S(1)}, s32[]{:S(2)}) async-start(s8[8638464]{0:T(1024)(128)(4,1)} %bitcast.15), calls=%async_computation.2 | async-start | bytes 499712
  41.4 2.9 %copy-start.1 = (bf16[2,128,384]{2,1,0:T(8,128)(2,1)S(1)}, bf16[2,128,384]{2,1,0:T(8,128)(2,1)}, u32[]{:S(2)}) copy-start(bf16[2,128,384]{2,1,0:T(8,128)(2,1)} %constant.31.pz_hbm) | copy-start | bytes 589828
  41.4 2.9 %copy-start.5 = (bf16[640,128]{1,0:T(8,128)(2,1)S(1)}, bf16[640,128]{1,0:T(8,128)(2,1)}, u32[]{:S(2)}) copy-start(bf16[640,128]{1,0:T(8,128)(2,1)} %constant.19.clone.tile_hbm) | copy-start | bytes 491524
  41.4 6.7 %collective-permute-start.6 = (f32[4,1024]{1,0:T(4,128)S(1)}, f32[4,1024]{1,0:T(4,128)S(1)}, u32[]{:S(2)}, u32[]{:S(2)}) collective-permute-start(f32[4,1024]{1,0:T(4,128)S(1)} %slice.73), channel_id=1, source_target_pairs={{0,96},{1,97},{2,98},{3,99},{4,100},{5,101},{6,102},{7,103},{8,104... | collective-permute-start | bytes 49160 | tf_op jit(solution)/shard_map/ppermute | solution.py:461
  49.6 0.9 %copy-start.4 = (bf16[640,128]{1,0:T(8,128)(2,1)S(1)}, bf16[640,128]{1,0:T(8,128)(2,1)}, u32[]{:S(2)}) copy-start(bf16[640,128]{1,0:T(8,128)(2,1)} %copy-done.3) | copy-start | bytes 491524
  (6 other events, 4.5 us)
where the time goes:
time: 55.1 us; the launch traced here: 54.7 us
  starting transfers between devices  21.4 us (39%)
  Pallas kernels  19.8 us (36%)
  local copies, waits for them, and re-layouts  8.84 us (16%)
  waiting for transfers between devices  3.55 us (6%)
  other arithmetic  0.82 us (1%)
    ppermute x8, starting transfers between devices, exchange(): lax.ppermute(value, ('gx', 'gy'), [(i, i ^ mask) for i in range(128)])  15.5 us
    pallas_call x1, Pallas kernels, forward(): pl.pallas_call(forward_kernel, in_specs=[HBM] * 4, out_specs=[vm] * 6, ou...  7.63 us
    unnamed x41, local copies, waits for them, and re-layouts  6.93 us
    ppermute x2, starting transfers between devices, odd_pairs(): lax.ppermute(value, axis, [(i, (i + 1) % count if i % 2 else (i - 1) % co...  5.88 us
    pallas_call x4, Pallas kernels, schwarz(): pl.pallas_call(kernel, in_specs=[UNUSED] + [vm] * 10, out_specs=vm, out_s...  5.86 us
    ppermute x8, waiting for transfers between devices, exchange(): lax.ppermute(value, ('gx', 'gy'), [(i, i ^ mask) for i in range(128)])  3.3 us
    pallas_call x1, Pallas kernels, early(): pl.pallas_call(early_kernel, in_specs=[UNUSED, vm, vm, vm, HBM, HBM], out...  2.57 us
    pallas_call x1, Pallas kernels, late(): pl.pallas_call(late_kernel, in_specs=[vm] * 7, out_specs=vm, out_shape=ja...  2.55 us
  transfers between devices with their start and end apart: 10, of which 2 were waited for; matrix products, arithmetic and copies ran while one was open for 2% of the time, Pallas kernels for 18%

commit v1 on v0

--- a/solution.py
+++ b/solution.py
@@ -82,13 +82,11 @@
 
 FACE = 12 * 384
 SLAB = 14 * 384
-CUT = 5120
-TAIL = COLS - CUT
-TAIL_WIDE = 2176
 PADDED = 7296
-BIG = 51 << 20
+BIG = 58 << 20
 ROW_CHUNKS = ((512, 73), (0, 256), (256, 128), (384, 128))
 SMALL = 24 << 20
+MIDDLE = 48 << 20
 HBM = pl.BlockSpec(memory_space=pltpu.HBM)
 UNUSED = pl.BlockSpec(memory_space=pl.ANY)
 
@@ -103,8 +101,8 @@
 
 def forward_kernel(
     r_hbm, rz_hbm, tile_hbm, f_ref,
-    msg_ref, own_ref, y2_ref, x1_ref, x2_ref, keep_ref,
-    r_ref, rz_ref, tile_ref, u_ref, acc_ref, small_sems, sems,
+    msg_ref, own_ref, y2_ref, x1_ref, x2_ref,
+    r_ref, rz_ref, tile_ref, keep_ref, u_ref, acc_ref, small_sems, sems,
 ):
     small = []
     for k, (src, dst) in enumerate(((r_hbm, r_ref), (rz_hbm, rz_ref), (tile_hbm, tile_ref))):
@@ -114,10 +112,12 @@
     for k, (start, size) in enumerate(ROW_CHUNKS):
         rows = pl.ds(start, size)
         copies.append(pltpu.make_async_copy(f_ref.at[rows, :], keep_ref.at[rows, :], sems.at[k]))
-        copies[-1].start()
+    copies[0].start()
 
     u_ref[...] = jnp.zeros_like(u_ref)
     small[0].wait()
+    for copy in copies[1:]:
+        copy.start()
     r0 = [float(v) for v in restrict_np[0]]
     r1 = [float(v) for v in restrict_np[1]]
     for y_elem in range(2):
@@ -138,7 +138,10 @@
                 row = (a * 3 + y_elem + t) * 8
                 u_ref[row : row + 4, :] += sum(table[j] * sums[j][a] for j in range(6))
     small[1].wait()
-    vert = dot3(split(u_ref[...]), (rz_ref[0], rz_ref[1])).astype(BF)
+    vert = lax.dot_general(
+        u_ref[...], rz_ref[...], (((1,), (0,)), ((), ())),
+        precision=lax.Precision.HIGHEST, preferred_element_type=F32,
+    ).astype(BF)
     small[2].wait()
     spread = dot(vert, tile_ref[...])
     spread = jnp.where(ab_mask(72, 640), spread, 0.0)
@@ -176,12 +179,13 @@
     return pl.pallas_call(
         forward_kernel,
         in_specs=[HBM] * 4,
-        out_specs=[vm] * 6,
-        out_shape=[jax.ShapeDtypeStruct(v, F32) for v in shapes] + [jax.ShapeDtypeStruct((VLOC, COLS), BF)],
+        out_specs=[vm] * 5,
+        out_shape=[jax.ShapeDtypeStruct(v, F32) for v in shapes],
         scratch_shapes=[
             pltpu.VMEM((12, 12, 4, 384), F32),
-            pltpu.VMEM((2, 384, 128), BF),
+            pltpu.VMEM((384, 128), F32),
             pltpu.VMEM((128, 640), BF),
+            pltpu.VMEM((VLOC, COLS), BF),
             pltpu.VMEM((72, 384), F32),
             pltpu.VMEM((8, PADDED), F32),
             pltpu.SemaphoreType.DMA((3,)),
@@ -190,7 +194,28 @@
         compiler_params=pltpu.CompilerParams(vmem_limit_bytes=BIG),
         cost_estimate=pl.CostEstimate(flops=2 * 8 * VLOC * COLS, bytes_accessed=9_500_000, transcendentals=0),
         name="forward",
-    )(field, jnp.stack([jnp.asarray(v) for v in split_np(rz)]), jnp.asarray(tile), factor)
+    )(field, jnp.asarray(rz), jnp.asarray(tile), factor)
+
+
+def join_kernel(msg_ref, y1_ref, y2_ref, level_ref, rest_ref):
+    level_ref[...] = msg_ref[:, :SEP] + y1_ref[:, :SEP]
+    rest_ref[...] = msg_ref[:, SEP : LEVELS * SEP] + y1_ref[:, SEP : LEVELS * SEP]
+
+
+def join(msg, y1, y2):
+    vm = pl.BlockSpec(memory_space=pltpu.VMEM)
+    return pl.pallas_call(
+        join_kernel,
+        in_specs=[vm, vm, UNUSED],
+        out_specs=[vm] * 2,
+        out_shape=[
+            jax.ShapeDtypeStruct((4, SEP), F32),
+            jax.ShapeDtypeStruct((4, (LEVELS - 1) * SEP), F32),
+        ],
+        compiler_params=pltpu.CompilerParams(vmem_limit_bytes=MIDDLE),
+        cost_estimate=pl.CostEstimate(flops=30_000, bytes_accessed=400_000, transcendentals=0),
+        name="join",
+    )(msg, y1, y2)
 
 
 def faces_kernel(wait_ref, x1_ref, x2_ref, y1_ref, y2_ref, m1_ref, m2_ref):
@@ -316,8 +341,48 @@
     )(wait, sx, sy, dt, lx, ly, lz)
 
 
-def schwarz_kernel(
-    first, wait_ref, r_ref, y1_ref, y2_ref, m1_ref, m2_ref, a_ref, b_ref, zf_ref, zb_ref, rs_ref, out_ref, x_ref
+def shifted(left, right):
+    pair = jnp.concatenate([left, right], axis=1)
+    pair = jnp.concatenate([pair, jnp.zeros((4, 2 * SEP), F32)], axis=0)
+    return pltpu.roll(pair, LEAF, 1)[:, SEP:]
+
+
+def chunk_values(chunk, level_refs):
+    if chunk:
+        return shifted(level_refs[0][...], level_refs[1][...]).astype(BF)
+    own, level = level_refs
+    lane = lax.broadcasted_iota(jnp.int32, (4, 128), 1)
+    rest = pltpu.roll(jnp.concatenate([level[...], jnp.zeros((4, SEP), F32)], axis=0), LEAF, 1)
+    head = jnp.where(lane < LEAF, own[...], rest[:4, :128])
+    head = jnp.concatenate([head, jnp.zeros((4, 128), F32)], axis=0)
+    return jnp.concatenate([head, rest[:, 128:]], axis=1).astype(BF)
+
+
+def schwarz_kernel(first, chunks, *refs):
+    wait_ref, r_ref, y1_ref, y2_ref, m1_ref, m2_ref, a_ref, b_ref, zf_ref, zb_ref, rs_ref = refs[:11]
+    refs = refs[11:]
+    level_refs = refs[: len(chunks) + 1] if chunks else ()
+    refs = refs[len(level_refs) :]
+    if chunks:
+        f_ref, out_ref, v_ref, x_ref, chunk_ref, sem = refs
+        cols = pl.ds(chunks[0] * SEP, len(chunks) * SEP)
+        copy = pltpu.make_async_copy(f_ref.at[:, cols], chunk_ref, sem)
+        copy.start()
+    else:
+        out_ref, x_ref = refs
+    schwarz_body(first, r_ref, y1_ref, y2_ref, m1_ref, m2_ref, a_ref, b_ref, zf_ref, zb_ref, rs_ref, out_ref, x_ref)
+    if chunks:
+        copy.wait()
+        total = jnp.zeros((8, VLOC), F32)
+        for k, chunk in enumerate(chunks):
+            values = chunk_values(chunk, level_refs[k : k + 2])
+            total = total + dot(values, chunk_ref[:, k * SEP : k * SEP + SEP], NT)
+        v_ref[:, :VLOC] = total
+        v_ref[:, VLOC:] = jnp.zeros((8, 640 - VLOC), F32)
+
+
+def schwarz_body(
+    first, r_ref, y1_ref, y2_ref, m1_ref, m2_ref, a_ref, b_ref, zf_ref, zb_ref, rs_ref, out_ref, x_ref
 ):
     gy_odd, gx_odd = parities()
     tail = LEVELS * SEP
@@ -351,85 +416,107 @@
         out_ref[k] = dot3((b_ref[0][:192], b_ref[1][:192]), t4)
 
 
-def schwarz(first, count, wait, field, y1, y2, m1, m2, tabs):
+def schwarz(first, wait, chunks, levels, factor, field, y1, y2, m1, m2, tabs):
     vm = pl.BlockSpec(memory_space=pltpu.VMEM)
-    kernel = lambda *refs: schwarz_kernel(first, *refs)
+    kernel = lambda *refs: schwarz_kernel(first, chunks, *refs)
+    extra = (*levels, factor) if chunks else ()
+    out = jax.ShapeDtypeStruct((1, 192, 384), F32)
+    scratch = [pltpu.VMEM((1, 224, 384), F32)]
+    if chunks:
+        scratch += [pltpu.VMEM((VLOC, len(chunks) * SEP), BF), pltpu.SemaphoreType.DMA]
     return pl.pallas_call(
         kernel,
-        in_specs=[UNUSED] + [vm] * 10,
-        out_specs=vm,
-        out_shape=jax.ShapeDtypeStruct((count, 192, 384), F32),
-        scratch_shapes=[pltpu.VMEM((count, 224, 384), F32)],
-        compiler_params=pltpu.CompilerParams(vmem_limit_bytes=SMALL),
-        cost_estimate=pl.CostEstimate(flops=900_000_000 * count, bytes_accessed=700_000 * count, transcendentals=0),
+        in_specs=[UNUSED] + [vm] * 10 + ([vm] * len(levels) + [HBM] if chunks else []),
+        out_specs=[vm, vm] if chunks else vm,
+        out_shape=[out, jax.ShapeDtypeStruct((8, 640), F32)] if chunks else out,
+        scratch_shapes=scratch,
+        compiler_params=pltpu.CompilerParams(vmem_limit_bytes=MIDDLE),
+        cost_estimate=pl.CostEstimate(flops=900_000_000, bytes_accessed=700_000, transcendentals=0),
         name="schwarz",
-    )(wait, field, y1, y2, m1, m2, *tabs)
-
-
-def early_kernel(
-    wait_ref, sep_ref, own_ref, f_ref, pz_hbm, tile_hbm,
-    v_ref, keep_ref, last_ref, pz_ref, tile_ref,
-    nv_ref, sems,
-):
+    )(wait, field, y1, y2, m1, m2, *tabs, *extra)
+
+
+PACK_LAST = SEP
+PACK_PZ = PACK_LAST + 128
+PACK_TILE = PACK_PZ + 384
+PACK_V = PACK_TILE + 128
+PACK = PACK_V + 640
+
+
+def pack_kernel(*refs):
+    l5_ref, l6_ref, v0_ref, v1_ref, v2_ref, const_ref, f_ref, pack_ref, chunk_ref, narrow_ref, sems = refs
+    pairs = [
+        (f_ref.at[:, pl.ds(5 * SEP, SEP)], chunk_ref),
+        (f_ref.at[:, pl.ds(LEVELS * SEP, LEAF)], narrow_ref),
+        (f_ref.at[:, pl.ds(6 * SEP, SEP)], pack_ref.at[:, pl.ds(0, SEP)]),
+        (const_ref, pack_ref.at[:, pl.ds(PACK_PZ, 512)]),
+    ]
     copies = []
-    pairs = [(f_ref.at[:, pl.ds(CUT, LEVELS * SEP - CUT)], keep_ref), (pz_hbm, pz_ref)]
-    pairs.append((tile_hbm, tile_ref))
     for k, (src, dst) in enumerate(pairs):
         copies.append(pltpu.make_async_copy(src, dst, sems.at[k]))
         copies[-1].start()
-    lane = lax.broadcasted_iota(jnp.int32, (4, 128), 1)
-    sep = pltpu.roll(jnp.concatenate([sep_ref[...], jnp.zeros((4, CUT), F32)], axis=0), LEAF, 1)
-    first = jnp.where(lane < LEAF, own_ref[...], sep[:4, :128])
-    first = jnp.concatenate([first, jnp.zeros((4, 128), F32)], axis=0)
-    nv_ref[:, :128] = first.astype(BF)
-    nv_ref[:, 128:] = sep[:, 128:].astype(BF)
-    last_ref[:, LEAF:] = jnp.zeros((VLOC, 128 - LEAF), BF)
-    last_ref[:, :LEAF] = f_ref[:, LEVELS * SEP :]
-    v_ref[:, VLOC:] = jnp.zeros((8, 640 - VLOC), F32)
-    v_ref[:, :VLOC] = dot(nv_ref[...], f_ref[:, :CUT], NT)
-    for copy in copies:
-        copy.wait()
-
-
-def early(wait, sep, own, factor):
+    values = shifted(l5_ref[...], l6_ref[...]).astype(BF)
+    copies[0].wait()
+    v = dot(values, chunk_ref[...], NT)
+    v = jnp.concatenate([v, jnp.zeros((8, 640 - VLOC), F32)], axis=1)
+    v = v + (v0_ref[...] + (v1_ref[...] + v2_ref[...]))
+    for k in range(3):
+        term = v.astype(BF)
+        v = v - term.astype(F32)
+        pack_ref[16 * k : 16 * k + 16, PACK_V:] = jnp.concatenate([term, jnp.zeros((8, 640), BF)], axis=0)
+    end = jnp.concatenate([l6_ref[:, SEP - 128 :], jnp.zeros((12, 128), F32)], axis=0)
+    end = pltpu.roll(end, LEAF, 1)
+    pack_ref[48:64, PACK_V : PACK_V + 128] = end.astype(BF)
+    copies[1].wait()
+    pack_ref[:, PACK_LAST : PACK_LAST + LEAF] = narrow_ref[...]
+    pack_ref[:, PACK_LAST + LEAF : PACK_PZ] = jnp.zeros((VLOC, 128 - LEAF), BF)
+    copies[2].wait()
+    copies[3].wait()
+
+
+def packed(l5, l6, v0, v1, v2, factor):
     pz = np.zeros((128, 384), np.float32)
     pz[:65] = line_table(prolong_np, 64).T
-    tile = np.zeros((640, 128), ml_dtypes.bfloat16)
+    hi, lo = split_np(pz)
+    const = np.zeros((VLOC, 512), ml_dtypes.bfloat16)
+    const[:128, :384] = hi
+    const[128:256, :384] = lo
     for ab in range(9):
         for c in range(65):
-            tile[ab * 65 + c, c] = 1
+            const[ab * 65 + c, 384 + c] = 1
     vm = pl.BlockSpec(memory_space=pltpu.VMEM)
     return pl.pallas_call(
-        early_kernel,
-        in_specs=[UNUSED, vm, vm, vm, HBM, HBM],
-        out_specs=[vm] * 5,
-        out_shape=[
-            jax.ShapeDtypeStruct((8, 640), F32),
-            jax.ShapeDtypeStruct((VLOC, LEVELS * SEP - CUT), BF),
-            jax.ShapeDtypeStruct((VLOC, 128), BF),
-            jax.ShapeDtypeStruct((2, 128, 384), BF),
-            jax.ShapeDtypeStruct((640, 128), BF),
+        pack_kernel,
+        in_specs=[vm] * 5 + [HBM] * 2,
+        out_specs=vm,
+        out_shape=jax.ShapeDtypeStruct((VLOC, PACK), BF),
+        scratch_shapes=[
+            pltpu.VMEM((VLOC, SEP), BF),
+            pltpu.VMEM((VLOC, LEAF), BF),
+            pltpu.SemaphoreType.DMA((4,)),
         ],
-        scratch_shapes=[
-            pltpu.VMEM((8, CUT), BF),
-            pltpu.SemaphoreType.DMA((3,)),
-        ],
-        compiler_params=pltpu.CompilerParams(vmem_limit_bytes=SMALL),
-        cost_estimate=pl.CostEstimate(flops=2 * 8 * VLOC * CUT, bytes_accessed=9_000_000, transcendentals=0),
-        name="early",
-    )(wait, sep, own, factor, jnp.stack([jnp.asarray(v) for v in split_np(pz)]), jnp.asarray(tile))
-
-
-def late_kernel(top_ref, v_ref, keep_ref, last_ref, s_ref, pz_ref, tile_ref, out_ref):
-    nv = jnp.concatenate([top_ref[...], jnp.zeros((4, TAIL_WIDE), F32)], axis=0).astype(BF)
-    v = v_ref[...]
-    add = dot(nv[:, : LEVELS * SEP - CUT], keep_ref[...], NT)
-    add = add + dot(nv[:, LEVELS * SEP - CUT :], last_ref[...], NT)
-    v = v + jnp.concatenate([add, jnp.zeros((8, 640 - VLOC), F32)], axis=1)
+        compiler_params=pltpu.CompilerParams(vmem_limit_bytes=MIDDLE),
+        cost_estimate=pl.CostEstimate(flops=2 * 8 * VLOC * SEP, bytes_accessed=4_000_000, transcendentals=0),
+        name="pack",
+    )(l5, l6, v0, v1, v2, jnp.asarray(const), factor)
+
+
+def late_kernel(mine_ref, got_ref, pack_ref, s_ref, out_ref):
+    top = jnp.concatenate([mine_ref[...] + got_ref[...], jnp.zeros((4, SEP), F32)], axis=0)
+    top = pltpu.roll(jnp.concatenate([top, jnp.zeros((8, 128), F32)], axis=1), LEAF, 1)
+    lane = lax.broadcasted_iota(jnp.int32, (8, 128), 1)
+    head = jnp.where(lane < LEAF, pack_ref[48:64, PACK_V : PACK_V + 128][:8].astype(F32), top[:, :128])
+    nv = jnp.concatenate([head, top[:, 128:]], axis=1).astype(BF)
+    add = dot(nv, pack_ref[:, :PACK_PZ], NT)
+    v = jnp.concatenate([add, jnp.zeros((8, 640 - VLOC), F32)], axis=1)
+    for k in range(3):
+        v = v + pack_ref[32 - 16 * k : 48 - 16 * k, PACK_V:][:8].astype(F32)
     spread = jnp.where(ab_mask(72, 640), jnp.concatenate([v] * 9, axis=0), 0.0)
     hi, lo = split(spread)
-    vert = dot(hi, tile_ref[...]) + dot(lo, tile_ref[...])
-    lines = dot3(split(vert), (pz_ref[0], pz_ref[1]))
+    tile = pack_ref[:, PACK_TILE:PACK_V]
+    vert = dot(hi[:, :VLOC], tile) + dot(lo[:, :VLOC], tile)
+    tables = (pack_ref[:128, PACK_PZ:PACK_TILE], pack_ref[128:256, PACK_PZ:PACK_TILE])
+    lines = dot3(split(vert), tables)
     p0 = [float(q) for q in prolong_np[0]]
     p1 = [float(q) for q in prolong_np[1]]
     for y in range(12):
@@ -444,17 +531,17 @@
             out_ref[x, y] = s_ref[x, y] + (p0[i] * planes[e] + p1[i] * planes[e + 1])
 
 
-def late(top, vertex, keep, last, solved, pz, tile):
+def late(mine, got, pack, solved):
     vm = pl.BlockSpec(memory_space=pltpu.VMEM)
     return pl.pallas_call(
         late_kernel,
-        in_specs=[vm] * 7,
+        in_specs=[vm] * 4,
         out_specs=vm,
         out_shape=jax.ShapeDtypeStruct((12, 12, 4, 384), F32),
         compiler_params=pltpu.CompilerParams(vmem_limit_bytes=SMALL),
-        cost_estimate=pl.CostEstimate(flops=2 * 8 * VLOC * TAIL, bytes_accessed=5_000_000, transcendentals=0),
+        cost_estimate=pl.CostEstimate(flops=2 * 8 * VLOC * SEP, bytes_accessed=5_000_000, transcendentals=0),
         name="late",
-    )(top, vertex, keep, last, solved, pz, tile)
+    )(mine, got, pack, solved)
 
 
 def exchange(value, mask):
@@ -472,36 +559,38 @@
 def local(residual, sx, sy, depth_vectors, lam_x, lam_y, lam_z, coarse_factor):
     factor = coarse_factor.reshape(VLOC, COLS)
     field = residual.transpose(1, 2, 0, 3)
-    msg, own, y2, x1, x2, kept = forward(field, factor)
+    msg, own, y2, x1, x2 = forward(field, factor)
     got1 = exchange(msg, 1)
     got2 = odd_pairs(y2, "gy")
-    tabs = tables(
-        own, sx, sy, depth_vectors.transpose(1, 2, 0).reshape(64, 64), lam_x, lam_y, lam_z.transpose(1, 0)
-    )
-    sep = msg[:, : LEVELS * SEP] + got1[:, : LEVELS * SEP]
-    done = [sep[:, :SEP]]
-    sep = sep[:, SEP:]
-    for mask in MASKS[1:]:
+    level, sep = join(msg, got1, got2)
+    done = [own, level]
+    for mask in MASKS[1:-1]:
         sep = sep + exchange(sep, mask)
         done.append(sep[:, :SEP])
         sep = sep[:, SEP:]
-    m1, m2 = faces(done[FACES_AFTER - 1], x1, x2, got1, got2)
+    got = exchange(sep, MASKS[-1])
+    dt = depth_vectors.transpose(1, 2, 0).reshape(64, 64)
+    tabs = tables(done[TABLES_AFTER], sx, sy, dt, lam_x, lam_y, lam_z.transpose(1, 0))
+    m1, m2 = faces(tabs[4], x1, x2, got1, got2)
     m1 = exchange(m1, 16)
     m2 = odd_pairs(m2, "gx")
-    parts = [
-        schwarz(first, count, done[level - 1], field, got1, got2, m1, m2, tabs)
-        for first, count, level in SCHWARZ_AFTER
-    ]
-    vertex, keep, last, pz, tile = early(done[EARLY_AFTER - 1], jnp.concatenate(done[:5], axis=1), own, kept)
+    parts = []
+    vertex = []
+    for n, (level, chunks) in enumerate(WORK):
+        levels = done[chunks[0] : chunks[-1] + 2] if chunks else ()
+        part = schwarz(n, done[level], chunks, levels, factor, field, got1, got2, m1, m2, tabs)
+        if chunks:
+            part, more = part
+            vertex.append(more)
+        parts.append(part)
+    pack = packed(done[5], done[6], *vertex, factor)
     solved = jnp.concatenate(parts, axis=0).reshape(4, 12, 16, 384)[:, :, :12].transpose(1, 2, 0, 3)
-    top = jnp.concatenate([done[4][:, SEP - LEAF :], done[5], done[6], jnp.zeros((4, TAIL_WIDE - TAIL), F32)], axis=1)
-    out = late(top, vertex, keep, last, solved, pz, tile)
+    out = late(sep, got, pack, solved)
     return out.transpose(2, 0, 1, 3)
 
 
-FACES_AFTER = 2
-SCHWARZ_AFTER = ((0, 1, 3), (1, 1, 3), (2, 1, 4), (3, 1, 5))
-EARLY_AFTER = 5
+TABLES_AFTER = 1
+WORK = ((2, (0, 1)), (3, (2,)), (4, ()), (5, (3, 4)))
 
 
 def solution(mesh):

time: 55.1 us -> 48.6 us (0.88)
  local copies, waits for them, and re-layouts: 8.84 us -> 1.93 us
  Pallas kernels: 19.8 us -> 20.6 us
  other arithmetic: 0.82 us -> 0.18 us
  starting transfers between devices: 21.4 us -> 22 us
    unnamed x41 -> x24, local copies, waits for them, and re-layouts: 6.93 us -> 0.97 us
    ppermute x8, waiting for transfers between devices: 3.3 us -> 0.02 us  [exchange(): lax.ppermute(value, ('gx', 'gy'), [(i, i ^ mask) for i in range(128)])]
    ppermute x2, waiting for transfers between devices: 0.25 us -> 3.32 us  [odd_pairs(): lax.ppermute(value, axis, [(i, (i + 1) % count if i % 2 else (i - 1) % co...]
    concatenate x2 -> x0, local copies, waits for them, and re-layouts: 0.85 us -> none  [the longest x1 0.84 us: local(): jnp.concatenate([done[4][:, SEP - LEAF:], done[5], done[6], jnp.zeros((4,...]
    pallas_call x7 -> x8, Pallas kernels: 18.6 us -> 19.4 us  [the longest x4 9.8 us: schwarz(): pl.pallas_call(kernel, in_specs=[UNUSED] + [vm] * 10 + ([vm] * len(levels...]
    add x6 -> x5, other arithmetic: 0.71 us -> 0.1 us  [local(): sep = sep + exchange(sep, mask)]
    ppermute x8, starting transfers between devices: 15.5 us -> 16.1 us  [exchange(): lax.ppermute(value, ('gx', 'gy'), [(i, i ^ mask) for i in range(128)])]
  transfers between devices with their start and end apart: 10 -> 10, of which waited for: 2 -> 2; matrix products, arithmetic and copies ran while one was open for 2% -> 2% of each run, Pallas kernels for 18% -> 26%
where the time goes in v1:
time: 48.6 us; the launch traced here: 48.4 us
  starting transfers between devices  22 us (45%)
  Pallas kernels  20.6 us (42%)
  waiting for transfers between devices  3.34 us (7%)
  local copies, waits for them, and re-layouts  1.93 us (4%)
    ppermute x8, starting transfers between devices, exchange(): lax.ppermute(value, ('gx', 'gy'), [(i, i ^ mask) for i in range(128)])  16.1 us
    pallas_call x4, Pallas kernels, schwarz(): pl.pallas_call(kernel, in_specs=[UNUSED] + [vm] * 10 + ([vm] * len(levels...  9.8 us
    ppermute x2, starting transfers between devices, odd_pairs(): lax.ppermute(value, axis, [(i, (i + 1) % count if i % 2 else (i - 1) % co...  5.88 us
    pallas_call x1, Pallas kernels, forward(): pl.pallas_call(forward_kernel, in_specs=[HBM] * 4, out_specs=[vm] * 5, ou...  5.66 us
    ppermute x2, waiting for transfers between devices, odd_pairs(): lax.ppermute(value, axis, [(i, (i + 1) % count if i % 2 else (i - 1) % co...  3.32 us
    pallas_call x1, Pallas kernels, late(): pl.pallas_call(late_kernel, in_specs=[vm] * 4, out_specs=vm, out_shape=ja...  2.12 us
    pallas_call x1, Pallas kernels, packed(): pl.pallas_call(pack_kernel, in_specs=[vm] * 5 + [HBM] * 2, out_specs=vm,...  1.82 us
    pallas_call x1, Pallas kernels, tables(): pl.pallas_call(tables_kernel, in_specs=[UNUSED] + [vm] * 6, out_specs=[vm...  1.15 us
  transfers between devices with their start and end apart: 10, of which 2 were waited for; matrix products, arithmetic and copies ran while one was open for 2% of the time, Pallas kernels for 26%

profile of v1, /device:TPU:1, one launch (start us, length us, event | category | flops | bytes accessed | tf_op | source)
XLA Modules:
  0.0 48.4 jit_solution(18264470480175290183)
XLA Ops:
  0.0 5.7 %forward.1 = (f32[4,11776]{1,0:T(4,128)}, f32[4,128]{1,0:T(4,128)}, f32[4,4608]{1,0:T(4,128)}, f32[4,4608]{1,0:T(4,128)}, f32[4,4608]{1,0:T(4,128)}) custom-call(f32[12,12,4,384]{3,2,1,0:T(4,128)} %bitcast.10, f32[384,128]{1,0:T(8,128)} %constant.6.clone.rz_hbm, bf16[128,640]{1,0:T(8,128)(2,1)} %constant.7.clone.tile_hbm, bf16[585,7233]{1,0:T(8,128)(2,1)} %bitcast.17), custom_call_target="tpu_custom_call" | custom-call | flops 67700880 | bytes 9500000 | tf_op jit(solution)/shard_map/forward/pallas_call | solution.py:179
  5.7 2.1 %collective-permute-start = (f32[4,11776]{1,0:T(4,128)}, f32[4,11776]{1,0:T(4,128)S(1)}, u32[]{:S(2)}, u32[]{:S(2)}) collective-permute-start(f32[4,11776]{1,0:T(4,128)} %get-tuple-element.25.msg_ref), channel_id=1, source_target_pairs={{0,1},{1,0},{2,3},{3,2},{4,5},{5,4},{6,7},{7,6},{8,9},{9,8},{10,11... | collective-permute-start | bytes 565256 | tf_op jit(solution)/shard_map/ppermute | solution.py:548
  7.8 4.3 %collective-permute-start.1 = (f32[4,4608]{1,0:T(4,128)}, f32[4,4608]{1,0:T(4,128)S(1)}, u32[]{:S(2)}, u32[]{:S(2)}) collective-permute-start(f32[4,4608]{1,0:T(4,128)} %get-tuple-element.26), channel_id=1, source_target_pairs={{0,15},{1,2},{2,1},{3,4},{4,3},{5,6},{6,5},{7,8},{8,7},{9,10},{10,... | collective-permute-start | bytes 221192 | tf_op jit(solution)/shard_map/ppermute | solution.py:553
  12.1 2.5 %collective-permute-done.1.y2_ref.refs_3_ = f32[4,4608]{1,0:T(4,128)S(1)} collective-permute-done((f32[4,4608]{1,0:T(4,128)}, f32[4,4608]{1,0:T(4,128)S(1)}, u32[]{:S(2)}, u32[]{:S(2)}) %collective-permute-start.1) | collective-permute-done | bytes 73760 | tf_op jit(solution)/shard_map/ppermute | solution.py:553
  14.6 0.9 %copy-done.2 = f32[4,11776]{1,0:T(4,128)S(1)} copy-done((f32[4,11776]{1,0:T(4,128)S(1)}, f32[4,11776]{1,0:T(4,128)}, u32[]{:S(2)}) %copy-start.2) | copy-done | bytes 188440
  15.5 0.7 %collective-permute-start.2 = (f32[4,6144]{1,0:T(4,128)S(1)}, f32[4,6144]{1,0:T(4,128)S(1)}, u32[]{:S(2)}, u32[]{:S(2)}) collective-permute-start(f32[4,6144]{1,0:T(4,128)S(1)} %get-tuple-element.27), channel_id=1, source_target_pairs={{0,3},{1,2},{2,1},{3,0},{4,7},{5,6},{6,5},{7,4},{8,11},{9,10},{10,... | collective-permute-start | bytes 294920 | tf_op jit(solution)/shard_map/ppermute | solution.py:548
  16.2 1.1 %tables.1 = (bf16[2,256,256]{2,1,0:T(8,128)(2,1)S(1)}, bf16[2,256,256]{2,1,0:T(8,128)(2,1)S(1)}, bf16[2,2,256,256]{3,2,1,0:T(8,128)(2,1)S(1)}, bf16[2,2,256,256]{3,2,1,0:T(8,128)(2,1)S(1)}, f32[256,512]{1,0:T(8,128)S(1)}) custom-call(f32[4,1024]{1,0:T(4,128)S(1)} %get-tuple-element.28.wait_ref.refs_12_, f32[2,8,8]{2,1,0:T(8,128)S(1)} %copy-done.7, ...), custom_call_target="tpu_custom_call" | custom-call | flops 1000000000 | bytes 2000000 | tf_op jit(solution)/shard_map/tables/pallas_call | solution.py:327
  17.5 2.5 %collective-permute-start.8 = (f32[4,5376]{1,0:T(4,128)S(1)}, f32[4,5376]{1,0:T(4,128)S(1)}, u32[]{:S(2)}, u32[]{:S(2)}) collective-permute-start(f32[4,5376]{1,0:T(4,128)S(1)} %get-tuple-element.32), channel_id=1, source_target_pairs={{0,16},{1,17},{2,18},{3,19},{4,20},{5,21},{6,22},{7,23},{8,24},{9,... | collective-permute-start | bytes 258056 | tf_op jit(solution)/shard_map/ppermute | solution.py:548
  19.9 1.6 %collective-permute-start.9 = (f32[4,5376]{1,0:T(4,128)S(1)}, f32[4,5376]{1,0:T(4,128)S(1)}, u32[]{:S(2)}, u32[]{:S(2)}) collective-permute-start(f32[4,5376]{1,0:T(4,128)S(1)} %get-tuple-element.33), channel_id=1, source_target_pairs={{0,112},{16,32},{32,16},{48,64},{64,48},{80,96},{96,80},{112,0},{1... | collective-permute-start | bytes 258056 | tf_op jit(solution)/shard_map/ppermute | solution.py:553
  21.6 1.4 %collective-permute-start.3 = (f32[4,5120]{1,0:T(4,128)S(1)}, f32[4,5120]{1,0:T(4,128)S(1)}, u32[]{:S(2)}, u32[]{:S(2)}) collective-permute-start(f32[4,5120]{1,0:T(4,128)S(1)} %slice.44), channel_id=1, source_target_pairs={{0,4},{1,5},{2,6},{3,7},{4,0},{5,1},{6,2},{7,3},{8,12},{9,13},{10,... | collective-permute-start | bytes 245768 | tf_op jit(solution)/shard_map/ppermute | solution.py:548
  23.0 0.9 %collective-permute-done.9.refs_5_ = f32[4,5376]{1,0:T(4,128)S(1)} collective-permute-done((f32[4,5376]{1,0:T(4,128)S(1)}, f32[4,5376]{1,0:T(4,128)S(1)}, u32[]{:S(2)}, u32[]{:S(2)}) %collective-permute-start.9) | collective-permute-done | bytes 86048 | tf_op jit(solution)/shard_map/ppermute | solution.py:553
  23.9 2.6 %schwarz.4 = (f32[1,192,384]{2,1,0:T(8,128)S(1)}, f32[8,640]{1,0:T(8,128)S(1)}) custom-call(f32[4,1024]{1,0:T(4,128)S(1)} %slice.51.refs_0_.refs_13_.refs_11_, f32[12,12,4,384]{3,2,1,0:T(4,128)S(1)} %bitcast.11, f32[4,11776]{1,0:T(4,128)S(1)} %collective-permute-done.y1_ref.refs_2_, f32[4,4608]{1,0:T(4,128)S(1)} %collective-permute-done.1.y2_ref.refs_3_, ...), custom_call_target="tpu_custom_call" | custom-call | flops 900000000 | bytes 700000 | tf_op jit(solution)/shard_map/schwarz/pallas_call | solution.py:427
  26.6 4.0 %collective-permute-start.4 = (f32[4,4096]{1,0:T(4,128)S(1)}, f32[4,4096]{1,0:T(4,128)S(1)}, u32[]{:S(2)}, u32[]{:S(2)}) collective-permute-start(f32[4,4096]{1,0:T(4,128)S(1)} %slice.45), channel_id=1, source_target_pairs={{0,12},{1,13},{2,14},{3,15},{4,8},{5,9},{6,10},{7,11},{8,4},{9,5},... | collective-permute-start | bytes 196616 | tf_op jit(solution)/shard_map/ppermute | solution.py:548
  30.6 3.1 %schwarz.5 = (f32[1,192,384]{2,1,0:T(8,128)S(1)}, f32[8,640]{1,0:T(8,128)S(1)}) custom-call(f32[4,1024]{1,0:T(4,128)S(1)} %slice.52.refs_0_.refs_12_.refs_11_, f32[12,12,4,384]{3,2,1,0:T(4,128)S(1)} %bitcast.12, f32[4,11776]{1,0:T(4,128)S(1)} %collective-permute-done.y1_ref.refs_2_, f32[4,4608]{1,0:T(4,128)S(1)} %collective-permute-done.1.y2_ref.refs_3_, ...), custom_call_target="tpu_custom_call" | custom-call | flops 900000000 | bytes 700000 | tf_op jit(solution)/shard_map/schwarz/pallas_call | solution.py:427
  33.7 2.8 %collective-permute-start.5 = (f32[4,3072]{1,0:T(4,128)S(1)}, f32[4,3072]{1,0:T(4,128)S(1)}, u32[]{:S(2)}, u32[]{:S(2)}) collective-permute-start(f32[4,3072]{1,0:T(4,128)S(1)} %slice.46), channel_id=1, source_target_pairs={{0,16},{1,17},{2,18},{3,19},{4,20},{5,21},{6,22},{7,23},{8,24},{9,... | collective-permute-start | bytes 147464 | tf_op jit(solution)/shard_map/ppermute | solution.py:548
  36.5 1.5 %schwarz.7 = f32[1,192,384]{2,1,0:T(8,128)S(1)} custom-call(f32[4,1024]{1,0:T(4,128)S(1)} %slice.53.refs_12_.refs_0_, f32[12,12,4,384]{3,2,1,0:T(4,128)S(1)} %bitcast.13, f32[4,11776]{1,0:T(4,128)S(1)} %collective-permute-done.y1_ref.refs_2_, f32[4,4608]{1,0:T(4,128)S(1)} %collective-permute-done.1.y2_ref.refs_3_, ...), custom_call_target="tpu_custom_call" | custom-call | flops 900000000 | bytes 700000 | tf_op jit(solution)/shard_map/schwarz/pallas_call | solution.py:427
  38.0 0.3 collective-permute-start.6
  38.3 2.6 %schwarz.6 = (f32[1,192,384]{2,1,0:T(8,128)S(1)}, f32[8,640]{1,0:T(8,128)S(1)}) custom-call(f32[4,1024]{1,0:T(4,128)S(1)} %slice.49.refs_0_.refs_13_, f32[12,12,4,384]{3,2,1,0:T(4,128)S(1)} %bitcast.14, f32[4,11776]{1,0:T(4,128)S(1)} %collective-permute-done.y1_ref.refs_2_, f32[4,4608]{1,0:T(4,128)S(1)} %collective-permute-done.1.y2_ref.refs_3_, ...), custom_call_target="tpu_custom_call" | custom-call | flops 900000000 | bytes 700000 | tf_op jit(solution)/shard_map/schwarz/pallas_call | solution.py:427
  40.9 0.1 pad_maximum_fusion
  41.0 0.8 %copy.12 = f32[4,192,384]{2,0,1:T(4,128)S(1)} copy(f32[4,192,384]{2,1,0:T(8,128)S(1)} %pad_maximum_fusion) | data formatting | bytes 2359296 | tf_op jit(solution)/shard_map/concatenate | solution.py:587
  41.9 2.4 %collective-permute-start.7 = (f32[4,1024]{1,0:T(4,128)S(1)}, f32[4,1024]{1,0:T(4,128)S(1)}, u32[]{:S(2)}, u32[]{:S(2)}) collective-permute-start(f32[4,1024]{1,0:T(4,128)S(1)} %get-tuple-element.46.mine_ref), channel_id=1, source_target_pairs={{0,96},{1,97},{2,98},{3,99},{4,100},{5,101},{6,102},{7,103},{8,104... | collective-permute-start | bytes 49160 | tf_op jit(solution)/shard_map/ppermute | solution.py:548
  44.2 0.2 slice_bitcast_fusion.s_ref
  44.4 1.8 %pack.1.pack_ref = bf16[585,2304]{1,0:T(8,128)(2,1)S(1)} custom-call(f32[4,1024]{1,0:T(4,128)S(1)} %slice.49.refs_0_.refs_13_, f32[4,1024]{1,0:T(4,128)S(1)} %get-tuple-element.45.refs_1_, f32[8,640]{1,0:T(8,128)S(1)} %get-tuple-element.39.refs_2_, f32[8,640]{1,0:T(8,128)S(1)} %get-tuple-element.40.refs_3_, f32[8,640]{1,0:T(8,128)S(1)} %get-tuple-element.41.refs_4_, ...), custom_call_target="tpu_custom_call" | custom-call | flops 9584640 | bytes 4000000 | tf_op jit(solution)/shard_map/pack/pallas_call | solution.py:488
  46.2 2.1 %late.1 = f32[12,12,4,384]{3,2,1,0:T(4,128)} custom-call(f32[4,1024]{1,0:T(4,128)S(1)} %get-tuple-element.46.mine_ref, f32[4,1024]{1,0:T(4,128)S(1)} %collective-permute-done.7.got_ref, bf16[585,2304]{1,0:T(8,128)(2,1)S(1)} %pack.1.pack_ref, f32[12,12,4,384]{3,2,1,0:T(4,128)S(1)} %slice_bitcast_fusion.s_ref), custom_call_target="tpu_custom_call" | custom-call | flops 9584640 | bytes 5000000 | tf_op jit(solution)/shard_map/late/pallas_call | solution.py:536
  (47 shorter events, 0.3 us)
Async XLA Ops:
  0.0 16.2 %copy-start.6 = (f32[64,8,8]{0,2,1:T(8,128)S(1)}, f32[64,8,8]{0,2,1:T(8,128)}, u32[]{:S(2)}) copy-start(f32[64,8,8]{0,2,1:T(8,128)} %param.14) | copy-start | bytes 49156
  0.0 16.2 %copy-start.7 = (f32[2,8,8]{2,1,0:T(8,128)S(1)}, f32[2,8,8]{2,1,0:T(8,128)}, u32[]{:S(2)}) copy-start(f32[2,8,8]{2,1,0:T(8,128)} %sx_ref.1) | copy-start | bytes 1540
  0.0 16.2 %copy-start.8 = (f32[2,8,8]{2,1,0:T(8,128)S(1)}, f32[2,8,8]{2,1,0:T(8,128)}, u32[]{:S(2)}) copy-start(f32[2,8,8]{2,1,0:T(8,128)} %sy_ref.1) | copy-start | bytes 1540
  0.0 16.2 %copy-start.9 = (f32[64,8]{0,1:T(8,128)S(1)}, f32[64,8]{0,1:T(8,128)}, u32[]{:S(2)}) copy-start(f32[64,8]{0,1:T(8,128)} %param.17) | copy-start | bytes 6148
  0.0 16.2 %copy-start.10 = (f32[2,8]{1,0:T(2,128)S(1)}, f32[2,8]{1,0:T(2,128)}, u32[]{:S(2)}) copy-start(f32[2,8]{1,0:T(2,128)} %lx_ref.1) | copy-start | bytes 196
  0.0 16.2 %copy-start.11 = (f32[2,8]{1,0:T(2,128)S(1)}, f32[2,8]{1,0:T(2,128)}, u32[]{:S(2)}) copy-start(f32[2,8]{1,0:T(2,128)} %ly_ref.1) | copy-start | bytes 196
  5.7 8.9 %collective-permute-start = (f32[4,11776]{1,0:T(4,128)}, f32[4,11776]{1,0:T(4,128)S(1)}, u32[]{:S(2)}, u32[]{:S(2)}) collective-permute-start(f32[4,11776]{1,0:T(4,128)} %get-tuple-element.25.msg_ref), channel_id=1, source_target_pairs={{0,1},{1,0},{2,3},{3,2},{4,5},{5,4},{6,7},{7,6},{8,9},{9,8},{10,11... | collective-permute-start | bytes 565256 | tf_op jit(solution)/shard_map/ppermute | solution.py:548
  7.8 6.7 %collective-permute-start.1 = (f32[4,4608]{1,0:T(4,128)}, f32[4,4608]{1,0:T(4,128)S(1)}, u32[]{:S(2)}, u32[]{:S(2)}) collective-permute-start(f32[4,4608]{1,0:T(4,128)} %get-tuple-element.26), channel_id=1, source_target_pairs={{0,15},{1,2},{2,1},{3,4},{4,3},{5,6},{6,5},{7,8},{8,7},{9,10},{10,... | collective-permute-start | bytes 221192 | tf_op jit(solution)/shard_map/ppermute | solution.py:553
  14.6 0.9 %copy-start.2 = (f32[4,11776]{1,0:T(4,128)S(1)}, f32[4,11776]{1,0:T(4,128)}, u32[]{:S(2)}) copy-start(f32[4,11776]{1,0:T(4,128)} %get-tuple-element.25.msg_ref) | copy-start | bytes 565252
  15.5 6.0 %collective-permute-start.2 = (f32[4,6144]{1,0:T(4,128)S(1)}, f32[4,6144]{1,0:T(4,128)S(1)}, u32[]{:S(2)}, u32[]{:S(2)}) collective-permute-start(f32[4,6144]{1,0:T(4,128)S(1)} %get-tuple-element.27), channel_id=1, source_target_pairs={{0,3},{1,2},{2,1},{3,0},{4,7},{5,6},{6,5},{7,4},{8,11},{9,10},{10,... | collective-permute-start | bytes 294920 | tf_op jit(solution)/shard_map/ppermute | solution.py:548
  16.2 1.2 %copy-start.3 = (f32[4,4608]{1,0:T(4,128)S(1)}, f32[4,4608]{1,0:T(4,128)}, u32[]{:S(2)}) copy-start(f32[4,4608]{1,0:T(4,128)} %get-tuple-element.30.x1_ref) | copy-start | bytes 221188
  16.2 1.2 %copy-start.4 = (f32[4,4608]{1,0:T(4,128)S(1)}, f32[4,4608]{1,0:T(4,128)}, u32[]{:S(2)}) copy-start(f32[4,4608]{1,0:T(4,128)} %get-tuple-element.31.x2_ref) | copy-start | bytes 221188
  17.4 6.5 %copy-start = (f32[4,12,12,384]{3,0,2,1:T(4,128)S(1)}, f32[4,12,12,384]{3,0,2,1:T(4,128)}, u32[]{:S(2)}) copy-start(f32[4,12,12,384]{3,0,2,1:T(4,128)} %param.11) | copy-start | bytes 2654212
  17.4 6.4 %copy-start.5 = (f32[4,128]{1,0:T(4,128)S(1)}, f32[4,128]{1,0:T(4,128)}, u32[]{:S(2)}) copy-start(f32[4,128]{1,0:T(4,128)} %get-tuple-element.38.refs_11_) | copy-start | bytes 6148
  17.5 5.5 %collective-permute-start.8 = (f32[4,5376]{1,0:T(4,128)S(1)}, f32[4,5376]{1,0:T(4,128)S(1)}, u32[]{:S(2)}, u32[]{:S(2)}) collective-permute-start(f32[4,5376]{1,0:T(4,128)S(1)} %get-tuple-element.32), channel_id=1, source_target_pairs={{0,16},{1,17},{2,18},{3,19},{4,20},{5,21},{6,22},{7,23},{8,24},{9,... | collective-permute-start | bytes 258056 | tf_op jit(solution)/shard_map/ppermute | solution.py:548
  19.9 3.9 %collective-permute-start.9 = (f32[4,5376]{1,0:T(4,128)S(1)}, f32[4,5376]{1,0:T(4,128)S(1)}, u32[]{:S(2)}, u32[]{:S(2)}) collective-permute-start(f32[4,5376]{1,0:T(4,128)S(1)} %get-tuple-element.33), channel_id=1, source_target_pairs={{0,112},{16,32},{32,16},{48,64},{64,48},{80,96},{96,80},{112,0},{1... | collective-permute-start | bytes 258056 | tf_op jit(solution)/shard_map/ppermute | solution.py:553
  21.6 4.9 %collective-permute-start.3 = (f32[4,5120]{1,0:T(4,128)S(1)}, f32[4,5120]{1,0:T(4,128)S(1)}, u32[]{:S(2)}, u32[]{:S(2)}) collective-permute-start(f32[4,5120]{1,0:T(4,128)S(1)} %slice.44), channel_id=1, source_target_pairs={{0,4},{1,5},{2,6},{3,7},{4,0},{5,1},{6,2},{7,3},{8,12},{9,13},{10,... | collective-permute-start | bytes 245768 | tf_op jit(solution)/shard_map/ppermute | solution.py:548
  26.6 7.1 %collective-permute-start.4 = (f32[4,4096]{1,0:T(4,128)S(1)}, f32[4,4096]{1,0:T(4,128)S(1)}, u32[]{:S(2)}, u32[]{:S(2)}) collective-permute-start(f32[4,4096]{1,0:T(4,128)S(1)} %slice.45), channel_id=1, source_target_pairs={{0,12},{1,13},{2,14},{3,15},{4,8},{5,9},{6,10},{7,11},{8,4},{9,5},... | collective-permute-start | bytes 196616 | tf_op jit(solution)/shard_map/ppermute | solution.py:548
  33.7 4.2 %collective-permute-start.5 = (f32[4,3072]{1,0:T(4,128)S(1)}, f32[4,3072]{1,0:T(4,128)S(1)}, u32[]{:S(2)}, u32[]{:S(2)}) collective-permute-start(f32[4,3072]{1,0:T(4,128)S(1)} %slice.46), channel_id=1, source_target_pairs={{0,16},{1,17},{2,18},{3,19},{4,20},{5,21},{6,22},{7,23},{8,24},{9,... | collective-permute-start | bytes 147464 | tf_op jit(solution)/shard_map/ppermute | solution.py:548
  38.0 3.8 %collective-permute-start.6 = (f32[4,2048]{1,0:T(4,128)S(1)}, f32[4,2048]{1,0:T(4,128)S(1)}, u32[]{:S(2)}, u32[]{:S(2)}) collective-permute-start(f32[4,2048]{1,0:T(4,128)S(1)} %slice.47), channel_id=1, source_target_pairs={{0,32},{1,33},{2,34},{3,35},{4,36},{5,37},{6,38},{7,39},{8,40},{9,... | collective-permute-start | bytes 98312 | tf_op jit(solution)/shard_map/ppermute | solution.py:548
  41.8 2.6 %copy-start.1 = (bf16[585,512]{1,0:T(8,128)(2,1)S(1)}, bf16[585,512]{1,0:T(8,128)(2,1)}, u32[]{:S(2)}) copy-start(bf16[585,512]{1,0:T(8,128)(2,1)} %constant.8.clone.refs_5_) | copy-start | bytes 1797124
  41.9 4.4 %collective-permute-start.7 = (f32[4,1024]{1,0:T(4,128)S(1)}, f32[4,1024]{1,0:T(4,128)S(1)}, u32[]{:S(2)}, u32[]{:S(2)}) collective-permute-start(f32[4,1024]{1,0:T(4,128)S(1)} %get-tuple-element.46.mine_ref), channel_id=1, source_target_pairs={{0,96},{1,97},{2,98},{3,99},{4,100},{5,101},{6,102},{7,103},{8,104... | collective-permute-start | bytes 49160 | tf_op jit(solution)/shard_map/ppermute | solution.py:548

commit v2 on v1

--- a/solution.py
+++ b/solution.py
@@ -83,7 +83,7 @@
 FACE = 12 * 384
 SLAB = 14 * 384
 PADDED = 7296
-BIG = 58 << 20
+BIG = 55040 << 10
 ROW_CHUNKS = ((512, 73), (0, 256), (256, 128), (384, 128))
 SMALL = 24 << 20
 MIDDLE = 48 << 20
@@ -197,16 +197,16 @@
     )(field, jnp.asarray(rz), jnp.asarray(tile), factor)
 
 
-def join_kernel(msg_ref, y1_ref, y2_ref, level_ref, rest_ref):
+def join_kernel(wait_ref, msg_ref, y1_ref, y2_ref, level_ref, rest_ref):
     level_ref[...] = msg_ref[:, :SEP] + y1_ref[:, :SEP]
     rest_ref[...] = msg_ref[:, SEP : LEVELS * SEP] + y1_ref[:, SEP : LEVELS * SEP]
 
 
-def join(msg, y1, y2):
+def join(wait, msg, y1, y2):
     vm = pl.BlockSpec(memory_space=pltpu.VMEM)
     return pl.pallas_call(
         join_kernel,
-        in_specs=[vm, vm, UNUSED],
+        in_specs=[UNUSED, vm, vm, UNUSED],
         out_specs=[vm] * 2,
         out_shape=[
             jax.ShapeDtypeStruct((4, SEP), F32),
@@ -215,7 +215,7 @@
         compiler_params=pltpu.CompilerParams(vmem_limit_bytes=MIDDLE),
         cost_estimate=pl.CostEstimate(flops=30_000, bytes_accessed=400_000, transcendentals=0),
         name="join",
-    )(msg, y1, y2)
+    )(wait, msg, y1, y2)
 
 
 def faces_kernel(wait_ref, x1_ref, x2_ref, y1_ref, y2_ref, m1_ref, m2_ref):
@@ -251,7 +251,13 @@
     )(wait, x1, x2, y1, y2)
 
 
-def tables_kernel(wait_ref, sx_ref, sy_ref, dt_ref, lx_ref, ly_ref, lz_ref, a_ref, b_ref, zf_ref, zb_ref, rs_ref):
+def tables_kernel(
+    wait_ref, r_ref, sx_ref, sy_ref, dt_ref, lx_ref, ly_ref, lz_ref, a_ref, b_ref, zf_ref, zb_ref, rs_ref, xs_ref
+):
+    xs_ref[...] = jnp.zeros_like(xs_ref)
+    for n in range(4):
+        for x in range(12):
+            xs_ref[n, 16 * x : 16 * x + 12, :] = r_ref[x, :, n, :]
     lane = lax.broadcasted_iota(jnp.int32, (8, 256), 1)
     sub = lax.broadcasted_iota(jnp.int32, (8, 256), 0)
     slab = lane // 16
@@ -322,23 +328,24 @@
         zb_ref[1, g] = jnp.where(mid, lo.astype(F32), 0.0).astype(BF)
 
 
-def tables(wait, sx, sy, dt, lx, ly, lz):
+def tables(wait, field, sx, sy, dt, lx, ly, lz):
     vm = pl.BlockSpec(memory_space=pltpu.VMEM)
     return pl.pallas_call(
         tables_kernel,
-        in_specs=[UNUSED] + [vm] * 6,
-        out_specs=[vm] * 5,
+        in_specs=[UNUSED] + [vm] * 7,
+        out_specs=[vm] * 6,
         out_shape=[
             jax.ShapeDtypeStruct((2, 256, 256), BF),
             jax.ShapeDtypeStruct((2, 256, 256), BF),
             jax.ShapeDtypeStruct((2, 2, 256, 256), BF),
             jax.ShapeDtypeStruct((2, 2, 256, 256), BF),
             jax.ShapeDtypeStruct((256, 512), F32),
+            jax.ShapeDtypeStruct((4, 224, 384), F32),
         ],
         compiler_params=pltpu.CompilerParams(vmem_limit_bytes=SMALL),
         cost_estimate=pl.CostEstimate(flops=1_000_000_000, bytes_accessed=2_000_000, transcendentals=0),
         name="tables",
-    )(wait, sx, sy, dt, lx, ly, lz)
+    )(wait, field, sx, sy, dt, lx, ly, lz)
 
 
 def shifted(left, right):
@@ -386,11 +393,10 @@
 ):
     gy_odd, gx_odd = parities()
     tail = LEVELS * SEP
-    x_ref[...] = jnp.zeros_like(x_ref)
     for k in range(out_ref.shape[0]):
         n = first + k
+        x_ref[k] = r_ref[n]
         for x in range(12):
-            x_ref[k, 16 * x : 16 * x + 12, :] = r_ref[x, :, n, :]
             one = y1_ref[n : n + 1, tail + 384 * x : tail + 384 * x + 384]
             two = y2_ref[n : n + 1, 384 * x : 384 * x + 384]
             x_ref[k, 16 * x + 12 : 16 * x + 13, :] = jnp.where(gy_odd, one, two)
@@ -444,7 +450,7 @@
 
 
 def pack_kernel(*refs):
-    l5_ref, l6_ref, v0_ref, v1_ref, v2_ref, const_ref, f_ref, pack_ref, chunk_ref, narrow_ref, sems = refs
+    l5_ref, l6_ref, *vertex_refs, const_ref, f_ref, pack_ref, chunk_ref, narrow_ref, sems = refs
     pairs = [
         (f_ref.at[:, pl.ds(5 * SEP, SEP)], chunk_ref),
         (f_ref.at[:, pl.ds(LEVELS * SEP, LEAF)], narrow_ref),
@@ -459,7 +465,7 @@
     copies[0].wait()
     v = dot(values, chunk_ref[...], NT)
     v = jnp.concatenate([v, jnp.zeros((8, 640 - VLOC), F32)], axis=1)
-    v = v + (v0_ref[...] + (v1_ref[...] + v2_ref[...]))
+    v = v + sum(ref[...] for ref in vertex_refs)
     for k in range(3):
         term = v.astype(BF)
         v = v - term.astype(F32)
@@ -474,7 +480,7 @@
     copies[3].wait()
 
 
-def packed(l5, l6, v0, v1, v2, factor):
+def packed(l5, l6, vertex, factor):
     pz = np.zeros((128, 384), np.float32)
     pz[:65] = line_table(prolong_np, 64).T
     hi, lo = split_np(pz)
@@ -487,7 +493,7 @@
     vm = pl.BlockSpec(memory_space=pltpu.VMEM)
     return pl.pallas_call(
         pack_kernel,
-        in_specs=[vm] * 5 + [HBM] * 2,
+        in_specs=[vm] * (2 + len(vertex)) + [HBM] * 2,
         out_specs=vm,
         out_shape=jax.ShapeDtypeStruct((VLOC, PACK), BF),
         scratch_shapes=[
@@ -498,7 +504,7 @@
         compiler_params=pltpu.CompilerParams(vmem_limit_bytes=MIDDLE),
         cost_estimate=pl.CostEstimate(flops=2 * 8 * VLOC * SEP, bytes_accessed=4_000_000, transcendentals=0),
         name="pack",
-    )(l5, l6, v0, v1, v2, jnp.asarray(const), factor)
+    )(l5, l6, *vertex, jnp.asarray(const), factor)
 
 
 def late_kernel(mine_ref, got_ref, pack_ref, s_ref, out_ref):
@@ -561,35 +567,35 @@
     field = residual.transpose(1, 2, 0, 3)
     msg, own, y2, x1, x2 = forward(field, factor)
     got1 = exchange(msg, 1)
+    dt = depth_vectors.transpose(1, 2, 0).reshape(64, 64)
+    tabs = tables(own, field, sx, sy, dt, lam_x, lam_y, lam_z.transpose(1, 0))
     got2 = odd_pairs(y2, "gy")
-    level, sep = join(msg, got1, got2)
+    level, sep = join(tabs[4], msg, got1, got2)
     done = [own, level]
     for mask in MASKS[1:-1]:
         sep = sep + exchange(sep, mask)
         done.append(sep[:, :SEP])
         sep = sep[:, SEP:]
     got = exchange(sep, MASKS[-1])
-    dt = depth_vectors.transpose(1, 2, 0).reshape(64, 64)
-    tabs = tables(done[TABLES_AFTER], sx, sy, dt, lam_x, lam_y, lam_z.transpose(1, 0))
-    m1, m2 = faces(tabs[4], x1, x2, got1, got2)
+    m1, m2 = faces(done[FACES_AFTER], x1, x2, got1, got2)
     m1 = exchange(m1, 16)
     m2 = odd_pairs(m2, "gx")
     parts = []
     vertex = []
     for n, (level, chunks) in enumerate(WORK):
         levels = done[chunks[0] : chunks[-1] + 2] if chunks else ()
-        part = schwarz(n, done[level], chunks, levels, factor, field, got1, got2, m1, m2, tabs)
+        part = schwarz(n, done[level], chunks, levels, factor, tabs[5], got1, got2, m1, m2, tabs[:5])
         if chunks:
             part, more = part
             vertex.append(more)
         parts.append(part)
-    pack = packed(done[5], done[6], *vertex, factor)
+    pack = packed(done[5], done[6], vertex, factor)
     solved = jnp.concatenate(parts, axis=0).reshape(4, 12, 16, 384)[:, :, :12].transpose(1, 2, 0, 3)
     out = late(sep, got, pack, solved)
     return out.transpose(2, 0, 1, 3)
 
 
-TABLES_AFTER = 1
+FACES_AFTER = 1
 WORK = ((2, (0, 1)), (3, (2,)), (4, ()), (5, (3, 4)))
 
 

time: 48.6 us -> 46.3 us (0.953)
  waiting for transfers between devices: 3.34 us -> 1.99 us
  local copies, waits for them, and re-layouts: 1.93 us -> 1 us
    ppermute x2, waiting for transfers between devices: 3.32 us -> 1.97 us  [odd_pairs(): lax.ppermute(value, axis, [(i, (i + 1) % count if i % 2 else (i - 1) % co...]
    unnamed x24 -> x20, local copies, waits for them, and re-layouts: 0.97 us -> 0.05 us
  transfers between devices with their start and end apart: 10 -> 10, of which waited for: 2 -> 2; matrix products, arithmetic and copies ran while one was open for 2% -> 2% of each run, Pallas kernels for 26% -> 28%
where the time goes in v2:
time: 46.3 us; the launch traced here: 46.1 us
  starting transfers between devices  22 us (48%)
  Pallas kernels  20.6 us (44%)
  waiting for transfers between devices  1.99 us (4%)
  local copies, waits for them, and re-layouts  1 us (2%)
    ppermute x8, starting transfers between devices, exchange(): lax.ppermute(value, ('gx', 'gy'), [(i, i ^ mask) for i in range(128)])  16.1 us
    pallas_call x4, Pallas kernels, schwarz(): pl.pallas_call(kernel, in_specs=[UNUSED] + [vm] * 10 + ([vm] * len(levels...  9.55 us
    ppermute x2, starting transfers between devices, odd_pairs(): lax.ppermute(value, axis, [(i, (i + 1) % count if i % 2 else (i - 1) % co...  5.88 us
    pallas_call x1, Pallas kernels, forward(): pl.pallas_call(forward_kernel, in_specs=[HBM] * 4, out_specs=[vm] * 5, ou...  5.68 us
    pallas_call x1, Pallas kernels, late(): pl.pallas_call(late_kernel, in_specs=[vm] * 4, out_specs=vm, out_shape=ja...  2.12 us
    ppermute x2, waiting for transfers between devices, odd_pairs(): lax.ppermute(value, axis, [(i, (i + 1) % count if i % 2 else (i - 1) % co...  1.97 us
    pallas_call x1, Pallas kernels, packed(): pl.pallas_call(pack_kernel, in_specs=[vm] * (2 + len(vertex)) + [HBM] * 2...  1.82 us
    pallas_call x1, Pallas kernels, tables(): pl.pallas_call(tables_kernel, in_specs=[UNUSED] + [vm] * 7, out_specs=[vm...  1.36 us
  transfers between devices with their start and end apart: 10, of which 2 were waited for; matrix products, arithmetic and copies ran while one was open for 2% of the time, Pallas kernels for 28%

profile of v2, /device:TPU:1, one launch (start us, length us, event | category | flops | bytes accessed | tf_op | source)
XLA Modules:
  0.0 46.1 jit_solution(16898365771133416697)
XLA Ops:
  0.0 5.7 %forward.1 = (f32[4,11776]{1,0:T(4,128)}, f32[4,128]{1,0:T(4,128)S(1)}, f32[4,4608]{1,0:T(4,128)S(1)}, f32[4,4608]{1,0:T(4,128)S(1)}, f32[4,4608]{1,0:T(4,128)}) custom-call(f32[12,12,4,384]{3,2,1,0:T(4,128)} %bitcast.10, f32[384,128]{1,0:T(8,128)} %constant.6.clone.rz_hbm, bf16[128,640]{1,0:T(8,128)(2,1)} %constant.7.clone.tile_hbm, bf16[585,7233]{1,0:T(8,128)(2,1)} %bitcast.14), custom_call_target="tpu_custom_call" | custom-call | flops 67700880 | bytes 9500000 | tf_op jit(solution)/shard_map/forward/pallas_call | solution.py:179
  5.7 2.1 %collective-permute-start = (f32[4,11776]{1,0:T(4,128)}, f32[4,11776]{1,0:T(4,128)S(1)}, u32[]{:S(2)}, u32[]{:S(2)}) collective-permute-start(f32[4,11776]{1,0:T(4,128)} %get-tuple-element.28.msg_ref), channel_id=1, source_target_pairs={{0,1},{1,0},{2,3},{3,2},{4,5},{5,4},{6,7},{7,6},{8,9},{9,8},{10,11... | collective-permute-start | bytes 565256 | tf_op jit(solution)/shard_map/ppermute | solution.py:554
  7.9 4.3 %collective-permute-start.1 = (f32[4,4608]{1,0:T(4,128)S(1)}, f32[4,4608]{1,0:T(4,128)S(1)}, u32[]{:S(2)}, u32[]{:S(2)}) collective-permute-start(f32[4,4608]{1,0:T(4,128)S(1)} %get-tuple-element.29), channel_id=1, source_target_pairs={{0,15},{1,2},{2,1},{3,4},{4,3},{5,6},{6,5},{7,8},{8,7},{9,10},{10,... | collective-permute-start | bytes 221192 | tf_op jit(solution)/shard_map/ppermute | solution.py:559
  12.2 1.4 %tables.1 = (bf16[2,256,256]{2,1,0:T(8,128)(2,1)S(1)}, bf16[2,256,256]{2,1,0:T(8,128)(2,1)S(1)}, bf16[2,2,256,256]{3,2,1,0:T(8,128)(2,1)S(1)}, bf16[2,2,256,256]...) custom-call(f32[4,128]{1,0:T(4,128)S(1)} %get-tuple-element.26.wait_ref.refs_11_, ...), custom_call_target="tpu_custom_call" | custom-call | flops 1000000000 | bytes 2000000 | tf_op jit(solution)/shard_map/tables/pallas_call | solution.py:333
  13.6 0.8 %collective-permute-done.1.y2_ref.refs_3_ = f32[4,4608]{1,0:T(4,128)S(1)} collective-permute-done((f32[4,4608]{1,0:T(4,128)S(1)}, f32[4,4608]{1,0:T(4,128)S(1)}, u32[]{:S(2)}, u32[]{:S(2)}) %collective-permute-start.1) | collective-permute-done | bytes 73760 | tf_op jit(solution)/shard_map/ppermute | solution.py:559
  14.4 0.7 %collective-permute-start.2 = (f32[4,6144]{1,0:T(4,128)S(1)}, f32[4,6144]{1,0:T(4,128)S(1)}, u32[]{:S(2)}, u32[]{:S(2)}) collective-permute-start(f32[4,6144]{1,0:T(4,128)S(1)} %get-tuple-element.30), channel_id=1, source_target_pairs={{0,3},{1,2},{2,1},{3,0},{4,7},{5,6},{6,5},{7,4},{8,11},{9,10},{10,... | collective-permute-start | bytes 294920 | tf_op jit(solution)/shard_map/ppermute | solution.py:554
  15.1 2.5 %collective-permute-start.8 = (f32[4,5376]{1,0:T(4,128)S(1)}, f32[4,5376]{1,0:T(4,128)S(1)}, u32[]{:S(2)}, u32[]{:S(2)}) collective-permute-start(f32[4,5376]{1,0:T(4,128)S(1)} %get-tuple-element.35), channel_id=1, source_target_pairs={{0,16},{1,17},{2,18},{3,19},{4,20},{5,21},{6,22},{7,23},{8,24},{9,... | collective-permute-start | bytes 258056 | tf_op jit(solution)/shard_map/ppermute | solution.py:554
  17.6 1.6 %collective-permute-start.9 = (f32[4,5376]{1,0:T(4,128)S(1)}, f32[4,5376]{1,0:T(4,128)S(1)}, u32[]{:S(2)}, u32[]{:S(2)}) collective-permute-start(f32[4,5376]{1,0:T(4,128)S(1)} %get-tuple-element.36), channel_id=1, source_target_pairs={{0,112},{16,32},{32,16},{48,64},{64,48},{80,96},{96,80},{112,0},{1... | collective-permute-start | bytes 258056 | tf_op jit(solution)/shard_map/ppermute | solution.py:559
  19.3 1.4 %collective-permute-start.3 = (f32[4,5120]{1,0:T(4,128)S(1)}, f32[4,5120]{1,0:T(4,128)S(1)}, u32[]{:S(2)}, u32[]{:S(2)}) collective-permute-start(f32[4,5120]{1,0:T(4,128)S(1)} %slice.44), channel_id=1, source_target_pairs={{0,4},{1,5},{2,6},{3,7},{4,0},{5,1},{6,2},{7,3},{8,12},{9,13},{10,... | collective-permute-start | bytes 245768 | tf_op jit(solution)/shard_map/ppermute | solution.py:554
  20.6 1.1 %collective-permute-done.9.refs_5_ = f32[4,5376]{1,0:T(4,128)S(1)} collective-permute-done((f32[4,5376]{1,0:T(4,128)S(1)}, f32[4,5376]{1,0:T(4,128)S(1)}, u32[]{:S(2)}, u32[]{:S(2)}) %collective-permute-start.9) | collective-permute-done | bytes 86048 | tf_op jit(solution)/shard_map/ppermute | solution.py:559
  21.8 2.6 %schwarz.4 = (f32[1,192,384]{2,1,0:T(8,128)S(1)}, f32[8,640]{1,0:T(8,128)S(1)}) custom-call(f32[4,1024]{1,0:T(4,128)S(1)} %slice.51.refs_0_.refs_13_.refs_11_, f32[4,224,384]{2,1,0:T(8,128)S(1)} %get-tuple-element.31.refs_1_, f32[4,11776]{1,0:T(4,128)S(1)} %collective-permute-done.y1_ref.refs_2_, f32[4,4608]{1,0:T(4,128)S(1)} %collective-permute-done.1.y2_ref.refs_3_, ...), custom_call_target="tpu_custom_call" | custom-call | flops 900000000 | bytes 700000 | tf_op jit(solution)/shard_map/schwarz/pallas_call | solution.py:433
  24.4 3.7 %collective-permute-start.4 = (f32[4,4096]{1,0:T(4,128)S(1)}, f32[4,4096]{1,0:T(4,128)S(1)}, u32[]{:S(2)}, u32[]{:S(2)}) collective-permute-start(f32[4,4096]{1,0:T(4,128)S(1)} %slice.45), channel_id=1, source_target_pairs={{0,12},{1,13},{2,14},{3,15},{4,8},{5,9},{6,10},{7,11},{8,4},{9,5},... | collective-permute-start | bytes 196616 | tf_op jit(solution)/shard_map/ppermute | solution.py:554
  28.2 3.0 %schwarz.5 = (f32[1,192,384]{2,1,0:T(8,128)S(1)}, f32[8,640]{1,0:T(8,128)S(1)}) custom-call(f32[4,1024]{1,0:T(4,128)S(1)} %slice.52.refs_0_.refs_12_.refs_11_, f32[4,224,384]{2,1,0:T(8,128)S(1)} %get-tuple-element.31.refs_1_, f32[4,11776]{1,0:T(4,128)S(1)} %collective-permute-done.y1_ref.refs_2_, f32[4,4608]{1,0:T(4,128)S(1)} %collective-permute-done.1.y2_ref.refs_3_, ...), custom_call_target="tpu_custom_call" | custom-call | flops 900000000 | bytes 700000 | tf_op jit(solution)/shard_map/schwarz/pallas_call | solution.py:433
  31.2 2.8 %collective-permute-start.5 = (f32[4,3072]{1,0:T(4,128)S(1)}, f32[4,3072]{1,0:T(4,128)S(1)}, u32[]{:S(2)}, u32[]{:S(2)}) collective-permute-start(f32[4,3072]{1,0:T(4,128)S(1)} %slice.46), channel_id=1, source_target_pairs={{0,16},{1,17},{2,18},{3,19},{4,20},{5,21},{6,22},{7,23},{8,24},{9,... | collective-permute-start | bytes 147464 | tf_op jit(solution)/shard_map/ppermute | solution.py:554
  34.0 1.4 %schwarz.7 = f32[1,192,384]{2,1,0:T(8,128)S(1)} custom-call(f32[4,1024]{1,0:T(4,128)S(1)} %slice.53.refs_12_.refs_0_, f32[4,224,384]{2,1,0:T(8,128)S(1)} %get-tuple-element.31.refs_1_, f32[4,11776]{1,0:T(4,128)S(1)} %collective-permute-done.y1_ref.refs_2_, f32[4,4608]{1,0:T(4,128)S(1)} %collective-permute-done.1.y2_ref.refs_3_, ...), custom_call_target="tpu_custom_call" | custom-call | flops 900000000 | bytes 700000 | tf_op jit(solution)/shard_map/schwarz/pallas_call | solution.py:433
  35.5 0.6 %collective-permute-start.6 = (f32[4,2048]{1,0:T(4,128)S(1)}, f32[4,2048]{1,0:T(4,128)S(1)}, u32[]{:S(2)}, u32[]{:S(2)}) collective-permute-start(f32[4,2048]{1,0:T(4,128)S(1)} %slice.47), channel_id=1, source_target_pairs={{0,32},{1,33},{2,34},{3,35},{4,36},{5,37},{6,38},{7,39},{8,40},{9,... | collective-permute-start | bytes 98312 | tf_op jit(solution)/shard_map/ppermute | solution.py:554
  36.1 2.6 %schwarz.6 = (f32[1,192,384]{2,1,0:T(8,128)S(1)}, f32[8,640]{1,0:T(8,128)S(1)}) custom-call(f32[4,1024]{1,0:T(4,128)S(1)} %slice.49.refs_0_.refs_13_, f32[4,224,384]{2,1,0:T(8,128)S(1)} %get-tuple-element.31.refs_1_, f32[4,11776]{1,0:T(4,128)S(1)} %collective-permute-done.y1_ref.refs_2_, f32[4,4608]{1,0:T(4,128)S(1)} %collective-permute-done.1.y2_ref.refs_3_, ...), custom_call_target="tpu_custom_call" | custom-call | flops 900000000 | bytes 700000 | tf_op jit(solution)/shard_map/schwarz/pallas_call | solution.py:433
  38.7 0.1 pad_maximum_fusion
  38.8 0.8 %copy.12 = f32[4,192,384]{2,0,1:T(4,128)S(1)} copy(f32[4,192,384]{2,1,0:T(8,128)S(1)} %pad_maximum_fusion) | data formatting | bytes 2359296 | tf_op jit(solution)/shard_map/concatenate | solution.py:593
  39.5 0.0 copy-start.1
  39.6 2.3 %collective-permute-start.7 = (f32[4,1024]{1,0:T(4,128)S(1)}, f32[4,1024]{1,0:T(4,128)S(1)}, u32[]{:S(2)}, u32[]{:S(2)}) collective-permute-start(f32[4,1024]{1,0:T(4,128)S(1)} %get-tuple-element.48.mine_ref), channel_id=1, source_target_pairs={{0,96},{1,97},{2,98},{3,99},{4,100},{5,101},{6,102},{7,103},{8,104... | collective-permute-start | bytes 49160 | tf_op jit(solution)/shard_map/ppermute | solution.py:554
  41.9 0.2 slice_bitcast_fusion.s_ref
  42.1 1.8 %pack.1.pack_ref = bf16[585,2304]{1,0:T(8,128)(2,1)S(1)} custom-call(f32[4,1024]{1,0:T(4,128)S(1)} %slice.49.refs_0_.refs_13_, f32[4,1024]{1,0:T(4,128)S(1)} %get-tuple-element.47.refs_1_, f32[8,640]{1,0:T(8,128)S(1)} %get-tuple-element.41.refs_2_, f32[8,640]{1,0:T(8,128)S(1)} %get-tuple-element.42.refs_3_, f32[8,640]{1,0:T(8,128)S(1)} %get-tuple-element.43.refs_4_, ...), custom_call_target="tpu_custom_call" | custom-call | flops 9584640 | bytes 4000000 | tf_op jit(solution)/shard_map/pack/pallas_call | solution.py:494
  43.9 2.1 %late.1 = f32[12,12,4,384]{3,2,1,0:T(4,128)} custom-call(f32[4,1024]{1,0:T(4,128)S(1)} %get-tuple-element.48.mine_ref, f32[4,1024]{1,0:T(4,128)S(1)} %collective-permute-done.7.got_ref, bf16[585,2304]{1,0:T(8,128)(2,1)S(1)} %pack.1.pack_ref, f32[12,12,4,384]{3,2,1,0:T(4,128)S(1)} %slice_bitcast_fusion.s_ref), custom_call_target="tpu_custom_call" | custom-call | flops 9584640 | bytes 5000000 | tf_op jit(solution)/shard_map/late/pallas_call | solution.py:542
  (43 shorter events, 0.2 us)
Async XLA Ops:
  0.0 12.1 %copy-start = (f32[4,12,12,384]{3,0,2,1:T(4,128)S(1)}, f32[4,12,12,384]{3,0,2,1:T(4,128)}, u32[]{:S(2)}) copy-start(f32[4,12,12,384]{3,0,2,1:T(4,128)} %param.11) | copy-start | bytes 2654212
  0.0 12.1 %copy-start.4 = (f32[64,8,8]{0,2,1:T(8,128)S(1)}, f32[64,8,8]{0,2,1:T(8,128)}, u32[]{:S(2)}) copy-start(f32[64,8,8]{0,2,1:T(8,128)} %param.14) | copy-start | bytes 49156
  0.0 12.1 %copy-start.5 = (f32[2,8,8]{2,1,0:T(8,128)S(1)}, f32[2,8,8]{2,1,0:T(8,128)}, u32[]{:S(2)}) copy-start(f32[2,8,8]{2,1,0:T(8,128)} %sx_ref.1) | copy-start | bytes 1540
  0.0 12.1 %copy-start.6 = (f32[2,8,8]{2,1,0:T(8,128)S(1)}, f32[2,8,8]{2,1,0:T(8,128)}, u32[]{:S(2)}) copy-start(f32[2,8,8]{2,1,0:T(8,128)} %sy_ref.1) | copy-start | bytes 1540
  0.0 12.1 %copy-start.7 = (f32[64,8]{0,1:T(8,128)S(1)}, f32[64,8]{0,1:T(8,128)}, u32[]{:S(2)}) copy-start(f32[64,8]{0,1:T(8,128)} %param.17) | copy-start | bytes 6148
  0.0 12.1 %copy-start.8 = (f32[2,8]{1,0:T(2,128)S(1)}, f32[2,8]{1,0:T(2,128)}, u32[]{:S(2)}) copy-start(f32[2,8]{1,0:T(2,128)} %lx_ref.1) | copy-start | bytes 196
  0.0 12.1 %copy-start.9 = (f32[2,8]{1,0:T(2,128)S(1)}, f32[2,8]{1,0:T(2,128)}, u32[]{:S(2)}) copy-start(f32[2,8]{1,0:T(2,128)} %ly_ref.1) | copy-start | bytes 196
  5.7 8.6 %collective-permute-start = (f32[4,11776]{1,0:T(4,128)}, f32[4,11776]{1,0:T(4,128)S(1)}, u32[]{:S(2)}, u32[]{:S(2)}) collective-permute-start(f32[4,11776]{1,0:T(4,128)} %get-tuple-element.28.msg_ref), channel_id=1, source_target_pairs={{0,1},{1,0},{2,3},{3,2},{4,5},{5,4},{6,7},{7,6},{8,9},{9,8},{10,11... | collective-permute-start | bytes 565256 | tf_op jit(solution)/shard_map/ppermute | solution.py:554
  7.9 6.5 %collective-permute-start.1 = (f32[4,4608]{1,0:T(4,128)S(1)}, f32[4,4608]{1,0:T(4,128)S(1)}, u32[]{:S(2)}, u32[]{:S(2)}) collective-permute-start(f32[4,4608]{1,0:T(4,128)S(1)} %get-tuple-element.29), channel_id=1, source_target_pairs={{0,15},{1,2},{2,1},{3,4},{4,3},{5,6},{6,5},{7,8},{8,7},{9,10},{10,... | collective-permute-start | bytes 221192 | tf_op jit(solution)/shard_map/ppermute | solution.py:559
  12.2 2.2 %copy-start.2 = (f32[4,11776]{1,0:T(4,128)S(1)}, f32[4,11776]{1,0:T(4,128)}, u32[]{:S(2)}) copy-start(f32[4,11776]{1,0:T(4,128)} %get-tuple-element.28.msg_ref) | copy-start | bytes 565252
  12.2 2.9 %copy-start.3 = (f32[4,4608]{1,0:T(4,128)S(1)}, f32[4,4608]{1,0:T(4,128)}, u32[]{:S(2)}) copy-start(f32[4,4608]{1,0:T(4,128)} %get-tuple-element.34.x2_ref) | copy-start | bytes 221188
  14.4 4.8 %collective-permute-start.2 = (f32[4,6144]{1,0:T(4,128)S(1)}, f32[4,6144]{1,0:T(4,128)S(1)}, u32[]{:S(2)}, u32[]{:S(2)}) collective-permute-start(f32[4,6144]{1,0:T(4,128)S(1)} %get-tuple-element.30), channel_id=1, source_target_pairs={{0,3},{1,2},{2,1},{3,0},{4,7},{5,6},{6,5},{7,4},{8,11},{9,10},{10,... | collective-permute-start | bytes 294920 | tf_op jit(solution)/shard_map/ppermute | solution.py:554
  15.1 5.5 %collective-permute-start.8 = (f32[4,5376]{1,0:T(4,128)S(1)}, f32[4,5376]{1,0:T(4,128)S(1)}, u32[]{:S(2)}, u32[]{:S(2)}) collective-permute-start(f32[4,5376]{1,0:T(4,128)S(1)} %get-tuple-element.35), channel_id=1, source_target_pairs={{0,16},{1,17},{2,18},{3,19},{4,20},{5,21},{6,22},{7,23},{8,24},{9,... | collective-permute-start | bytes 258056 | tf_op jit(solution)/shard_map/ppermute | solution.py:554
  17.6 4.2 %collective-permute-start.9 = (f32[4,5376]{1,0:T(4,128)S(1)}, f32[4,5376]{1,0:T(4,128)S(1)}, u32[]{:S(2)}, u32[]{:S(2)}) collective-permute-start(f32[4,5376]{1,0:T(4,128)S(1)} %get-tuple-element.36), channel_id=1, source_target_pairs={{0,112},{16,32},{32,16},{48,64},{64,48},{80,96},{96,80},{112,0},{1... | collective-permute-start | bytes 258056 | tf_op jit(solution)/shard_map/ppermute | solution.py:559
  19.3 5.1 %collective-permute-start.3 = (f32[4,5120]{1,0:T(4,128)S(1)}, f32[4,5120]{1,0:T(4,128)S(1)}, u32[]{:S(2)}, u32[]{:S(2)}) collective-permute-start(f32[4,5120]{1,0:T(4,128)S(1)} %slice.44), channel_id=1, source_target_pairs={{0,4},{1,5},{2,6},{3,7},{4,0},{5,1},{6,2},{7,3},{8,12},{9,13},{10,... | collective-permute-start | bytes 245768 | tf_op jit(solution)/shard_map/ppermute | solution.py:554
  24.4 6.7 %collective-permute-start.4 = (f32[4,4096]{1,0:T(4,128)S(1)}, f32[4,4096]{1,0:T(4,128)S(1)}, u32[]{:S(2)}, u32[]{:S(2)}) collective-permute-start(f32[4,4096]{1,0:T(4,128)S(1)} %slice.45), channel_id=1, source_target_pairs={{0,12},{1,13},{2,14},{3,15},{4,8},{5,9},{6,10},{7,11},{8,4},{9,5},... | collective-permute-start | bytes 196616 | tf_op jit(solution)/shard_map/ppermute | solution.py:554
  31.2 4.2 %collective-permute-start.5 = (f32[4,3072]{1,0:T(4,128)S(1)}, f32[4,3072]{1,0:T(4,128)S(1)}, u32[]{:S(2)}, u32[]{:S(2)}) collective-permute-start(f32[4,3072]{1,0:T(4,128)S(1)} %slice.46), channel_id=1, source_target_pairs={{0,16},{1,17},{2,18},{3,19},{4,20},{5,21},{6,22},{7,23},{8,24},{9,... | collective-permute-start | bytes 147464 | tf_op jit(solution)/shard_map/ppermute | solution.py:554
  35.5 4.1 %collective-permute-start.6 = (f32[4,2048]{1,0:T(4,128)S(1)}, f32[4,2048]{1,0:T(4,128)S(1)}, u32[]{:S(2)}, u32[]{:S(2)}) collective-permute-start(f32[4,2048]{1,0:T(4,128)S(1)} %slice.47), channel_id=1, source_target_pairs={{0,32},{1,33},{2,34},{3,35},{4,36},{5,37},{6,38},{7,39},{8,40},{9,... | collective-permute-start | bytes 98312 | tf_op jit(solution)/shard_map/ppermute | solution.py:554
  39.5 2.5 %copy-start.1 = (bf16[585,512]{1,0:T(8,128)(2,1)S(1)}, bf16[585,512]{1,0:T(8,128)(2,1)}, u32[]{:S(2)}) copy-start(bf16[585,512]{1,0:T(8,128)(2,1)} %constant.8.clone.refs_5_) | copy-start | bytes 1797124
  39.6 4.3 %collective-permute-start.7 = (f32[4,1024]{1,0:T(4,128)S(1)}, f32[4,1024]{1,0:T(4,128)S(1)}, u32[]{:S(2)}, u32[]{:S(2)}) collective-permute-start(f32[4,1024]{1,0:T(4,128)S(1)} %get-tuple-element.48.mine_ref), channel_id=1, source_target_pairs={{0,96},{1,97},{2,98},{3,99},{4,100},{5,101},{6,102},{7,103},{8,104... | collective-permute-start | bytes 49160 | tf_op jit(solution)/shard_map/ppermute | solution.py:554

commit v3 on v2

--- a/solution.py
+++ b/solution.py
@@ -83,7 +83,7 @@
 FACE = 12 * 384
 SLAB = 14 * 384
 PADDED = 7296
-BIG = 55040 << 10
+BIG = 54272 << 10
 ROW_CHUNKS = ((512, 73), (0, 256), (256, 128), (384, 128))
 SMALL = 24 << 20
 MIDDLE = 48 << 20
@@ -100,14 +100,12 @@
 
 
 def forward_kernel(
-    r_hbm, rz_hbm, tile_hbm, f_ref,
+    r_hbm, f_ref,
     msg_ref, own_ref, y2_ref, x1_ref, x2_ref,
-    r_ref, rz_ref, tile_ref, keep_ref, u_ref, acc_ref, small_sems, sems,
+    r_ref, keep_ref, u_ref, acc_ref, field_sem, sems,
 ):
-    small = []
-    for k, (src, dst) in enumerate(((r_hbm, r_ref), (rz_hbm, rz_ref), (tile_hbm, tile_ref))):
-        small.append(pltpu.make_async_copy(src, dst, small_sems.at[k]))
-        small[-1].start()
+    field_copy = pltpu.make_async_copy(r_hbm, r_ref, field_sem)
+    field_copy.start()
     copies = []
     for k, (start, size) in enumerate(ROW_CHUNKS):
         rows = pl.ds(start, size)
@@ -115,7 +113,19 @@
     copies[0].start()
 
     u_ref[...] = jnp.zeros_like(u_ref)
-    small[0].wait()
+    z = lax.broadcasted_iota(jnp.int32, (384, 128), 0)
+    vertex = lax.broadcasted_iota(jnp.int32, (384, 128), 1)
+    elem = z // 6
+    low, high = jnp.zeros((384, 128), F32), jnp.zeros((384, 128), F32)
+    for k in range(6):
+        low = jnp.where(z - 6 * elem == k, float(restrict_np[0, k]), low)
+        high = jnp.where(z - 6 * elem == k, float(restrict_np[1, k]), high)
+    rz = jnp.where(vertex == elem, low, jnp.where(vertex == elem + 1, high, 0.0))
+    place = lax.broadcasted_iota(jnp.int32, (128, 640), 1)
+    row = lax.broadcasted_iota(jnp.int32, (128, 640), 0)
+    tile = jnp.where(row == place - 65 * (place // 65), 1.0, 0.0).astype(BF)
+
+    field_copy.wait()
     for copy in copies[1:]:
         copy.start()
     r0 = [float(v) for v in restrict_np[0]]
@@ -137,13 +147,11 @@
             for t, table in ((0, r0), (1, r1)):
                 row = (a * 3 + y_elem + t) * 8
                 u_ref[row : row + 4, :] += sum(table[j] * sums[j][a] for j in range(6))
-    small[1].wait()
     vert = lax.dot_general(
-        u_ref[...], rz_ref[...], (((1,), (0,)), ((), ())),
+        u_ref[...], rz, (((1,), (0,)), ((), ())),
         precision=lax.Precision.HIGHEST, preferred_element_type=F32,
     ).astype(BF)
-    small[2].wait()
-    spread = dot(vert, tile_ref[...])
+    spread = dot(vert, tile)
     spread = jnp.where(ab_mask(72, 640), spread, 0.0)
     v = sum(spread[8 * k : 8 * k + 8] for k in range(9)).astype(BF)[:, :VLOC]
 
@@ -168,33 +176,25 @@
 
 
 def forward(field, factor):
-    rz = np.zeros((384, 128), np.float32)
-    rz[:, :65] = line_table(restrict_np, 64)
-    tile = np.zeros((128, 640), ml_dtypes.bfloat16)
-    for ab in range(9):
-        for c in range(65):
-            tile[c, ab * 65 + c] = 1
     shapes = [(4, LEVELS * SEP + FACE), (4, 128), (4, FACE), (4, FACE), (4, FACE)]
     vm = pl.BlockSpec(memory_space=pltpu.VMEM)
     return pl.pallas_call(
         forward_kernel,
-        in_specs=[HBM] * 4,
+        in_specs=[HBM] * 2,
         out_specs=[vm] * 5,
         out_shape=[jax.ShapeDtypeStruct(v, F32) for v in shapes],
         scratch_shapes=[
             pltpu.VMEM((12, 12, 4, 384), F32),
-            pltpu.VMEM((384, 128), F32),
-            pltpu.VMEM((128, 640), BF),
             pltpu.VMEM((VLOC, COLS), BF),
             pltpu.VMEM((72, 384), F32),
             pltpu.VMEM((8, PADDED), F32),
-            pltpu.SemaphoreType.DMA((3,)),
+            pltpu.SemaphoreType.DMA,
             pltpu.SemaphoreType.DMA((len(ROW_CHUNKS),)),
         ],
         compiler_params=pltpu.CompilerParams(vmem_limit_bytes=BIG),
         cost_estimate=pl.CostEstimate(flops=2 * 8 * VLOC * COLS, bytes_accessed=9_500_000, transcendentals=0),
         name="forward",
-    )(field, jnp.asarray(rz), jnp.asarray(tile), factor)
+    )(field, factor)
 
 
 def join_kernel(wait_ref, msg_ref, y1_ref, y2_ref, level_ref, rest_ref):

time: 46.3 us -> 45.6 us (0.985)
  Pallas kernels: 20.6 us -> 19.9 us
    pallas_call x1, Pallas kernels: 5.68 us -> 5.01 us  [forward(): pl.pallas_call(forward_kernel, in_specs=[HBM] * 2, out_specs=[vm] * 5, ou...]
where the time goes in v3:
time: 45.6 us; the launch traced here: 45.4 us
  starting transfers between devices  22 us (48%)
  Pallas kernels  19.9 us (44%)
  waiting for transfers between devices  2.01 us (4%)
  local copies, waits for them, and re-layouts  0.99 us (2%)
    ppermute x8, starting transfers between devices, exchange(): lax.ppermute(value, ('gx', 'gy'), [(i, i ^ mask) for i in range(128)])  16.1 us
    pallas_call x4, Pallas kernels, schwarz(): pl.pallas_call(kernel, in_specs=[UNUSED] + [vm] * 10 + ([vm] * len(levels...  9.56 us
    ppermute x2, starting transfers between devices, odd_pairs(): lax.ppermute(value, axis, [(i, (i + 1) % count if i % 2 else (i - 1) % co...  5.88 us
    pallas_call x1, Pallas kernels, forward(): pl.pallas_call(forward_kernel, in_specs=[HBM] * 2, out_specs=[vm] * 5, ou...  5.01 us
    pallas_call x1, Pallas kernels, late(): pl.pallas_call(late_kernel, in_specs=[vm] * 4, out_specs=vm, out_shape=ja...  2.12 us
    ppermute x2, waiting for transfers between devices, odd_pairs(): lax.ppermute(value, axis, [(i, (i + 1) % count if i % 2 else (i - 1) % co...  1.99 us
    pallas_call x1, Pallas kernels, packed(): pl.pallas_call(pack_kernel, in_specs=[vm] * (2 + len(vertex)) + [HBM] * 2...  1.82 us
    pallas_call x1, Pallas kernels, tables(): pl.pallas_call(tables_kernel, in_specs=[UNUSED] + [vm] * 7, out_specs=[vm...  1.36 us
  transfers between devices with their start and end apart: 10, of which 2 were waited for; matrix products, arithmetic and copies ran while one was open for 2% of the time, Pallas kernels for 28%

profile of v3, /device:TPU:1, one launch (start us, length us, event | category | flops | bytes accessed | tf_op | source)
XLA Modules:
  0.0 45.4 jit_solution(13487843700648024055)
XLA Ops:
  0.0 5.0 %forward.1 = (f32[4,11776]{1,0:T(4,128)S(1)}, f32[4,128]{1,0:T(4,128)S(1)}, f32[4,4608]{1,0:T(4,128)S(1)}, f32[4,4608]{1,0:T(4,128)S(1)}, f32[4,4608]{1,0:T(4,128)S(1)}) custom-call(f32[12,12,4,384]{3,2,1,0:T(4,128)} %bitcast.10, bf16[585,7233]{1,0:T(8,128)(2,1)} %bitcast.14), custom_call_target="tpu_custom_call" | custom-call | flops 67700880 | bytes 9500000 | tf_op jit(solution)/shard_map/forward/pallas_call | solution.py:181
  5.1 2.1 %collective-permute-start = (f32[4,11776]{1,0:T(4,128)S(1)}, f32[4,11776]{1,0:T(4,128)S(1)}, u32[]{:S(2)}, u32[]{:S(2)}) collective-permute-start(f32[4,11776]{1,0:T(4,128)S(1)} %get-tuple-element.28.msg_ref), channel_id=1, source_target_pairs={{0,1},{1,0},{2,3},{3,2},{4,5},{5,4},{6,7},{7,6},{8,9},{9,8},{10,11... | collective-permute-start | bytes 565256 | tf_op jit(solution)/shard_map/ppermute | solution.py:554
  7.2 4.3 %collective-permute-start.1 = (f32[4,4608]{1,0:T(4,128)S(1)}, f32[4,4608]{1,0:T(4,128)S(1)}, u32[]{:S(2)}, u32[]{:S(2)}) collective-permute-start(f32[4,4608]{1,0:T(4,128)S(1)} %get-tuple-element.29), channel_id=1, source_target_pairs={{0,15},{1,2},{2,1},{3,4},{4,3},{5,6},{6,5},{7,8},{8,7},{9,10},{10,... | collective-permute-start | bytes 221192 | tf_op jit(solution)/shard_map/ppermute | solution.py:559
  11.5 1.4 %tables.1 = (bf16[2,256,256]{2,1,0:T(8,128)(2,1)S(1)}, bf16[2,256,256]{2,1,0:T(8,128)(2,1)S(1)}, bf16[2,2,256,256]{3,2,1,0:T(8,128)(2,1)S(1)}, bf16[2,2,256,256]...) custom-call(f32[4,128]{1,0:T(4,128)S(1)} %get-tuple-element.26.wait_ref.refs_11_, ...), custom_call_target="tpu_custom_call" | custom-call | flops 1000000000 | bytes 2000000 | tf_op jit(solution)/shard_map/tables/pallas_call | solution.py:333
  12.9 0.8 %collective-permute-done.1.y2_ref.refs_3_ = f32[4,4608]{1,0:T(4,128)S(1)} collective-permute-done((f32[4,4608]{1,0:T(4,128)S(1)}, f32[4,4608]{1,0:T(4,128)S(1)}, u32[]{:S(2)}, u32[]{:S(2)}) %collective-permute-start.1) | collective-permute-done | bytes 73760 | tf_op jit(solution)/shard_map/ppermute | solution.py:559
  13.7 0.7 %collective-permute-start.2 = (f32[4,6144]{1,0:T(4,128)S(1)}, f32[4,6144]{1,0:T(4,128)S(1)}, u32[]{:S(2)}, u32[]{:S(2)}) collective-permute-start(f32[4,6144]{1,0:T(4,128)S(1)} %get-tuple-element.30), channel_id=1, source_target_pairs={{0,3},{1,2},{2,1},{3,0},{4,7},{5,6},{6,5},{7,4},{8,11},{9,10},{10,... | collective-permute-start | bytes 294920 | tf_op jit(solution)/shard_map/ppermute | solution.py:554
  14.4 2.5 %collective-permute-start.8 = (f32[4,5376]{1,0:T(4,128)S(1)}, f32[4,5376]{1,0:T(4,128)S(1)}, u32[]{:S(2)}, u32[]{:S(2)}) collective-permute-start(f32[4,5376]{1,0:T(4,128)S(1)} %get-tuple-element.35), channel_id=1, source_target_pairs={{0,16},{1,17},{2,18},{3,19},{4,20},{5,21},{6,22},{7,23},{8,24},{9,... | collective-permute-start | bytes 258056 | tf_op jit(solution)/shard_map/ppermute | solution.py:554
  16.9 1.6 %collective-permute-start.9 = (f32[4,5376]{1,0:T(4,128)S(1)}, f32[4,5376]{1,0:T(4,128)S(1)}, u32[]{:S(2)}, u32[]{:S(2)}) collective-permute-start(f32[4,5376]{1,0:T(4,128)S(1)} %get-tuple-element.36), channel_id=1, source_target_pairs={{0,112},{16,32},{32,16},{48,64},{64,48},{80,96},{96,80},{112,0},{1... | collective-permute-start | bytes 258056 | tf_op jit(solution)/shard_map/ppermute | solution.py:559
  18.6 1.4 %collective-permute-start.3 = (f32[4,5120]{1,0:T(4,128)S(1)}, f32[4,5120]{1,0:T(4,128)S(1)}, u32[]{:S(2)}, u32[]{:S(2)}) collective-permute-start(f32[4,5120]{1,0:T(4,128)S(1)} %slice.44), channel_id=1, source_target_pairs={{0,4},{1,5},{2,6},{3,7},{4,0},{5,1},{6,2},{7,3},{8,12},{9,13},{10,... | collective-permute-start | bytes 245768 | tf_op jit(solution)/shard_map/ppermute | solution.py:554
  20.0 1.1 %collective-permute-done.9.refs_5_ = f32[4,5376]{1,0:T(4,128)S(1)} collective-permute-done((f32[4,5376]{1,0:T(4,128)S(1)}, f32[4,5376]{1,0:T(4,128)S(1)}, u32[]{:S(2)}, u32[]{:S(2)}) %collective-permute-start.9) | collective-permute-done | bytes 86048 | tf_op jit(solution)/shard_map/ppermute | solution.py:559
  21.1 2.6 %schwarz.4 = (f32[1,192,384]{2,1,0:T(8,128)S(1)}, f32[8,640]{1,0:T(8,128)S(1)}) custom-call(f32[4,1024]{1,0:T(4,128)S(1)} %slice.51.refs_0_.refs_13_.refs_11_, f32[4,224,384]{2,1,0:T(8,128)S(1)} %get-tuple-element.31.refs_1_, f32[4,11776]{1,0:T(4,128)S(1)} %collective-permute-done.y1_ref.refs_2_, f32[4,4608]{1,0:T(4,128)S(1)} %collective-permute-done.1.y2_ref.refs_3_, ...), custom_call_target="tpu_custom_call" | custom-call | flops 900000000 | bytes 700000 | tf_op jit(solution)/shard_map/schwarz/pallas_call | solution.py:433
  23.8 3.7 %collective-permute-start.4 = (f32[4,4096]{1,0:T(4,128)S(1)}, f32[4,4096]{1,0:T(4,128)S(1)}, u32[]{:S(2)}, u32[]{:S(2)}) collective-permute-start(f32[4,4096]{1,0:T(4,128)S(1)} %slice.45), channel_id=1, source_target_pairs={{0,12},{1,13},{2,14},{3,15},{4,8},{5,9},{6,10},{7,11},{8,4},{9,5},... | collective-permute-start | bytes 196616 | tf_op jit(solution)/shard_map/ppermute | solution.py:554
  27.5 3.0 %schwarz.5 = (f32[1,192,384]{2,1,0:T(8,128)S(1)}, f32[8,640]{1,0:T(8,128)S(1)}) custom-call(f32[4,1024]{1,0:T(4,128)S(1)} %slice.52.refs_0_.refs_12_.refs_11_, f32[4,224,384]{2,1,0:T(8,128)S(1)} %get-tuple-element.31.refs_1_, f32[4,11776]{1,0:T(4,128)S(1)} %collective-permute-done.y1_ref.refs_2_, f32[4,4608]{1,0:T(4,128)S(1)} %collective-permute-done.1.y2_ref.refs_3_, ...), custom_call_target="tpu_custom_call" | custom-call | flops 900000000 | bytes 700000 | tf_op jit(solution)/shard_map/schwarz/pallas_call | solution.py:433
  30.6 2.8 %collective-permute-start.5 = (f32[4,3072]{1,0:T(4,128)S(1)}, f32[4,3072]{1,0:T(4,128)S(1)}, u32[]{:S(2)}, u32[]{:S(2)}) collective-permute-start(f32[4,3072]{1,0:T(4,128)S(1)} %slice.46), channel_id=1, source_target_pairs={{0,16},{1,17},{2,18},{3,19},{4,20},{5,21},{6,22},{7,23},{8,24},{9,... | collective-permute-start | bytes 147464 | tf_op jit(solution)/shard_map/ppermute | solution.py:554
  33.3 1.4 %schwarz.7 = f32[1,192,384]{2,1,0:T(8,128)S(1)} custom-call(f32[4,1024]{1,0:T(4,128)S(1)} %slice.53.refs_12_.refs_0_, f32[4,224,384]{2,1,0:T(8,128)S(1)} %get-tuple-element.31.refs_1_, f32[4,11776]{1,0:T(4,128)S(1)} %collective-permute-done.y1_ref.refs_2_, f32[4,4608]{1,0:T(4,128)S(1)} %collective-permute-done.1.y2_ref.refs_3_, ...), custom_call_target="tpu_custom_call" | custom-call | flops 900000000 | bytes 700000 | tf_op jit(solution)/shard_map/schwarz/pallas_call | solution.py:433
  34.8 0.6 %collective-permute-start.6 = (f32[4,2048]{1,0:T(4,128)S(1)}, f32[4,2048]{1,0:T(4,128)S(1)}, u32[]{:S(2)}, u32[]{:S(2)}) collective-permute-start(f32[4,2048]{1,0:T(4,128)S(1)} %slice.47), channel_id=1, source_target_pairs={{0,32},{1,33},{2,34},{3,35},{4,36},{5,37},{6,38},{7,39},{8,40},{9,... | collective-permute-start | bytes 98312 | tf_op jit(solution)/shard_map/ppermute | solution.py:554
  35.4 2.6 %schwarz.6 = (f32[1,192,384]{2,1,0:T(8,128)S(1)}, f32[8,640]{1,0:T(8,128)S(1)}) custom-call(f32[4,1024]{1,0:T(4,128)S(1)} %slice.49.refs_0_.refs_13_, f32[4,224,384]{2,1,0:T(8,128)S(1)} %get-tuple-element.31.refs_1_, f32[4,11776]{1,0:T(4,128)S(1)} %collective-permute-done.y1_ref.refs_2_, f32[4,4608]{1,0:T(4,128)S(1)} %collective-permute-done.1.y2_ref.refs_3_, ...), custom_call_target="tpu_custom_call" | custom-call | flops 900000000 | bytes 700000 | tf_op jit(solution)/shard_map/schwarz/pallas_call | solution.py:433
  38.0 0.1 pad_maximum_fusion
  38.1 0.8 %copy.10 = f32[4,192,384]{2,0,1:T(4,128)S(1)} copy(f32[4,192,384]{2,1,0:T(8,128)S(1)} %pad_maximum_fusion) | data formatting | bytes 2359296 | tf_op jit(solution)/shard_map/concatenate | solution.py:593
  38.9 0.0 copy-start.1
  38.9 2.3 %collective-permute-start.7 = (f32[4,1024]{1,0:T(4,128)S(1)}, f32[4,1024]{1,0:T(4,128)S(1)}, u32[]{:S(2)}, u32[]{:S(2)}) collective-permute-start(f32[4,1024]{1,0:T(4,128)S(1)} %get-tuple-element.48.mine_ref), channel_id=1, source_target_pairs={{0,96},{1,97},{2,98},{3,99},{4,100},{5,101},{6,102},{7,103},{8,104... | collective-permute-start | bytes 49160 | tf_op jit(solution)/shard_map/ppermute | solution.py:554
  41.3 0.2 slice_bitcast_fusion.s_ref
  41.4 1.8 %pack.1.pack_ref = bf16[585,2304]{1,0:T(8,128)(2,1)S(1)} custom-call(f32[4,1024]{1,0:T(4,128)S(1)} %slice.49.refs_0_.refs_13_, f32[4,1024]{1,0:T(4,128)S(1)} %get-tuple-element.47.refs_1_, f32[8,640]{1,0:T(8,128)S(1)} %get-tuple-element.41.refs_2_, f32[8,640]{1,0:T(8,128)S(1)} %get-tuple-element.42.refs_3_, f32[8,640]{1,0:T(8,128)S(1)} %get-tuple-element.43.refs_4_, ...), custom_call_target="tpu_custom_call" | custom-call | flops 9584640 | bytes 4000000 | tf_op jit(solution)/shard_map/pack/pallas_call | solution.py:494
  43.3 2.1 %late.1 = f32[12,12,4,384]{3,2,1,0:T(4,128)} custom-call(f32[4,1024]{1,0:T(4,128)S(1)} %get-tuple-element.48.mine_ref, f32[4,1024]{1,0:T(4,128)S(1)} %collective-permute-done.7.got_ref, bf16[585,2304]{1,0:T(8,128)(2,1)S(1)} %pack.1.pack_ref, f32[12,12,4,384]{3,2,1,0:T(4,128)S(1)} %slice_bitcast_fusion.s_ref), custom_call_target="tpu_custom_call" | custom-call | flops 9584640 | bytes 5000000 | tf_op jit(solution)/shard_map/late/pallas_call | solution.py:542
  (39 shorter events, 0.2 us)
Async XLA Ops:
  0.0 11.5 %copy-start = (f32[4,12,12,384]{3,0,2,1:T(4,128)S(1)}, f32[4,12,12,384]{3,0,2,1:T(4,128)}, u32[]{:S(2)}) copy-start(f32[4,12,12,384]{3,0,2,1:T(4,128)} %param.9) | copy-start | bytes 2654212
  0.0 11.5 %copy-start.2 = (f32[64,8,8]{0,2,1:T(8,128)S(1)}, f32[64,8,8]{0,2,1:T(8,128)}, u32[]{:S(2)}) copy-start(f32[64,8,8]{0,2,1:T(8,128)} %param.12) | copy-start | bytes 49156
  0.0 11.5 %copy-start.3 = (f32[2,8,8]{2,1,0:T(8,128)S(1)}, f32[2,8,8]{2,1,0:T(8,128)}, u32[]{:S(2)}) copy-start(f32[2,8,8]{2,1,0:T(8,128)} %sx_ref.1) | copy-start | bytes 1540
  0.0 11.5 %copy-start.4 = (f32[2,8,8]{2,1,0:T(8,128)S(1)}, f32[2,8,8]{2,1,0:T(8,128)}, u32[]{:S(2)}) copy-start(f32[2,8,8]{2,1,0:T(8,128)} %sy_ref.1) | copy-start | bytes 1540
  0.0 11.5 %copy-start.5 = (f32[64,8]{0,1:T(8,128)S(1)}, f32[64,8]{0,1:T(8,128)}, u32[]{:S(2)}) copy-start(f32[64,8]{0,1:T(8,128)} %param.15) | copy-start | bytes 6148
  0.0 11.5 %copy-start.6 = (f32[2,8]{1,0:T(2,128)S(1)}, f32[2,8]{1,0:T(2,128)}, u32[]{:S(2)}) copy-start(f32[2,8]{1,0:T(2,128)} %lx_ref.1) | copy-start | bytes 196
  0.0 11.5 %copy-start.7 = (f32[2,8]{1,0:T(2,128)S(1)}, f32[2,8]{1,0:T(2,128)}, u32[]{:S(2)}) copy-start(f32[2,8]{1,0:T(2,128)} %ly_ref.1) | copy-start | bytes 196
  5.1 8.6 %collective-permute-start = (f32[4,11776]{1,0:T(4,128)S(1)}, f32[4,11776]{1,0:T(4,128)S(1)}, u32[]{:S(2)}, u32[]{:S(2)}) collective-permute-start(f32[4,11776]{1,0:T(4,128)S(1)} %get-tuple-element.28.msg_ref), channel_id=1, source_target_pairs={{0,1},{1,0},{2,3},{3,2},{4,5},{5,4},{6,7},{7,6},{8,9},{9,8},{10,11... | collective-permute-start | bytes 565256 | tf_op jit(solution)/shard_map/ppermute | solution.py:554
  7.2 6.5 %collective-permute-start.1 = (f32[4,4608]{1,0:T(4,128)S(1)}, f32[4,4608]{1,0:T(4,128)S(1)}, u32[]{:S(2)}, u32[]{:S(2)}) collective-permute-start(f32[4,4608]{1,0:T(4,128)S(1)} %get-tuple-element.29), channel_id=1, source_target_pairs={{0,15},{1,2},{2,1},{3,4},{4,3},{5,6},{6,5},{7,8},{8,7},{9,10},{10,... | collective-permute-start | bytes 221192 | tf_op jit(solution)/shard_map/ppermute | solution.py:559
  13.7 4.8 %collective-permute-start.2 = (f32[4,6144]{1,0:T(4,128)S(1)}, f32[4,6144]{1,0:T(4,128)S(1)}, u32[]{:S(2)}, u32[]{:S(2)}) collective-permute-start(f32[4,6144]{1,0:T(4,128)S(1)} %get-tuple-element.30), channel_id=1, source_target_pairs={{0,3},{1,2},{2,1},{3,0},{4,7},{5,6},{6,5},{7,4},{8,11},{9,10},{10,... | collective-permute-start | bytes 294920 | tf_op jit(solution)/shard_map/ppermute | solution.py:554
  14.4 5.5 %collective-permute-start.8 = (f32[4,5376]{1,0:T(4,128)S(1)}, f32[4,5376]{1,0:T(4,128)S(1)}, u32[]{:S(2)}, u32[]{:S(2)}) collective-permute-start(f32[4,5376]{1,0:T(4,128)S(1)} %get-tuple-element.35), channel_id=1, source_target_pairs={{0,16},{1,17},{2,18},{3,19},{4,20},{5,21},{6,22},{7,23},{8,24},{9,... | collective-permute-start | bytes 258056 | tf_op jit(solution)/shard_map/ppermute | solution.py:554
  16.9 4.2 %collective-permute-start.9 = (f32[4,5376]{1,0:T(4,128)S(1)}, f32[4,5376]{1,0:T(4,128)S(1)}, u32[]{:S(2)}, u32[]{:S(2)}) collective-permute-start(f32[4,5376]{1,0:T(4,128)S(1)} %get-tuple-element.36), channel_id=1, source_target_pairs={{0,112},{16,32},{32,16},{48,64},{64,48},{80,96},{96,80},{112,0},{1... | collective-permute-start | bytes 258056 | tf_op jit(solution)/shard_map/ppermute | solution.py:559
  18.6 5.1 %collective-permute-start.3 = (f32[4,5120]{1,0:T(4,128)S(1)}, f32[4,5120]{1,0:T(4,128)S(1)}, u32[]{:S(2)}, u32[]{:S(2)}) collective-permute-start(f32[4,5120]{1,0:T(4,128)S(1)} %slice.44), channel_id=1, source_target_pairs={{0,4},{1,5},{2,6},{3,7},{4,0},{5,1},{6,2},{7,3},{8,12},{9,13},{10,... | collective-permute-start | bytes 245768 | tf_op jit(solution)/shard_map/ppermute | solution.py:554
  23.8 6.7 %collective-permute-start.4 = (f32[4,4096]{1,0:T(4,128)S(1)}, f32[4,4096]{1,0:T(4,128)S(1)}, u32[]{:S(2)}, u32[]{:S(2)}) collective-permute-start(f32[4,4096]{1,0:T(4,128)S(1)} %slice.45), channel_id=1, source_target_pairs={{0,12},{1,13},{2,14},{3,15},{4,8},{5,9},{6,10},{7,11},{8,4},{9,5},... | collective-permute-start | bytes 196616 | tf_op jit(solution)/shard_map/ppermute | solution.py:554
  30.6 4.2 %collective-permute-start.5 = (f32[4,3072]{1,0:T(4,128)S(1)}, f32[4,3072]{1,0:T(4,128)S(1)}, u32[]{:S(2)}, u32[]{:S(2)}) collective-permute-start(f32[4,3072]{1,0:T(4,128)S(1)} %slice.46), channel_id=1, source_target_pairs={{0,16},{1,17},{2,18},{3,19},{4,20},{5,21},{6,22},{7,23},{8,24},{9,... | collective-permute-start | bytes 147464 | tf_op jit(solution)/shard_map/ppermute | solution.py:554
  34.8 4.1 %collective-permute-start.6 = (f32[4,2048]{1,0:T(4,128)S(1)}, f32[4,2048]{1,0:T(4,128)S(1)}, u32[]{:S(2)}, u32[]{:S(2)}) collective-permute-start(f32[4,2048]{1,0:T(4,128)S(1)} %slice.47), channel_id=1, source_target_pairs={{0,32},{1,33},{2,34},{3,35},{4,36},{5,37},{6,38},{7,39},{8,40},{9,... | collective-permute-start | bytes 98312 | tf_op jit(solution)/shard_map/ppermute | solution.py:554
  38.9 2.5 %copy-start.1 = (bf16[585,512]{1,0:T(8,128)(2,1)S(1)}, bf16[585,512]{1,0:T(8,128)(2,1)}, u32[]{:S(2)}) copy-start(bf16[585,512]{1,0:T(8,128)(2,1)} %constant.2.clone.refs_5_) | copy-start | bytes 1797124
  38.9 4.3 %collective-permute-start.7 = (f32[4,1024]{1,0:T(4,128)S(1)}, f32[4,1024]{1,0:T(4,128)S(1)}, u32[]{:S(2)}, u32[]{:S(2)}) collective-permute-start(f32[4,1024]{1,0:T(4,128)S(1)} %get-tuple-element.48.mine_ref), channel_id=1, source_target_pairs={{0,96},{1,97},{2,98},{3,99},{4,100},{5,101},{6,102},{7,103},{8,104... | collective-permute-start | bytes 49160 | tf_op jit(solution)/shard_map/ppermute | solution.py:554

commit v4 on v3

--- a/solution.py
+++ b/solution.py
@@ -419,14 +419,16 @@
                 [backs[0][:, :128], backs[0][:, 128:] + backs[1][:, :128], backs[1][:, 128:]], axis=1
             )
         )
-        out_ref[k] = dot3((b_ref[0][:192], b_ref[1][:192]), t4)
+        res = dot3((b_ref[0][:192], b_ref[1][:192]), t4)
+        for x in range(12):
+            out_ref[k, x] = res[16 * x : 16 * x + 12, :]
 
 
 def schwarz(first, wait, chunks, levels, factor, field, y1, y2, m1, m2, tabs):
     vm = pl.BlockSpec(memory_space=pltpu.VMEM)
     kernel = lambda *refs: schwarz_kernel(first, chunks, *refs)
     extra = (*levels, factor) if chunks else ()
-    out = jax.ShapeDtypeStruct((1, 192, 384), F32)
+    out = jax.ShapeDtypeStruct((1, 12, 12, 384), F32)
     scratch = [pltpu.VMEM((1, 224, 384), F32)]
     if chunks:
         scratch += [pltpu.VMEM((VLOC, len(chunks) * SEP), BF), pltpu.SemaphoreType.DMA]
@@ -590,7 +592,7 @@
             vertex.append(more)
         parts.append(part)
     pack = packed(done[5], done[6], vertex, factor)
-    solved = jnp.concatenate(parts, axis=0).reshape(4, 12, 16, 384)[:, :, :12].transpose(1, 2, 0, 3)
+    solved = jnp.concatenate(parts, axis=0).transpose(1, 2, 0, 3)
     out = late(sep, got, pack, solved)
     return out.transpose(2, 0, 1, 3)
 

time: 45.6 us -> 46.5 us (1.020)
  other arithmetic: 0.18 us -> 0.94 us
    pallas_call x0 -> x4, local copies, waits for them, and re-layouts: none -> 0.92 us  [schwarz(): pl.pallas_call(kernel, in_specs=[UNUSED] + [vm] * 10 + ([vm] * len(levels...]
    transpose x0 -> x1, other arithmetic: none -> 0.84 us  [local(): solved = jnp.concatenate(parts, axis=0).transpose(1, 2, 0, 3)]
    concatenate x1 -> x0, local copies, waits for them, and re-layouts: 0.76 us -> none  [local(): jnp.concatenate(parts, axis=0).reshape(4, 12, 16, 384)[:, :, :12]]
  transfers between devices with their start and end apart: 10 -> 10, of which waited for: 2 -> 2; matrix products, arithmetic and copies ran while one was open for 2% -> 4% of each run, Pallas kernels for 28% -> 28%
where the time goes in v4:
time: 46.5 us; the launch traced here: 45.8 us
  starting transfers between devices  21.7 us (47%)
  Pallas kernels  19.9 us (43%)
  waiting for transfers between devices  2.01 us (4%)
  local copies, waits for them, and re-layouts  0.99 us (2%)
  other arithmetic  0.94 us (2%)
    ppermute x8, starting transfers between devices, exchange(): lax.ppermute(value, ('gx', 'gy'), [(i, i ^ mask) for i in range(128)])  15.8 us
    pallas_call x4, Pallas kernels, schwarz(): pl.pallas_call(kernel, in_specs=[UNUSED] + [vm] * 10 + ([vm] * len(levels...  9.56 us
    ppermute x2, starting transfers between devices, odd_pairs(): lax.ppermute(value, axis, [(i, (i + 1) % count if i % 2 else (i - 1) % co...  5.88 us
    pallas_call x1, Pallas kernels, forward(): pl.pallas_call(forward_kernel, in_specs=[HBM] * 2, out_specs=[vm] * 5, ou...  5.01 us
    pallas_call x1, Pallas kernels, late(): pl.pallas_call(late_kernel, in_specs=[vm] * 4, out_specs=vm, out_shape=ja...  2.12 us
    ppermute x2, waiting for transfers between devices, odd_pairs(): lax.ppermute(value, axis, [(i, (i + 1) % count if i % 2 else (i - 1) % co...  1.99 us
    pallas_call x1, Pallas kernels, packed(): pl.pallas_call(pack_kernel, in_specs=[vm] * (2 + len(vertex)) + [HBM] * 2...  1.82 us
    pallas_call x1, Pallas kernels, tables(): pl.pallas_call(tables_kernel, in_specs=[UNUSED] + [vm] * 7, out_specs=[vm...  1.36 us
  transfers between devices with their start and end apart: 10, of which 2 were waited for; matrix products, arithmetic and copies ran while one was open for 4% of the time, Pallas kernels for 28%

profile of v4, /device:TPU:1, one launch (start us, length us, event | category | flops | bytes accessed | tf_op | source)
XLA Modules:
  0.0 45.8 jit_solution(8529099085800513693)
XLA Ops:
  0.0 5.0 %forward.1 = (f32[4,11776]{1,0:T(4,128)S(1)}, f32[4,128]{1,0:T(4,128)S(1)}, f32[4,4608]{1,0:T(4,128)S(1)}, f32[4,4608]{1,0:T(4,128)S(1)}, f32[4,4608]{1,0:T(4,128)S(1)}) custom-call(f32[12,12,4,384]{3,2,1,0:T(4,128)} %bitcast.9, bf16[585,7233]{1,0:T(8,128)(2,1)} %bitcast.13), custom_call_target="tpu_custom_call" | custom-call | flops 67700880 | bytes 9500000 | tf_op jit(solution)/shard_map/forward/pallas_call | solution.py:181
  5.1 2.1 %collective-permute-start = (f32[4,11776]{1,0:T(4,128)S(1)}, f32[4,11776]{1,0:T(4,128)S(1)}, u32[]{:S(2)}, u32[]{:S(2)}) collective-permute-start(f32[4,11776]{1,0:T(4,128)S(1)} %get-tuple-element.28.msg_ref), channel_id=1, source_target_pairs={{0,1},{1,0},{2,3},{3,2},{4,5},{5,4},{6,7},{7,6},{8,9},{9,8},{10,11... | collective-permute-start | bytes 565256 | tf_op jit(solution)/shard_map/ppermute | solution.py:556
  7.2 4.3 %collective-permute-start.1 = (f32[4,4608]{1,0:T(4,128)S(1)}, f32[4,4608]{1,0:T(4,128)S(1)}, u32[]{:S(2)}, u32[]{:S(2)}) collective-permute-start(f32[4,4608]{1,0:T(4,128)S(1)} %get-tuple-element.29), channel_id=1, source_target_pairs={{0,15},{1,2},{2,1},{3,4},{4,3},{5,6},{6,5},{7,8},{8,7},{9,10},{10,... | collective-permute-start | bytes 221192 | tf_op jit(solution)/shard_map/ppermute | solution.py:561
  11.5 1.4 %tables.1 = (bf16[2,256,256]{2,1,0:T(8,128)(2,1)S(1)}, bf16[2,256,256]{2,1,0:T(8,128)(2,1)S(1)}, bf16[2,2,256,256]{3,2,1,0:T(8,128)(2,1)S(1)}, bf16[2,2,256,256]...) custom-call(f32[4,128]{1,0:T(4,128)S(1)} %get-tuple-element.26.wait_ref.refs_11_, ...), custom_call_target="tpu_custom_call" | custom-call | flops 1000000000 | bytes 2000000 | tf_op jit(solution)/shard_map/tables/pallas_call | solution.py:333
  12.9 0.8 %collective-permute-done.1.y2_ref.refs_3_ = f32[4,4608]{1,0:T(4,128)S(1)} collective-permute-done((f32[4,4608]{1,0:T(4,128)S(1)}, f32[4,4608]{1,0:T(4,128)S(1)}, u32[]{:S(2)}, u32[]{:S(2)}) %collective-permute-start.1) | collective-permute-done | bytes 73760 | tf_op jit(solution)/shard_map/ppermute | solution.py:561
  13.7 0.7 %collective-permute-start.2 = (f32[4,6144]{1,0:T(4,128)S(1)}, f32[4,6144]{1,0:T(4,128)S(1)}, u32[]{:S(2)}, u32[]{:S(2)}) collective-permute-start(f32[4,6144]{1,0:T(4,128)S(1)} %get-tuple-element.30), channel_id=1, source_target_pairs={{0,3},{1,2},{2,1},{3,0},{4,7},{5,6},{6,5},{7,4},{8,11},{9,10},{10,... | collective-permute-start | bytes 294920 | tf_op jit(solution)/shard_map/ppermute | solution.py:556
  14.4 2.5 %collective-permute-start.8 = (f32[4,5376]{1,0:T(4,128)S(1)}, f32[4,5376]{1,0:T(4,128)S(1)}, u32[]{:S(2)}, u32[]{:S(2)}) collective-permute-start(f32[4,5376]{1,0:T(4,128)S(1)} %get-tuple-element.35), channel_id=1, source_target_pairs={{0,16},{1,17},{2,18},{3,19},{4,20},{5,21},{6,22},{7,23},{8,24},{9,... | collective-permute-start | bytes 258056 | tf_op jit(solution)/shard_map/ppermute | solution.py:556
  16.9 1.6 %collective-permute-start.9 = (f32[4,5376]{1,0:T(4,128)S(1)}, f32[4,5376]{1,0:T(4,128)S(1)}, u32[]{:S(2)}, u32[]{:S(2)}) collective-permute-start(f32[4,5376]{1,0:T(4,128)S(1)} %get-tuple-element.36), channel_id=1, source_target_pairs={{0,112},{16,32},{32,16},{48,64},{64,48},{80,96},{96,80},{112,0},{1... | collective-permute-start | bytes 258056 | tf_op jit(solution)/shard_map/ppermute | solution.py:561
  18.6 1.4 %collective-permute-start.3 = (f32[4,5120]{1,0:T(4,128)S(1)}, f32[4,5120]{1,0:T(4,128)S(1)}, u32[]{:S(2)}, u32[]{:S(2)}) collective-permute-start(f32[4,5120]{1,0:T(4,128)S(1)} %slice.40), channel_id=1, source_target_pairs={{0,4},{1,5},{2,6},{3,7},{4,0},{5,1},{6,2},{7,3},{8,12},{9,13},{10,... | collective-permute-start | bytes 245768 | tf_op jit(solution)/shard_map/ppermute | solution.py:556
  20.0 1.1 %collective-permute-done.9.refs_5_ = f32[4,5376]{1,0:T(4,128)S(1)} collective-permute-done((f32[4,5376]{1,0:T(4,128)S(1)}, f32[4,5376]{1,0:T(4,128)S(1)}, u32[]{:S(2)}, u32[]{:S(2)}) %collective-permute-start.9) | collective-permute-done | bytes 86048 | tf_op jit(solution)/shard_map/ppermute | solution.py:561
  21.1 2.6 %schwarz.4 = (f32[1,12,12,384]{3,2,1,0:T(8,128)S(1)}, f32[8,640]{1,0:T(8,128)S(1)}) custom-call(f32[4,1024]{1,0:T(4,128)S(1)} %slice.47.refs_0_.refs_13_.refs_11_, f32[4,224,384]{2,1,0:T(8,128)S(1)} %get-tuple-element.31.refs_1_, f32[4,11776]{1,0:T(4,128)S(1)} %collective-permute-done.y1_ref.refs_2_, f32[4,4608]{1,0:T(4,128)S(1)} %collective-permute-done.1.y2_ref.refs_3_, ...), custom_call_target="tpu_custom_call" | custom-call | flops 900000000 | bytes 700000 | tf_op jit(solution)/shard_map/schwarz/pallas_call | solution.py:435
  23.7 0.2 copy.10
  24.0 3.7 %collective-permute-start.4 = (f32[4,4096]{1,0:T(4,128)S(1)}, f32[4,4096]{1,0:T(4,128)S(1)}, u32[]{:S(2)}, u32[]{:S(2)}) collective-permute-start(f32[4,4096]{1,0:T(4,128)S(1)} %slice.41), channel_id=1, source_target_pairs={{0,12},{1,13},{2,14},{3,15},{4,8},{5,9},{6,10},{7,11},{8,4},{9,5},... | collective-permute-start | bytes 196616 | tf_op jit(solution)/shard_map/ppermute | solution.py:556
  27.7 3.0 %schwarz.5 = (f32[1,12,12,384]{3,2,1,0:T(8,128)S(1)}, f32[8,640]{1,0:T(8,128)S(1)}) custom-call(f32[4,1024]{1,0:T(4,128)S(1)} %slice.48.refs_0_.refs_12_.refs_11_, f32[4,224,384]{2,1,0:T(8,128)S(1)} %get-tuple-element.31.refs_1_, f32[4,11776]{1,0:T(4,128)S(1)} %collective-permute-done.y1_ref.refs_2_, f32[4,4608]{1,0:T(4,128)S(1)} %collective-permute-done.1.y2_ref.refs_3_, ...), custom_call_target="tpu_custom_call" | custom-call | flops 900000000 | bytes 700000 | tf_op jit(solution)/shard_map/schwarz/pallas_call | solution.py:435
  30.7 0.2 copy.11
  31.0 2.8 %collective-permute-start.5 = (f32[4,3072]{1,0:T(4,128)S(1)}, f32[4,3072]{1,0:T(4,128)S(1)}, u32[]{:S(2)}, u32[]{:S(2)}) collective-permute-start(f32[4,3072]{1,0:T(4,128)S(1)} %slice.42), channel_id=1, source_target_pairs={{0,16},{1,17},{2,18},{3,19},{4,20},{5,21},{6,22},{7,23},{8,24},{9,... | collective-permute-start | bytes 147464 | tf_op jit(solution)/shard_map/ppermute | solution.py:556
  33.8 1.4 %schwarz.7 = f32[1,12,12,384]{3,2,1,0:T(8,128)S(1)} custom-call(f32[4,1024]{1,0:T(4,128)S(1)} %slice.49.refs_12_.refs_0_, f32[4,224,384]{2,1,0:T(8,128)S(1)} %get-tuple-element.31.refs_1_, f32[4,11776]{1,0:T(4,128)S(1)} %collective-permute-done.y1_ref.refs_2_, f32[4,4608]{1,0:T(4,128)S(1)} %collective-permute-done.1.y2_ref.refs_3_, ...), custom_call_target="tpu_custom_call" | custom-call | flops 900000000 | bytes 700000 | tf_op jit(solution)/shard_map/schwarz/pallas_call | solution.py:435
  35.2 0.2 copy.12
  35.5 0.3 collective-permute-start.6
  35.8 2.6 %schwarz.6 = (f32[1,12,12,384]{3,2,1,0:T(8,128)S(1)}, f32[8,640]{1,0:T(8,128)S(1)}) custom-call(f32[4,1024]{1,0:T(4,128)S(1)} %slice.45.refs_0_.refs_13_, f32[4,224,384]{2,1,0:T(8,128)S(1)} %get-tuple-element.31.refs_1_, f32[4,11776]{1,0:T(4,128)S(1)} %collective-permute-done.y1_ref.refs_2_, f32[4,4608]{1,0:T(4,128)S(1)} %collective-permute-done.1.y2_ref.refs_3_, ...), custom_call_target="tpu_custom_call" | custom-call | flops 900000000 | bytes 700000 | tf_op jit(solution)/shard_map/schwarz/pallas_call | solution.py:435
  38.7 2.4 %collective-permute-start.7 = (f32[4,1024]{1,0:T(4,128)S(1)}, f32[4,1024]{1,0:T(4,128)S(1)}, u32[]{:S(2)}, u32[]{:S(2)}) collective-permute-start(f32[4,1024]{1,0:T(4,128)S(1)} %get-tuple-element.48.mine_ref), channel_id=1, source_target_pairs={{0,96},{1,97},{2,98},{3,99},{4,100},{5,101},{6,102},{7,103},{8,104... | collective-permute-start | bytes 49160 | tf_op jit(solution)/shard_map/ppermute | solution.py:556
  41.0 0.8 %maximum_bitcast_fusion.s_ref = f32[12,12,4,384]{3,2,1,0:T(4,128)S(1)} fusion(f32[1,12,12,384]{3,0,2,1:T(1,128)S(1)} %copy.13, f32[1,12,12,384]{3,0,2,1:T(1,128)S(1)} %copy.12, f32[1,12,12,384]{3,0,2,1:T(1,128)S(1)} %copy.11, f32[1,12,12,384]{3,0,2,1:T(1,128)S(1)} %copy.10), kind=kLoop, calls=%fused_computation | loop fusion | flops 663552 | bytes 1769472 | tf_op jit(solution)/shard_map/transpose | solution.py:595
  41.9 1.8 %pack.1.pack_ref = bf16[585,2304]{1,0:T(8,128)(2,1)S(1)} custom-call(f32[4,1024]{1,0:T(4,128)S(1)} %slice.45.refs_0_.refs_13_, f32[4,1024]{1,0:T(4,128)S(1)} %get-tuple-element.47.refs_1_, f32[8,640]{1,0:T(8,128)S(1)} %get-tuple-element.41.refs_2_, f32[8,640]{1,0:T(8,128)S(1)} %get-tuple-element.42.refs_3_, f32[8,640]{1,0:T(8,128)S(1)} %get-tuple-element.43.refs_4_, ...), custom_call_target="tpu_custom_call" | custom-call | flops 9584640 | bytes 4000000 | tf_op jit(solution)/shard_map/pack/pallas_call | solution.py:496
  43.7 2.1 %late.1 = f32[12,12,4,384]{3,2,1,0:T(4,128)} custom-call(f32[4,1024]{1,0:T(4,128)S(1)} %get-tuple-element.48.mine_ref, f32[4,1024]{1,0:T(4,128)S(1)} %collective-permute-done.7.got_ref, bf16[585,2304]{1,0:T(8,128)(2,1)S(1)} %pack.1.pack_ref, f32[12,12,4,384]{3,2,1,0:T(4,128)S(1)} %maximum_bitcast_fusion.s_ref), custom_call_target="tpu_custom_call" | custom-call | flops 9584640 | bytes 5000000 | tf_op jit(solution)/shard_map/late/pallas_call | solution.py:544
  (41 shorter events, 0.5 us)
Async XLA Ops:
  0.0 11.5 %copy-start = (f32[4,12,12,384]{3,0,2,1:T(4,128)S(1)}, f32[4,12,12,384]{3,0,2,1:T(4,128)}, u32[]{:S(2)}) copy-start(f32[4,12,12,384]{3,0,2,1:T(4,128)} %param.9) | copy-start | bytes 2654212
  0.0 11.5 %copy-start.2 = (f32[64,8,8]{0,2,1:T(8,128)S(1)}, f32[64,8,8]{0,2,1:T(8,128)}, u32[]{:S(2)}) copy-start(f32[64,8,8]{0,2,1:T(8,128)} %param.12) | copy-start | bytes 49156
  0.0 11.5 %copy-start.3 = (f32[2,8,8]{2,1,0:T(8,128)S(1)}, f32[2,8,8]{2,1,0:T(8,128)}, u32[]{:S(2)}) copy-start(f32[2,8,8]{2,1,0:T(8,128)} %sx_ref.1) | copy-start | bytes 1540
  0.0 11.5 %copy-start.4 = (f32[2,8,8]{2,1,0:T(8,128)S(1)}, f32[2,8,8]{2,1,0:T(8,128)}, u32[]{:S(2)}) copy-start(f32[2,8,8]{2,1,0:T(8,128)} %sy_ref.1) | copy-start | bytes 1540
  0.0 11.5 %copy-start.5 = (f32[64,8]{0,1:T(8,128)S(1)}, f32[64,8]{0,1:T(8,128)}, u32[]{:S(2)}) copy-start(f32[64,8]{0,1:T(8,128)} %param.15) | copy-start | bytes 6148
  0.0 11.5 %copy-start.6 = (f32[2,8]{1,0:T(2,128)S(1)}, f32[2,8]{1,0:T(2,128)}, u32[]{:S(2)}) copy-start(f32[2,8]{1,0:T(2,128)} %lx_ref.1) | copy-start | bytes 196
  0.0 11.5 %copy-start.7 = (f32[2,8]{1,0:T(2,128)S(1)}, f32[2,8]{1,0:T(2,128)}, u32[]{:S(2)}) copy-start(f32[2,8]{1,0:T(2,128)} %ly_ref.1) | copy-start | bytes 196
  5.1 8.6 %collective-permute-start = (f32[4,11776]{1,0:T(4,128)S(1)}, f32[4,11776]{1,0:T(4,128)S(1)}, u32[]{:S(2)}, u32[]{:S(2)}) collective-permute-start(f32[4,11776]{1,0:T(4,128)S(1)} %get-tuple-element.28.msg_ref), channel_id=1, source_target_pairs={{0,1},{1,0},{2,3},{3,2},{4,5},{5,4},{6,7},{7,6},{8,9},{9,8},{10,11... | collective-permute-start | bytes 565256 | tf_op jit(solution)/shard_map/ppermute | solution.py:556
  7.2 6.5 %collective-permute-start.1 = (f32[4,4608]{1,0:T(4,128)S(1)}, f32[4,4608]{1,0:T(4,128)S(1)}, u32[]{:S(2)}, u32[]{:S(2)}) collective-permute-start(f32[4,4608]{1,0:T(4,128)S(1)} %get-tuple-element.29), channel_id=1, source_target_pairs={{0,15},{1,2},{2,1},{3,4},{4,3},{5,6},{6,5},{7,8},{8,7},{9,10},{10,... | collective-permute-start | bytes 221192 | tf_op jit(solution)/shard_map/ppermute | solution.py:561
  13.7 4.8 %collective-permute-start.2 = (f32[4,6144]{1,0:T(4,128)S(1)}, f32[4,6144]{1,0:T(4,128)S(1)}, u32[]{:S(2)}, u32[]{:S(2)}) collective-permute-start(f32[4,6144]{1,0:T(4,128)S(1)} %get-tuple-element.30), channel_id=1, source_target_pairs={{0,3},{1,2},{2,1},{3,0},{4,7},{5,6},{6,5},{7,4},{8,11},{9,10},{10,... | collective-permute-start | bytes 294920 | tf_op jit(solution)/shard_map/ppermute | solution.py:556
  14.4 5.5 %collective-permute-start.8 = (f32[4,5376]{1,0:T(4,128)S(1)}, f32[4,5376]{1,0:T(4,128)S(1)}, u32[]{:S(2)}, u32[]{:S(2)}) collective-permute-start(f32[4,5376]{1,0:T(4,128)S(1)} %get-tuple-element.35), channel_id=1, source_target_pairs={{0,16},{1,17},{2,18},{3,19},{4,20},{5,21},{6,22},{7,23},{8,24},{9,... | collective-permute-start | bytes 258056 | tf_op jit(solution)/shard_map/ppermute | solution.py:556
  16.9 4.2 %collective-permute-start.9 = (f32[4,5376]{1,0:T(4,128)S(1)}, f32[4,5376]{1,0:T(4,128)S(1)}, u32[]{:S(2)}, u32[]{:S(2)}) collective-permute-start(f32[4,5376]{1,0:T(4,128)S(1)} %get-tuple-element.36), channel_id=1, source_target_pairs={{0,112},{16,32},{32,16},{48,64},{64,48},{80,96},{96,80},{112,0},{1... | collective-permute-start | bytes 258056 | tf_op jit(solution)/shard_map/ppermute | solution.py:561
  18.6 5.3 %collective-permute-start.3 = (f32[4,5120]{1,0:T(4,128)S(1)}, f32[4,5120]{1,0:T(4,128)S(1)}, u32[]{:S(2)}, u32[]{:S(2)}) collective-permute-start(f32[4,5120]{1,0:T(4,128)S(1)} %slice.40), channel_id=1, source_target_pairs={{0,4},{1,5},{2,6},{3,7},{4,0},{5,1},{6,2},{7,3},{8,12},{9,13},{10,... | collective-permute-start | bytes 245768 | tf_op jit(solution)/shard_map/ppermute | solution.py:556
  24.0 7.0 %collective-permute-start.4 = (f32[4,4096]{1,0:T(4,128)S(1)}, f32[4,4096]{1,0:T(4,128)S(1)}, u32[]{:S(2)}, u32[]{:S(2)}) collective-permute-start(f32[4,4096]{1,0:T(4,128)S(1)} %slice.41), channel_id=1, source_target_pairs={{0,12},{1,13},{2,14},{3,15},{4,8},{5,9},{6,10},{7,11},{8,4},{9,5},... | collective-permute-start | bytes 196616 | tf_op jit(solution)/shard_map/ppermute | solution.py:556
  31.0 4.4 %collective-permute-start.5 = (f32[4,3072]{1,0:T(4,128)S(1)}, f32[4,3072]{1,0:T(4,128)S(1)}, u32[]{:S(2)}, u32[]{:S(2)}) collective-permute-start(f32[4,3072]{1,0:T(4,128)S(1)} %slice.42), channel_id=1, source_target_pairs={{0,16},{1,17},{2,18},{3,19},{4,20},{5,21},{6,22},{7,23},{8,24},{9,... | collective-permute-start | bytes 147464 | tf_op jit(solution)/shard_map/ppermute | solution.py:556
  35.5 3.1 %collective-permute-start.6 = (f32[4,2048]{1,0:T(4,128)S(1)}, f32[4,2048]{1,0:T(4,128)S(1)}, u32[]{:S(2)}, u32[]{:S(2)}) collective-permute-start(f32[4,2048]{1,0:T(4,128)S(1)} %slice.43), channel_id=1, source_target_pairs={{0,32},{1,33},{2,34},{3,35},{4,36},{5,37},{6,38},{7,39},{8,40},{9,... | collective-permute-start | bytes 98312 | tf_op jit(solution)/shard_map/ppermute | solution.py:556
  38.4 3.5 %copy-start.1 = (bf16[585,512]{1,0:T(8,128)(2,1)S(1)}, bf16[585,512]{1,0:T(8,128)(2,1)}, u32[]{:S(2)}) copy-start(bf16[585,512]{1,0:T(8,128)(2,1)} %constant.2.clone.refs_5_) | copy-start | bytes 1797124
  38.7 5.0 %collective-permute-start.7 = (f32[4,1024]{1,0:T(4,128)S(1)}, f32[4,1024]{1,0:T(4,128)S(1)}, u32[]{:S(2)}, u32[]{:S(2)}) collective-permute-start(f32[4,1024]{1,0:T(4,128)S(1)} %get-tuple-element.48.mine_ref), channel_id=1, source_target_pairs={{0,96},{1,97},{2,98},{3,99},{4,100},{5,101},{6,102},{7,103},{8,104... | collective-permute-start | bytes 49160 | tf_op jit(solution)/shard_map/ppermute | solution.py:556

commit v5 on v3

--- a/solution.py
+++ b/solution.py
@@ -383,7 +383,9 @@
         total = jnp.zeros((8, VLOC), F32)
         for k, chunk in enumerate(chunks):
             values = chunk_values(chunk, level_refs[k : k + 2])
-            total = total + dot(values, chunk_ref[:, k * SEP : k * SEP + SEP], NT)
+            for h in range(0, SEP, SEP // 2):
+                cols = slice(k * SEP + h, k * SEP + h + SEP // 2)
+                total = total + dot(values[:, h : h + SEP // 2], chunk_ref[:, cols], NT)
         v_ref[:, :VLOC] = total
         v_ref[:, VLOC:] = jnp.zeros((8, 640 - VLOC), F32)
 
@@ -463,7 +465,8 @@
         copies[-1].start()
     values = shifted(l5_ref[...], l6_ref[...]).astype(BF)
     copies[0].wait()
-    v = dot(values, chunk_ref[...], NT)
+    v = dot(values[:, : SEP // 2], chunk_ref[:, : SEP // 2], NT)
+    v = v + dot(values[:, SEP // 2 :], chunk_ref[:, SEP // 2 :], NT)
     v = jnp.concatenate([v, jnp.zeros((8, 640 - VLOC), F32)], axis=1)
     v = v + sum(ref[...] for ref in vertex_refs)
     for k in range(3):
@@ -513,7 +516,8 @@
     lane = lax.broadcasted_iota(jnp.int32, (8, 128), 1)
     head = jnp.where(lane < LEAF, pack_ref[48:64, PACK_V : PACK_V + 128][:8].astype(F32), top[:, :128])
     nv = jnp.concatenate([head, top[:, 128:]], axis=1).astype(BF)
-    add = dot(nv, pack_ref[:, :PACK_PZ], NT)
+    add = dot(nv[:, : SEP // 2], pack_ref[:, : SEP // 2], NT)
+    add = add + dot(nv[:, SEP // 2 :], pack_ref[:, SEP // 2 : PACK_PZ], NT)
     v = jnp.concatenate([add, jnp.zeros((8, 640 - VLOC), F32)], axis=1)
     for k in range(3):
         v = v + pack_ref[32 - 16 * k : 48 - 16 * k, PACK_V:][:8].astype(F32)

time: 45.6 us -> 45.7 us (level)
  no operation moved by 1% of the time
where the time goes in v5:
time: 45.7 us; the launch traced here: 45.4 us
  starting transfers between devices  22 us (48%)
  Pallas kernels  19.9 us (44%)
  waiting for transfers between devices  2.01 us (4%)
  local copies, waits for them, and re-layouts  0.99 us (2%)
    ppermute x8, starting transfers between devices, exchange(): lax.ppermute(value, ('gx', 'gy'), [(i, i ^ mask) for i in range(128)])  16.1 us
    pallas_call x4, Pallas kernels, schwarz(): pl.pallas_call(kernel, in_specs=[UNUSED] + [vm] * 10 + ([vm] * len(levels...  9.56 us
    ppermute x2, starting transfers between devices, odd_pairs(): lax.ppermute(value, axis, [(i, (i + 1) % count if i % 2 else (i - 1) % co...  5.88 us
    pallas_call x1, Pallas kernels, forward(): pl.pallas_call(forward_kernel, in_specs=[HBM] * 2, out_specs=[vm] * 5, ou...  5.01 us
    pallas_call x1, Pallas kernels, late(): pl.pallas_call(late_kernel, in_specs=[vm] * 4, out_specs=vm, out_shape=ja...  2.14 us
    ppermute x2, waiting for transfers between devices, odd_pairs(): lax.ppermute(value, axis, [(i, (i + 1) % count if i % 2 else (i - 1) % co...  1.99 us
    pallas_call x1, Pallas kernels, packed(): pl.pallas_call(pack_kernel, in_specs=[vm] * (2 + len(vertex)) + [HBM] * 2...  1.82 us
    pallas_call x1, Pallas kernels, tables(): pl.pallas_call(tables_kernel, in_specs=[UNUSED] + [vm] * 7, out_specs=[vm...  1.36 us
  transfers between devices with their start and end apart: 10, of which 2 were waited for; matrix products, arithmetic and copies ran while one was open for 2% of the time, Pallas kernels for 28%

profile of v5, /device:TPU:1, one launch (start us, length us, event | category | flops | bytes accessed | tf_op | source)
XLA Modules:
  0.0 45.4 jit_solution(15198201518136300185)
XLA Ops:
  0.0 5.0 %forward.1 = (f32[4,11776]{1,0:T(4,128)S(1)}, f32[4,128]{1,0:T(4,128)S(1)}, f32[4,4608]{1,0:T(4,128)S(1)}, f32[4,4608]{1,0:T(4,128)S(1)}, f32[4,4608]{1,0:T(4,128)S(1)}) custom-call(f32[12,12,4,384]{3,2,1,0:T(4,128)} %bitcast.10, bf16[585,7233]{1,0:T(8,128)(2,1)} %bitcast.14), custom_call_target="tpu_custom_call" | custom-call | flops 67700880 | bytes 9500000 | tf_op jit(solution)/shard_map/forward/pallas_call | solution.py:181
  5.1 2.1 %collective-permute-start = (f32[4,11776]{1,0:T(4,128)S(1)}, f32[4,11776]{1,0:T(4,128)S(1)}, u32[]{:S(2)}, u32[]{:S(2)}) collective-permute-start(f32[4,11776]{1,0:T(4,128)S(1)} %get-tuple-element.28.msg_ref), channel_id=1, source_target_pairs={{0,1},{1,0},{2,3},{3,2},{4,5},{5,4},{6,7},{7,6},{8,9},{9,8},{10,11... | collective-permute-start | bytes 565256 | tf_op jit(solution)/shard_map/ppermute | solution.py:558
  7.2 4.3 %collective-permute-start.1 = (f32[4,4608]{1,0:T(4,128)S(1)}, f32[4,4608]{1,0:T(4,128)S(1)}, u32[]{:S(2)}, u32[]{:S(2)}) collective-permute-start(f32[4,4608]{1,0:T(4,128)S(1)} %get-tuple-element.29), channel_id=1, source_target_pairs={{0,15},{1,2},{2,1},{3,4},{4,3},{5,6},{6,5},{7,8},{8,7},{9,10},{10,... | collective-permute-start | bytes 221192 | tf_op jit(solution)/shard_map/ppermute | solution.py:563
  11.5 1.4 %tables.1 = (bf16[2,256,256]{2,1,0:T(8,128)(2,1)S(1)}, bf16[2,256,256]{2,1,0:T(8,128)(2,1)S(1)}, bf16[2,2,256,256]{3,2,1,0:T(8,128)(2,1)S(1)}, bf16[2,2,256,256]...) custom-call(f32[4,128]{1,0:T(4,128)S(1)} %get-tuple-element.26.wait_ref.refs_11_, ...), custom_call_target="tpu_custom_call" | custom-call | flops 1000000000 | bytes 2000000 | tf_op jit(solution)/shard_map/tables/pallas_call | solution.py:333
  12.9 0.8 %collective-permute-done.1.y2_ref.refs_3_ = f32[4,4608]{1,0:T(4,128)S(1)} collective-permute-done((f32[4,4608]{1,0:T(4,128)S(1)}, f32[4,4608]{1,0:T(4,128)S(1)}, u32[]{:S(2)}, u32[]{:S(2)}) %collective-permute-start.1) | collective-permute-done | bytes 73760 | tf_op jit(solution)/shard_map/ppermute | solution.py:563
  13.7 0.7 %collective-permute-start.2 = (f32[4,6144]{1,0:T(4,128)S(1)}, f32[4,6144]{1,0:T(4,128)S(1)}, u32[]{:S(2)}, u32[]{:S(2)}) collective-permute-start(f32[4,6144]{1,0:T(4,128)S(1)} %get-tuple-element.30), channel_id=1, source_target_pairs={{0,3},{1,2},{2,1},{3,0},{4,7},{5,6},{6,5},{7,4},{8,11},{9,10},{10,... | collective-permute-start | bytes 294920 | tf_op jit(solution)/shard_map/ppermute | solution.py:558
  14.4 2.5 %collective-permute-start.8 = (f32[4,5376]{1,0:T(4,128)S(1)}, f32[4,5376]{1,0:T(4,128)S(1)}, u32[]{:S(2)}, u32[]{:S(2)}) collective-permute-start(f32[4,5376]{1,0:T(4,128)S(1)} %get-tuple-element.35), channel_id=1, source_target_pairs={{0,16},{1,17},{2,18},{3,19},{4,20},{5,21},{6,22},{7,23},{8,24},{9,... | collective-permute-start | bytes 258056 | tf_op jit(solution)/shard_map/ppermute | solution.py:558
  16.9 1.6 %collective-permute-start.9 = (f32[4,5376]{1,0:T(4,128)S(1)}, f32[4,5376]{1,0:T(4,128)S(1)}, u32[]{:S(2)}, u32[]{:S(2)}) collective-permute-start(f32[4,5376]{1,0:T(4,128)S(1)} %get-tuple-element.36), channel_id=1, source_target_pairs={{0,112},{16,32},{32,16},{48,64},{64,48},{80,96},{96,80},{112,0},{1... | collective-permute-start | bytes 258056 | tf_op jit(solution)/shard_map/ppermute | solution.py:563
  18.6 1.4 %collective-permute-start.3 = (f32[4,5120]{1,0:T(4,128)S(1)}, f32[4,5120]{1,0:T(4,128)S(1)}, u32[]{:S(2)}, u32[]{:S(2)}) collective-permute-start(f32[4,5120]{1,0:T(4,128)S(1)} %slice.44), channel_id=1, source_target_pairs={{0,4},{1,5},{2,6},{3,7},{4,0},{5,1},{6,2},{7,3},{8,12},{9,13},{10,... | collective-permute-start | bytes 245768 | tf_op jit(solution)/shard_map/ppermute | solution.py:558
  20.0 1.1 %collective-permute-done.9.refs_5_ = f32[4,5376]{1,0:T(4,128)S(1)} collective-permute-done((f32[4,5376]{1,0:T(4,128)S(1)}, f32[4,5376]{1,0:T(4,128)S(1)}, u32[]{:S(2)}, u32[]{:S(2)}) %collective-permute-start.9) | collective-permute-done | bytes 86048 | tf_op jit(solution)/shard_map/ppermute | solution.py:563
  21.1 2.6 %schwarz.4 = (f32[1,192,384]{2,1,0:T(8,128)S(1)}, f32[8,640]{1,0:T(8,128)S(1)}) custom-call(f32[4,1024]{1,0:T(4,128)S(1)} %slice.51.refs_0_.refs_13_.refs_11_, f32[4,224,384]{2,1,0:T(8,128)S(1)} %get-tuple-element.31.refs_1_, f32[4,11776]{1,0:T(4,128)S(1)} %collective-permute-done.y1_ref.refs_2_, f32[4,4608]{1,0:T(4,128)S(1)} %collective-permute-done.1.y2_ref.refs_3_, ...), custom_call_target="tpu_custom_call" | custom-call | flops 900000000 | bytes 700000 | tf_op jit(solution)/shard_map/schwarz/pallas_call | solution.py:435
  23.8 3.7 %collective-permute-start.4 = (f32[4,4096]{1,0:T(4,128)S(1)}, f32[4,4096]{1,0:T(4,128)S(1)}, u32[]{:S(2)}, u32[]{:S(2)}) collective-permute-start(f32[4,4096]{1,0:T(4,128)S(1)} %slice.45), channel_id=1, source_target_pairs={{0,12},{1,13},{2,14},{3,15},{4,8},{5,9},{6,10},{7,11},{8,4},{9,5},... | collective-permute-start | bytes 196616 | tf_op jit(solution)/shard_map/ppermute | solution.py:558
  27.5 3.0 %schwarz.5 = (f32[1,192,384]{2,1,0:T(8,128)S(1)}, f32[8,640]{1,0:T(8,128)S(1)}) custom-call(f32[4,1024]{1,0:T(4,128)S(1)} %slice.52.refs_0_.refs_12_.refs_11_, f32[4,224,384]{2,1,0:T(8,128)S(1)} %get-tuple-element.31.refs_1_, f32[4,11776]{1,0:T(4,128)S(1)} %collective-permute-done.y1_ref.refs_2_, f32[4,4608]{1,0:T(4,128)S(1)} %collective-permute-done.1.y2_ref.refs_3_, ...), custom_call_target="tpu_custom_call" | custom-call | flops 900000000 | bytes 700000 | tf_op jit(solution)/shard_map/schwarz/pallas_call | solution.py:435
  30.6 2.8 %collective-permute-start.5 = (f32[4,3072]{1,0:T(4,128)S(1)}, f32[4,3072]{1,0:T(4,128)S(1)}, u32[]{:S(2)}, u32[]{:S(2)}) collective-permute-start(f32[4,3072]{1,0:T(4,128)S(1)} %slice.46), channel_id=1, source_target_pairs={{0,16},{1,17},{2,18},{3,19},{4,20},{5,21},{6,22},{7,23},{8,24},{9,... | collective-permute-start | bytes 147464 | tf_op jit(solution)/shard_map/ppermute | solution.py:558
  33.3 1.4 %schwarz.7 = f32[1,192,384]{2,1,0:T(8,128)S(1)} custom-call(f32[4,1024]{1,0:T(4,128)S(1)} %slice.53.refs_12_.refs_0_, f32[4,224,384]{2,1,0:T(8,128)S(1)} %get-tuple-element.31.refs_1_, f32[4,11776]{1,0:T(4,128)S(1)} %collective-permute-done.y1_ref.refs_2_, f32[4,4608]{1,0:T(4,128)S(1)} %collective-permute-done.1.y2_ref.refs_3_, ...), custom_call_target="tpu_custom_call" | custom-call | flops 900000000 | bytes 700000 | tf_op jit(solution)/shard_map/schwarz/pallas_call | solution.py:435
  34.8 0.6 %collective-permute-start.6 = (f32[4,2048]{1,0:T(4,128)S(1)}, f32[4,2048]{1,0:T(4,128)S(1)}, u32[]{:S(2)}, u32[]{:S(2)}) collective-permute-start(f32[4,2048]{1,0:T(4,128)S(1)} %slice.47), channel_id=1, source_target_pairs={{0,32},{1,33},{2,34},{3,35},{4,36},{5,37},{6,38},{7,39},{8,40},{9,... | collective-permute-start | bytes 98312 | tf_op jit(solution)/shard_map/ppermute | solution.py:558
  35.4 2.6 %schwarz.6 = (f32[1,192,384]{2,1,0:T(8,128)S(1)}, f32[8,640]{1,0:T(8,128)S(1)}) custom-call(f32[4,1024]{1,0:T(4,128)S(1)} %slice.49.refs_0_.refs_13_, f32[4,224,384]{2,1,0:T(8,128)S(1)} %get-tuple-element.31.refs_1_, f32[4,11776]{1,0:T(4,128)S(1)} %collective-permute-done.y1_ref.refs_2_, f32[4,4608]{1,0:T(4,128)S(1)} %collective-permute-done.1.y2_ref.refs_3_, ...), custom_call_target="tpu_custom_call" | custom-call | flops 900000000 | bytes 700000 | tf_op jit(solution)/shard_map/schwarz/pallas_call | solution.py:435
  38.0 0.1 pad_maximum_fusion
  38.1 0.8 %copy.10 = f32[4,192,384]{2,0,1:T(4,128)S(1)} copy(f32[4,192,384]{2,1,0:T(8,128)S(1)} %pad_maximum_fusion) | data formatting | bytes 2359296 | tf_op jit(solution)/shard_map/concatenate | solution.py:597
  38.9 0.0 copy-start.1
  38.9 2.3 %collective-permute-start.7 = (f32[4,1024]{1,0:T(4,128)S(1)}, f32[4,1024]{1,0:T(4,128)S(1)}, u32[]{:S(2)}, u32[]{:S(2)}) collective-permute-start(f32[4,1024]{1,0:T(4,128)S(1)} %get-tuple-element.48.mine_ref), channel_id=1, source_target_pairs={{0,96},{1,97},{2,98},{3,99},{4,100},{5,101},{6,102},{7,103},{8,104... | collective-permute-start | bytes 49160 | tf_op jit(solution)/shard_map/ppermute | solution.py:558
  41.3 0.2 slice_bitcast_fusion.s_ref
  41.4 1.8 %pack.1.pack_ref = bf16[585,2304]{1,0:T(8,128)(2,1)S(1)} custom-call(f32[4,1024]{1,0:T(4,128)S(1)} %slice.49.refs_0_.refs_13_, f32[4,1024]{1,0:T(4,128)S(1)} %get-tuple-element.47.refs_1_, f32[8,640]{1,0:T(8,128)S(1)} %get-tuple-element.41.refs_2_, f32[8,640]{1,0:T(8,128)S(1)} %get-tuple-element.42.refs_3_, f32[8,640]{1,0:T(8,128)S(1)} %get-tuple-element.43.refs_4_, ...), custom_call_target="tpu_custom_call" | custom-call | flops 9584640 | bytes 4000000 | tf_op jit(solution)/shard_map/pack/pallas_call | solution.py:497
  43.3 2.1 %late.1 = f32[12,12,4,384]{3,2,1,0:T(4,128)} custom-call(f32[4,1024]{1,0:T(4,128)S(1)} %get-tuple-element.48.mine_ref, f32[4,1024]{1,0:T(4,128)S(1)} %collective-permute-done.7.got_ref, bf16[585,2304]{1,0:T(8,128)(2,1)S(1)} %pack.1.pack_ref, f32[12,12,4,384]{3,2,1,0:T(4,128)S(1)} %slice_bitcast_fusion.s_ref), custom_call_target="tpu_custom_call" | custom-call | flops 9584640 | bytes 5000000 | tf_op jit(solution)/shard_map/late/pallas_call | solution.py:546
  (39 shorter events, 0.2 us)
Async XLA Ops:
  0.0 11.5 %copy-start = (f32[4,12,12,384]{3,0,2,1:T(4,128)S(1)}, f32[4,12,12,384]{3,0,2,1:T(4,128)}, u32[]{:S(2)}) copy-start(f32[4,12,12,384]{3,0,2,1:T(4,128)} %param.9) | copy-start | bytes 2654212
  0.0 11.5 %copy-start.2 = (f32[64,8,8]{0,2,1:T(8,128)S(1)}, f32[64,8,8]{0,2,1:T(8,128)}, u32[]{:S(2)}) copy-start(f32[64,8,8]{0,2,1:T(8,128)} %param.12) | copy-start | bytes 49156
  0.0 11.5 %copy-start.3 = (f32[2,8,8]{2,1,0:T(8,128)S(1)}, f32[2,8,8]{2,1,0:T(8,128)}, u32[]{:S(2)}) copy-start(f32[2,8,8]{2,1,0:T(8,128)} %sx_ref.1) | copy-start | bytes 1540
  0.0 11.5 %copy-start.4 = (f32[2,8,8]{2,1,0:T(8,128)S(1)}, f32[2,8,8]{2,1,0:T(8,128)}, u32[]{:S(2)}) copy-start(f32[2,8,8]{2,1,0:T(8,128)} %sy_ref.1) | copy-start | bytes 1540
  0.0 11.5 %copy-start.5 = (f32[64,8]{0,1:T(8,128)S(1)}, f32[64,8]{0,1:T(8,128)}, u32[]{:S(2)}) copy-start(f32[64,8]{0,1:T(8,128)} %param.15) | copy-start | bytes 6148
  0.0 11.5 %copy-start.6 = (f32[2,8]{1,0:T(2,128)S(1)}, f32[2,8]{1,0:T(2,128)}, u32[]{:S(2)}) copy-start(f32[2,8]{1,0:T(2,128)} %lx_ref.1) | copy-start | bytes 196
  0.0 11.5 %copy-start.7 = (f32[2,8]{1,0:T(2,128)S(1)}, f32[2,8]{1,0:T(2,128)}, u32[]{:S(2)}) copy-start(f32[2,8]{1,0:T(2,128)} %ly_ref.1) | copy-start | bytes 196
  5.1 8.6 %collective-permute-start = (f32[4,11776]{1,0:T(4,128)S(1)}, f32[4,11776]{1,0:T(4,128)S(1)}, u32[]{:S(2)}, u32[]{:S(2)}) collective-permute-start(f32[4,11776]{1,0:T(4,128)S(1)} %get-tuple-element.28.msg_ref), channel_id=1, source_target_pairs={{0,1},{1,0},{2,3},{3,2},{4,5},{5,4},{6,7},{7,6},{8,9},{9,8},{10,11... | collective-permute-start | bytes 565256 | tf_op jit(solution)/shard_map/ppermute | solution.py:558
  7.2 6.5 %collective-permute-start.1 = (f32[4,4608]{1,0:T(4,128)S(1)}, f32[4,4608]{1,0:T(4,128)S(1)}, u32[]{:S(2)}, u32[]{:S(2)}) collective-permute-start(f32[4,4608]{1,0:T(4,128)S(1)} %get-tuple-element.29), channel_id=1, source_target_pairs={{0,15},{1,2},{2,1},{3,4},{4,3},{5,6},{6,5},{7,8},{8,7},{9,10},{10,... | collective-permute-start | bytes 221192 | tf_op jit(solution)/shard_map/ppermute | solution.py:563
  13.7 4.8 %collective-permute-start.2 = (f32[4,6144]{1,0:T(4,128)S(1)}, f32[4,6144]{1,0:T(4,128)S(1)}, u32[]{:S(2)}, u32[]{:S(2)}) collective-permute-start(f32[4,6144]{1,0:T(4,128)S(1)} %get-tuple-element.30), channel_id=1, source_target_pairs={{0,3},{1,2},{2,1},{3,0},{4,7},{5,6},{6,5},{7,4},{8,11},{9,10},{10,... | collective-permute-start | bytes 294920 | tf_op jit(solution)/shard_map/ppermute | solution.py:558
  14.4 5.5 %collective-permute-start.8 = (f32[4,5376]{1,0:T(4,128)S(1)}, f32[4,5376]{1,0:T(4,128)S(1)}, u32[]{:S(2)}, u32[]{:S(2)}) collective-permute-start(f32[4,5376]{1,0:T(4,128)S(1)} %get-tuple-element.35), channel_id=1, source_target_pairs={{0,16},{1,17},{2,18},{3,19},{4,20},{5,21},{6,22},{7,23},{8,24},{9,... | collective-permute-start | bytes 258056 | tf_op jit(solution)/shard_map/ppermute | solution.py:558
  16.9 4.2 %collective-permute-start.9 = (f32[4,5376]{1,0:T(4,128)S(1)}, f32[4,5376]{1,0:T(4,128)S(1)}, u32[]{:S(2)}, u32[]{:S(2)}) collective-permute-start(f32[4,5376]{1,0:T(4,128)S(1)} %get-tuple-element.36), channel_id=1, source_target_pairs={{0,112},{16,32},{32,16},{48,64},{64,48},{80,96},{96,80},{112,0},{1... | collective-permute-start | bytes 258056 | tf_op jit(solution)/shard_map/ppermute | solution.py:563
  18.6 5.1 %collective-permute-start.3 = (f32[4,5120]{1,0:T(4,128)S(1)}, f32[4,5120]{1,0:T(4,128)S(1)}, u32[]{:S(2)}, u32[]{:S(2)}) collective-permute-start(f32[4,5120]{1,0:T(4,128)S(1)} %slice.44), channel_id=1, source_target_pairs={{0,4},{1,5},{2,6},{3,7},{4,0},{5,1},{6,2},{7,3},{8,12},{9,13},{10,... | collective-permute-start | bytes 245768 | tf_op jit(solution)/shard_map/ppermute | solution.py:558
  23.8 6.7 %collective-permute-start.4 = (f32[4,4096]{1,0:T(4,128)S(1)}, f32[4,4096]{1,0:T(4,128)S(1)}, u32[]{:S(2)}, u32[]{:S(2)}) collective-permute-start(f32[4,4096]{1,0:T(4,128)S(1)} %slice.45), channel_id=1, source_target_pairs={{0,12},{1,13},{2,14},{3,15},{4,8},{5,9},{6,10},{7,11},{8,4},{9,5},... | collective-permute-start | bytes 196616 | tf_op jit(solution)/shard_map/ppermute | solution.py:558
  30.6 4.2 %collective-permute-start.5 = (f32[4,3072]{1,0:T(4,128)S(1)}, f32[4,3072]{1,0:T(4,128)S(1)}, u32[]{:S(2)}, u32[]{:S(2)}) collective-permute-start(f32[4,3072]{1,0:T(4,128)S(1)} %slice.46), channel_id=1, source_target_pairs={{0,16},{1,17},{2,18},{3,19},{4,20},{5,21},{6,22},{7,23},{8,24},{9,... | collective-permute-start | bytes 147464 | tf_op jit(solution)/shard_map/ppermute | solution.py:558
  34.8 4.1 %collective-permute-start.6 = (f32[4,2048]{1,0:T(4,128)S(1)}, f32[4,2048]{1,0:T(4,128)S(1)}, u32[]{:S(2)}, u32[]{:S(2)}) collective-permute-start(f32[4,2048]{1,0:T(4,128)S(1)} %slice.47), channel_id=1, source_target_pairs={{0,32},{1,33},{2,34},{3,35},{4,36},{5,37},{6,38},{7,39},{8,40},{9,... | collective-permute-start | bytes 98312 | tf_op jit(solution)/shard_map/ppermute | solution.py:558
  38.9 2.5 %copy-start.1 = (bf16[585,512]{1,0:T(8,128)(2,1)S(1)}, bf16[585,512]{1,0:T(8,128)(2,1)}, u32[]{:S(2)}) copy-start(bf16[585,512]{1,0:T(8,128)(2,1)} %constant.2.clone.refs_5_) | copy-start | bytes 1797124
  38.9 4.3 %collective-permute-start.7 = (f32[4,1024]{1,0:T(4,128)S(1)}, f32[4,1024]{1,0:T(4,128)S(1)}, u32[]{:S(2)}, u32[]{:S(2)}) collective-permute-start(f32[4,1024]{1,0:T(4,128)S(1)} %get-tuple-element.48.mine_ref), channel_id=1, source_target_pairs={{0,96},{1,97},{2,98},{3,99},{4,100},{5,101},{6,102},{7,103},{8,104... | collective-permute-start | bytes 49160 | tf_op jit(solution)/shard_map/ppermute | solution.py:558
